TPU v7x, 512 devices: a whole 4x4x16 slice. The times are simulated.
512 devices in a mesh: queue: 16 (over x, y), seq: 32 (over z, core).
Axes of the slice: x: 4, y: 4, z: 16, core: 2. Of those that a mesh axis runs over, the one named last changes fastest.
Arguments:
- t_qkv: bfloat16 [4, 16, 2304, 1728], P(None, 'queue', 'seq'), may hold values from -6 to 6
- hidden: bfloat16 [4, 16, 2304, 1152], P(None, 'queue', 'seq'), may hold values from -6 to 6
- latents: bfloat16 [4, 16, 2304, 16], P(None, 'queue', 'seq'), may hold values from -6 to 6
- fresh: bfloat16 [4, 2304, 16], P(None, 'seq'), may hold values from -6 to 6
- levels: int32 [16], replicated, may hold values from 1 to 64, as said below
- alpha_bar: float32 [65], replicated, may hold values from 0.05 to 0.95
- modulation: bfloat16 [65, 6, 1152], replicated, may hold values from -3 to 3
- w_tout: bfloat16 [576, 1152], P('queue'), may hold values from -0.25 to 0.25
- w_final: bfloat16 [1152, 16], replicated, may hold values from -0.1875 to 0.1875
- w_embed: bfloat16 [16, 1152], replicated, may hold values from -1.5 to 1.5
- w_sqkv: bfloat16 [1152, 1728], P('queue'), may hold values from -0.20623948 to 0.20623948
- w_sout: bfloat16 [576, 1152], P('queue'), may hold values from -0.25 to 0.25
Outputs:
- queued: bfloat16 [4, 16, 2304, 16], P(None, 'queue', 'seq')
- block_out: bfloat16 [4, 16, 2304, 1152], P(None, 'queue', 'seq')
Inputs may be any that keep to these rules, and one draw needn't show every extreme that they name: levels rise strictly along the queue; the head frame is at level 1 and the tail frame at level 64.
All inputs are finite; a program needn't handle non-finite values.
Results may differ from a plain program's by a relative error of at most 0.011.
Values may be sent and summed in bfloat16 or wider, within the bound.
No kernel may reach another device: no remote copies, remote signals or barrier semaphores. Data moves between devices by JAX's collectives and lax.ppermute only.
A program may use at most 64 MiB of HBM per device.

v0:
```python
import math

import jax
import jax.numpy as jnp
import numpy as np
from jax import lax
from jax.experimental import pallas as pl
from jax.experimental.pallas import tpu as pltpu
from jax.sharding import PartitionSpec as P

HEADS = 8
HDIM = 72
HALF = HDIM // 2
SLOT = 40
HSLOT = 2 * SLOT
SCORE_SCALE = 1.0 / math.sqrt(HDIM)
LOG2E = math.log2(math.e)
F32 = jnp.float32
BF16 = jnp.bfloat16
VMEM_LIMIT = 56 * 1024 * 1024


def mm(a, b):
    return jnp.dot(a, b, preferred_element_type=F32)


def mm_nt(a, b):
    return lax.dot_general(a, b, (((1,), (1,)), ((), ())), preferred_element_type=F32)


def call(kernel, out_shape, args, scratch=(), smem=(), flops=0, grid=None, in_specs=None, out_specs=None):
    moved = sum(a.size * a.dtype.itemsize for a in args)
    if in_specs is None:
        in_specs = [
            pl.BlockSpec(memory_space=pltpu.SMEM if i in smem else pltpu.VMEM) for i in range(len(args))
        ]
        out_specs = pl.BlockSpec(memory_space=pltpu.VMEM)
    return pl.pallas_call(
        kernel,
        out_shape=out_shape,
        in_specs=in_specs,
        out_specs=out_specs,
        scratch_shapes=list(scratch),
        compiler_params=pltpu.CompilerParams(vmem_limit_bytes=VMEM_LIMIT),
        cost_estimate=pl.CostEstimate(flops=flops, bytes_accessed=moved, transcendentals=0),
        **({"grid": grid} if grid else {}),
    )(*args)


def layer_norm(values):
    center = values - jnp.mean(values, axis=-1, keepdims=True)
    spread = jnp.mean(center * center, axis=-1, keepdims=True)
    return center * lax.rsqrt(spread + 1e-06)


def pack_kernel(x_ref, o_ref):
    width = o_ref.shape[-1]
    for part in range(o_ref.shape[0]):
        o_ref[part] = x_ref[0, :, part * width : (part + 1) * width]


def temporal_columns():
    pick = np.zeros((6 * HDIM, 1024), np.float32)
    for head in range(2):
        base = 3 * HDIM * head
        for i in range(HDIM):
            pick[base + i, 256 * head + i] = 1.0
            pick[base + HDIM + i, 256 * head + 128 + i] = 1.0
            place = HSLOT * head + (i // HALF) * SLOT + i % HALF
            pick[base + 2 * HDIM + i, 512 + 256 * head + place] = 1.0
    return pick


def temporal_kernel(x_ref, pick_ref, o_ref, parts, total):
    frames, tokens, _ = x_ref.shape
    pick = pick_ref[...]
    for f in range(frames):
        parts[f] = mm(x_ref[f], pick)
    rows = frames * 8
    same = (
        lax.broadcasted_iota(jnp.int32, (rows, rows), 0) % 8
        == lax.broadcasted_iota(jnp.int32, (rows, rows), 1) % 8
    )
    for block in range(tokens // 8):
        piece = parts[:, 8 * block : 8 * block + 8, :].reshape(rows, 1024).astype(BF16)
        out = None
        for head in range(2):
            q = piece[:, 256 * head : 256 * head + 128]
            k = piece[:, 256 * head + 128 : 256 * head + 256]
            v = piece[:, 512 + 256 * head : 512 + 256 * head + 2 * HSLOT]
            scores = jnp.where(same, mm_nt(q, k) * SCORE_SCALE, -jnp.inf)
            top = jnp.max(scores, axis=-1, keepdims=True)
            raised = jnp.exp(scores - top)
            weights = (raised / jnp.sum(raised, axis=-1, keepdims=True)).astype(BF16)
            found = mm(weights, v)
            out = found if out is None else out + found
        total[:, 8 * block : 8 * block + 8, :] = out.reshape(frames, 8, 2 * HSLOT)
    o_ref[...] = total[...].astype(BF16)


def step_kernel(coef_ref, att_ref, hid_ref, lat_ref, w_ref, wf_ref, mod_ref, o_ref):
    videos, tokens, width = hid_ref.shape
    rows = videos * tokens
    pairs = att_ref.shape[0] // videos
    att = att_ref[...].astype(F32).reshape(videos, pairs, tokens, 2 * HSLOT)
    proj = None
    for p in range(pairs):
        part = att[:, p].reshape(rows, 2 * HSLOT).astype(BF16)
        term = mm(part, w_ref[2 * HSLOT * p : 2 * HSLOT * (p + 1), :])
        proj = term if proj is None else proj + term
    residual = hid_ref[...].astype(F32).reshape(rows, width) + mod_ref[0:1, :] * proj
    final_in = (layer_norm(residual) * (1.0 + mod_ref[2:3, :]) + mod_ref[1:2, :]).astype(BF16)
    predicted = mm_nt(wf_ref[...], final_in)
    for v in range(videos):
        pred = predicted[:, tokens * v : tokens * (v + 1)]
        clean = (lat_ref[v].astype(F32) - coef_ref[0] * pred) * coef_ref[1]
        o_ref[v] = (coef_ref[2] * clean + coef_ref[3] * pred).astype(BF16)


def spatial_kernel(
    group_ref, lat_ref, wemb_ref, ua_ref, va_ref, cb_ref, sb_ref, mod_ref, wq_ref, wkv_ref,
    o_ref, xs, keys, vals, qs, outs,
):
    chunks, _, tokens = lat_ref.shape
    members = o_ref.shape[0]
    total_rows = chunks * tokens
    own_rows = members * tokens
    wemb = wemb_ref[...]
    gain = 1.0 + mod_ref[4:5, :]
    shift = mod_ref[3:4, :]

    def build(pair, carry):
        made = []
        for i in range(2):
            c = 2 * pair + i
            latent = lat_ref[c].astype(F32).T.astype(BF16)
            place = ua_ref[c] * cb_ref[...] + va_ref[c] * sb_ref[...]
            embedded = mm(latent, wemb) + place
            made.append(layer_norm(embedded) * gain + shift)
        start = pl.multiple_of(pair * (2 * tokens), 2 * tokens)
        xs[pl.ds(start, 2 * tokens), :] = jnp.concatenate(made, axis=0).astype(BF16)
        return carry

    lax.fori_loop(0, chunks // 2, build, 0)

    lane = lax.broadcasted_iota(jnp.int32, (1, HSLOT), 1)
    ones = jnp.where(lane == HALF, 1.0, 0.0)
    block = 384

    def project(step, carry):
        start = pl.multiple_of(step * block, block)
        kv = mm(xs[pl.ds(start, block), :], wkv_ref[...])
        for h in range(HEADS):
            at = (HDIM + HSLOT) * h
            keys[h, pl.ds(start, block), :] = kv[:, at : at + HDIM].astype(BF16)
            vals[h, pl.ds(start, block), :] = (kv[:, at + HDIM : at + HDIM + HSLOT] + ones).astype(BF16)
        return carry

    lax.fori_loop(0, total_rows // block, project, 0)

    first = pl.multiple_of(group_ref[0] * own_rows, own_rows)
    q_all = mm(xs[pl.ds(first, own_rows), :], wq_ref[...])
    for h in range(HEADS):
        qs[h] = q_all[:, HDIM * h : HDIM * (h + 1)].astype(BF16)

    def attend(h, carry):
        scores = mm_nt(qs[h], keys[h])
        top = jnp.max(scores, axis=-1, keepdims=True)
        raised = jnp.exp2((scores - top) * (SCORE_SCALE * LOG2E)).astype(BF16)
        found = mm(raised, vals[h])
        outs[h] = found * (1.0 / found[:, HALF : HALF + 1])
        return carry

    lax.fori_loop(0, HEADS, attend, 0)
    merged = jnp.concatenate([outs[h] for h in range(HEADS)], axis=-1)
    o_ref[...] = merged.reshape(members, tokens, HEADS * HSLOT).astype(BF16)


def finish_kernel(seq_ref, att_ref, lat_ref, wemb_ref, ua_ref, va_ref, cb_ref, sb_ref, mod_ref, w_ref, o_ref):
    videos, tokens, width = o_ref.shape
    att = att_ref[...].astype(F32).reshape(videos * tokens, HEADS * HSLOT).astype(BF16)
    gated = mm(att, w_ref[...]) * mod_ref[5:6, :]
    s = seq_ref[0]
    place = ua_ref[s] * cb_ref[...] + va_ref[s] * sb_ref[...]
    for v in range(videos):
        latent = lat_ref[v].astype(F32).T.astype(BF16)
        embedded = mm(latent, wemb_ref[...]) + place
        o_ref[v] = (embedded + gated[tokens * v : tokens * (v + 1), :]).astype(BF16)


def position_factors(chunks, tokens, width):
    half = width // 2
    frequency = jnp.exp(jnp.arange(half, dtype=F32) * (-math.log(10000.0) / half))
    start = (jnp.arange(chunks, dtype=F32) * tokens)[:, None] * frequency[None, :]
    inner = jnp.arange(tokens, dtype=F32)[:, None] * frequency[None, :]
    sin_a, cos_a, sin_b, cos_b = jnp.sin(start), jnp.cos(start), jnp.sin(inner), jnp.cos(inner)
    ua = jnp.concatenate([sin_a, cos_a], axis=-1).reshape(chunks, 1, width)
    va = jnp.concatenate([cos_a, -sin_a], axis=-1).reshape(chunks, 1, width)
    cb = jnp.concatenate([cos_b, cos_b], axis=-1)
    sb = jnp.concatenate([sin_b, sin_b], axis=-1)
    return ua, va, cb, sb


def pad_rows(weight):
    return jnp.pad(weight, ((0, SLOT - HALF), (0, 0)))


def spread(value, axis):
    count = lax.axis_size(axis)
    copies = jnp.broadcast_to(value[None], (count,) + value.shape)
    return lax.all_to_all(copies, axis, split_axis=0, concat_axis=0, tiled=True)


def shards(
    t_qkv, hidden, latents, fresh, levels, alpha_bar, modulation, w_tout, w_final, w_embed, w_sqkv, w_sout,
):
    frames = lax.axis_size("queue")
    seqs = lax.axis_size("seq")
    queue_pos = lax.axis_index("queue")
    seq_pos = lax.axis_index("seq")
    videos, _, tokens, width = hidden.shape
    top_level = alpha_bar.shape[0] - 1
    pairs = frames // videos

    by_head = w_sqkv.reshape(-1, HEADS, 3, HDIM)
    q_cols = by_head[:, :, 0].reshape(-1, HEADS * HDIM)
    v_cols = jnp.pad(
        by_head[:, :, 2].reshape(-1, HEADS, 2, HALF), ((0, 0), (0, 0), (0, 0), (0, SLOT - HALF))
    ).reshape(-1, HEADS, HSLOT)
    kv_cols = jnp.concatenate([by_head[:, :, 1], v_cols], axis=-1).reshape(-1, HEADS * (HDIM + HSLOT))
    w_spatial = lax.all_gather(jnp.concatenate([q_cols, kv_cols], axis=-1), "queue", axis=0, tiled=True)

    width_part = t_qkv.shape[-1] // pairs
    packed = call(
        pack_kernel,
        jax.ShapeDtypeStruct((frames, tokens, width_part), BF16),
        (t_qkv.reshape(videos, tokens, -1),),
        grid=(videos,),
        in_specs=[pl.BlockSpec((1, tokens, t_qkv.shape[-1]), lambda v: (v, 0, 0))],
        out_specs=pl.BlockSpec((pairs, tokens, width_part), lambda v: (v, 0, 0)),
    )
    arrived = lax.all_to_all(packed, "queue", split_axis=0, concat_axis=0, tiled=True)
    w_t = spread(pad_rows(w_tout), "queue").reshape(frames * SLOT, width)

    attended = call(
        temporal_kernel,
        jax.ShapeDtypeStruct((frames, tokens, 2 * HSLOT), BF16),
        (arrived, jnp.asarray(temporal_columns(), BF16)),
        scratch=[pltpu.VMEM((frames, tokens, 1024), F32), pltpu.VMEM((frames, tokens, 2 * HSLOT), F32)],
        flops=4_000_000_000,
    )
    returned = lax.all_to_all(attended, "queue", split_axis=0, concat_axis=0, tiled=True)

    level = lax.dynamic_index_in_dim(levels, queue_pos, 0, keepdims=False)
    following = lax.dynamic_index_in_dim(
        jnp.concatenate([levels[1:], jnp.full((1,), top_level + 1, levels.dtype)]), queue_pos, 0, keepdims=False
    )
    mods = lax.dynamic_index_in_dim(modulation, level, 0, keepdims=False).astype(F32)
    new_mods = lax.dynamic_index_in_dim(modulation, following - 1, 0, keepdims=False).astype(F32)
    a = lax.dynamic_index_in_dim(alpha_bar, level, 0, keepdims=False)
    b = lax.dynamic_index_in_dim(alpha_bar, level - 1, 0, keepdims=False)
    coef = jnp.stack([jnp.sqrt(1.0 - a), 1.0 / jnp.sqrt(a), jnp.sqrt(b), jnp.sqrt(1.0 - b)])

    stepped = call(
        step_kernel,
        jax.ShapeDtypeStruct((videos, latents.shape[-1], tokens), BF16),
        (
            coef,
            returned,
            hidden.reshape(videos, tokens, width),
            latents.reshape(videos, tokens, -1).transpose(0, 2, 1),
            w_t,
            w_final.T,
            mods,
        ),
        smem=(0,),
        flops=1_000_000_000,
    )
    arriving = lax.ppermute(stepped, "queue", [(f, f - 1) for f in range(1, frames)])
    queued = jnp.where(queue_pos == frames - 1, fresh.transpose(0, 2, 1), arriving)

    everyone = lax.all_to_all(
        jnp.tile(queued, (seqs // videos, 1, 1)), "seq", split_axis=0, concat_axis=0, tiled=True
    )
    ua, va, cb, sb = position_factors(seqs, tokens, width)
    groups = [[videos * g + i for i in range(videos)] for g in range(seqs // videos)]
    sout_shard, everyone = lax.optimization_barrier((pad_rows(w_sout), everyone))
    w_s = spread(sout_shard, "queue").reshape(frames * SLOT, width)
    rows = seqs * tokens
    spatial = call(
        spatial_kernel,
        jax.ShapeDtypeStruct((videos, tokens, HEADS * HSLOT), BF16),
        (
            (seq_pos // videos).reshape(1), everyone, w_embed, ua, va, cb, sb, new_mods,
            w_spatial[:, : HEADS * HDIM], w_spatial[:, HEADS * HDIM :],
        ),
        scratch=[
            pltpu.VMEM((rows, width), BF16),
            pltpu.VMEM((HEADS, rows, HDIM), BF16),
            pltpu.VMEM((HEADS, rows, HSLOT), BF16),
            pltpu.VMEM((HEADS, videos * tokens, HDIM), BF16),
            pltpu.VMEM((HEADS, videos * tokens, HSLOT), F32),
        ],
        smem=(0,),
        flops=20_000_000_000,
    )
    heads_out = lax.all_to_all(
        spatial, "seq", split_axis=0, concat_axis=0, tiled=True, axis_index_groups=groups
    )
    block_out = call(
        finish_kernel,
        jax.ShapeDtypeStruct((videos, tokens, width), BF16),
        (seq_pos.reshape(1), heads_out, queued, w_embed, ua, va, cb, sb, new_mods, w_s),
        smem=(0,),
        flops=1_000_000_000,
    )
    return (
        queued.transpose(0, 2, 1).reshape(videos, 1, tokens, -1),
        block_out.reshape(videos, 1, tokens, width),
    )


def solution(mesh):
    in_specs = (
        P(None, "queue", "seq", None),
        P(None, "queue", "seq", None),
        P(None, "queue", "seq", None),
        P(None, "seq", None),
        P(),
        P(),
        P(),
        P("queue", None),
        P(),
        P(),
        P("queue", None),
        P("queue", None),
    )
    out_specs = (P(None, "queue", "seq", None), P(None, "queue", "seq", None))
    return jax.shard_map(shards, mesh=mesh, in_specs=in_specs, out_specs=out_specs, check_vma=False)
```

profile of v0, /device:TPU:24, one launch (start us, length us, event | category | flops | bytes accessed | tf_op | source)
XLA Modules:
  0.0 216.5 jit_solution(3344951514018883184)
XLA Ops:
  7.2 0.0 all-gather.2.cloned.1.call-start
  7.2 1.2 copy.25
  8.6 0.1 pad_maximum_fusion.2
  8.7 0.2 copy.35
  8.9 0.1 copy.34
  9.0 0.8 pad_maximum_fusion.3
  9.8 0.0 all-gather.2.cloned.1.call-update
  9.9 3.7 %shard_map.140 = bf16[16,72,432]{2,1,0:T(8,128)(2,1)} custom-call(bf16[4,72,1728]{2,1,0:T(8,128)(2,1)} %bitcast.47), custom_call_target="tpu_custom_call" | custom-call | bytes 995328 | tf_op jit(solution)/shard_map/pallas_call | solution.py:38
  13.5 23.9 %all_to_all.30.x_ref = bf16[16,72,432]{2,1,0:T(8,128)(2,1)} all-to-all(bf16[16,72,432]{2,1,0:T(8,128)(2,1)} %shard_map.140), channel_id=1, replica_groups=mesh['queue'=16,'seq'=32] {'queue'}, dimensions={0} | all-to-all | bytes 1990656 | tf_op jit(solution)/shard_map/all_to_all | solution.py:242
  37.4 6.3 %shard_map.141 = bf16[16,72,160]{2,1,0:T(8,128)(2,1)} custom-call(bf16[16,72,432]{2,1,0:T(8,128)(2,1)} %all_to_all.30.x_ref, bf16[432,1024]{1,0:T(8,128)(2,1)} %constant.72.clone.pick_ref), custom_call_target="tpu_custom_call" | custom-call | flops 4000000000 | bytes 1880064 | tf_op jit(solution)/shard_map/pallas_call | solution.py:38
  43.7 5.4 %all-to-all-start.1 = ((bf16[16,72,160]{2,1,0:T(8,128)(2,1)}), bf16[16,72,160]{2,1,0:T(8,128)(2,1)S(1)}, u32[]{:S(2)}, u32[]{:S(2)}) async-start(bf16[16,72,160]{2,1,0:T(8,128)(2,1)} %shard_map.141), calls=%async_computation.1 | async-start | bytes 1179648 | tf_op jit(solution)/shard_map/all_to_all | solution.py:252
  49.0 0.6 dynamic_slice.21
  52.9 0.7 fusion.6
  56.3 0.1 slice.18
  56.5 0.1 pad_add_fusion
  56.5 0.4 all-to-all-done.1.att_ref
  56.9 1.4 broadcast_in_dim.4
  58.3 0.0 copy-done.2
  58.3 6.9 %all-to-all-start.2 = ((bf16[16,40,1152]{2,1,0:T(8,128)(2,1)}), bf16[16,40,1152]{2,1,0:T(8,128)(2,1)S(1)}, u32[]{:S(2)}, u32[]{:S(2)}) async-start(bf16[16,40,1152]{2,1,0:T(8,128)(2,1)} %broadcast_in_dim.4), calls=%async_computation.2 | async-start | bytes 2949120 | tf_op jit(solution)/shard_map/all_to_all | solution.py:211
  65.1 0.7 pad_maximum_fusion.5.coef_ref
  65.8 0.6 dynamic_slice.25
  67.7 1.0 constant_dynamic-slice_fusion
  68.7 0.7 fusion
  69.4 0.6 fusion.4.mod_ref
  70.0 0.6 fusion.3.mod_ref
  70.7 25.8 %all-to-all-done.2 = bf16[16,40,1152]{2,1,0:T(8,128)(2,1)S(1)} async-done(((bf16[16,40,1152]{2,1,0:T(8,128)(2,1)}), bf16[16,40,1152]{2,1,0:T(8,128)(2,1)S(1)}, u32[]{:S(2)}, u32[]{:S(2)}) %all-to-all-start.2) | async-done | bytes 1474592 | tf_op jit(solution)/shard_map/all_to_all | solution.py:211
  96.4 1.2 copy-done
  97.6 4.2 %shard_map.142 = bf16[4,16,72]{2,1,0:T(8,128)(2,1)} custom-call(f32[4]{0:T(128)} %pad_maximum_fusion.5.coef_ref, bf16[16,72,160]{2,1,0:T(8,128)(2,1)} %copy-done.2, bf16[4,72,1152]{2,1,0:T(8,128)(2,1)} %bitcast.52, bf16[4,16,72]{2,1,0:T(8,128)(2,1)} %bitcast.54, bf16[640,1152]{1,0:T(8,128)(2,1)} %bitcast.44, bf16[16,1152]{1,0:T(8,128)(2,1)} %bitcast.53, ...), custom_call_target="tpu_custom_call" | custom-call | flops 1000000000 | bytes 2580496 | tf_op jit(solution)/shard_map/pallas_call | solution.py:38
  101.8 2.8 %collective-permute-start = (bf16[4,16,72]{2,1,0:T(8,128)(2,1)}, bf16[4,16,72]{2,1,0:T(8,128)(2,1)S(1)}, u32[]{:S(2)}, u32[]{:S(2)}) collective-permute-start(bf16[4,16,72]{2,1,0:T(8,128)(2,1)} %shard_map.142), channel_id=1, source_target_pairs={{32,0},{64,32},{96,64},{128,96},{160,128},{192,160},{224,192},{256... | collective-permute-start | bytes 27656 | tf_op jit(solution)/shard_map/ppermute | solution.py:279
  104.6 0.4 fusion.2
  104.9 4.8 %collective-permute-done = bf16[4,16,72]{2,1,0:T(8,128)(2,1)S(1)} collective-permute-done((bf16[4,16,72]{2,1,0:T(8,128)(2,1)}, bf16[4,16,72]{2,1,0:T(8,128)(2,1)S(1)}, u32[]{:S(2)}, u32[]{:S(2)}) %collective-permute-start) | collective-permute-done | bytes 9248 | tf_op jit(solution)/shard_map/ppermute | solution.py:279
  109.7 0.0 copy-start.6
  109.7 0.7 tile.4
  110.4 15.4 %all-to-all-start.3 = ((bf16[32,16,72]{2,1,0:T(8,128)(2,1)}), bf16[32,16,72]{2,1,0:T(8,128)(2,1)S(1)}, u32[]{:S(2)}, u32[]{:S(2)}) async-start(bf16[32,16,72]{2,1,0:T(8,128)(2,1)} %bitcast.14), calls=%async_computation.3 | async-start | bytes 262144 | tf_op jit(solution)/shard_map/all_to_all | solution.py:282
  125.8 0.1 pad_maximum_fusion.4
  125.9 0.8 copy.30.ua_ref
  126.8 0.8 reshape.89.va_ref
  127.5 1.0 pad_maximum_fusion
  128.6 14.5 %all-to-all-done.3.lat_ref = bf16[32,16,72]{2,1,0:T(8,128)(2,1)S(1)} async-done(((bf16[32,16,72]{2,1,0:T(8,128)(2,1)}), bf16[32,16,72]{2,1,0:T(8,128)(2,1)S(1)}, u32[]{:S(2)}, u32[]{:S(2)}) %all-to-all-start.3) | async-done | bytes 73760 | tf_op jit(solution)/shard_map/all_to_all | solution.py:282
  143.0 1.3 broadcast_in_dim.5
  144.3 5.5 %all-to-all-start.5 = ((bf16[16,40,1152]{2,1,0:T(8,128)(2,1)}), bf16[16,40,1152]{2,1,0:T(8,128)(2,1)S(1)}, u32[]{:S(2)}, u32[]{:S(2)}) async-start(bf16[16,40,1152]{2,1,0:T(8,128)(2,1)} %broadcast_in_dim.5), calls=%async_computation.5 | async-start | bytes 2949120 | tf_op jit(solution)/shard_map/all_to_all | solution.py:211
  149.8 0.0 all-gather.2.cloned.1.call-done
  149.9 4.9 %slice.28.wkv_ref = bf16[1152,1216]{1,0:T(8,128)(2,1)} slice(bf16[1152,1792]{1,0:T(8,128)(2,1)} %all-gather.2.cloned.1.call-done), slice={[0:1152], [576:1792]} | slice | bytes 5603328 | tf_op jit(solution)/shard_map/slice | solution.py:295
  154.7 2.7 %slice.27.wq_ref = bf16[1152,576]{1,0:T(8,128)(2,1)} slice(bf16[1152,1792]{1,0:T(8,128)(2,1)} %all-gather.2.cloned.1.call-done), slice={[0:1152], [0:576]} | slice | bytes 2654208 | tf_op jit(solution)/shard_map/slice | solution.py:295
  157.4 37.2 %shard_map.143 = bf16[4,72,640]{2,1,0:T(8,128)(2,1)} custom-call(s32[1]{0:T(128)} %bitcast.13.group_ref, bf16[32,16,72]{2,1,0:T(8,128)(2,1)} %copy-done.3, bf16[16,1152]{1,0:T(8,128)(2,1)} %wemb_ref.3, f32[32,1,1152]{2,1,0:T(1,128)} %copy.30.ua_ref, f32[32,1,1152]{2,1,0:T(1,128)} %reshape.89.va_ref, f32[72,1152]{1,0:T(8,128)} %get-tuple-element.24.cb_ref, ...), custom_call_target="tpu_custom_call" | custom-call | flops 20000000000 | bytes 5225476 | tf_op jit(solution)/shard_map/pallas_call | solution.py:38
  194.6 0.0 all-to-all-done.5
  194.6 11.4 %all_to_all.31.att_ref = bf16[4,72,640]{2,1,0:T(8,128)(2,1)} all-to-all(bf16[4,72,640]{2,1,0:T(8,128)(2,1)} %shard_map.143), channel_id=1, replica_groups={{0,1,2,3},{4,5,6,7},{8,9,10,11},{12,13,14,15},{16,17,18,19},{20,21,22,2..., dimensions={0} | all-to-all | bytes 737280 | tf_op jit(solution)/shard_map/all_to_all | solution.py:307
  206.0 3.6 %shard_map.144 = bf16[4,72,1152]{2,1,0:T(8,128)(2,1)} custom-call(s32[1]{0:T(128)} %bitcast.12.seq_ref, bf16[4,72,640]{2,1,0:T(8,128)(2,1)} %all_to_all.31.att_ref, bf16[4,16,72]{2,1,0:T(8,128)(2,1)} %copy-done.6, bf16[16,1152]{1,0:T(8,128)(2,1)} %wemb_ref.3, f32[32,1,1152]{2,1,0:T(1,128)} %copy.30.ua_ref, f32[32,1,1152]{2,1,0:T(1,128)} %reshape.89.va_ref, ...), custom_call_target="tpu_custom_call" | custom-call | flops 1000000000 | bytes 2875396 | tf_op jit(solution)/shard_map/pallas_call | solution.py:38
  (26 shorter events, 0.2 us)
Async XLA Ops:
  7.2 142.7 %all-gather.2.cloned.1.call-start = ((), (), s32[]{:S(2)}) async-start(), calls=%async_computation.6 | async-start | bytes 4386816 | tf_op jit(solution)/shard_map/all_gather | solution.py:231
  37.4 11.6 %copy-start.9 = (s32[16]{0:T(128)S(1)}, s32[16]{0:T(128)}, u32[]{:S(2)}) copy-start(s32[16]{0:T(128)} %param.17) | copy-start | bytes 196
  37.4 15.5 %copy-start.8 = (f32[65]{0:T(128)S(1)}, f32[65]{0:T(128)}, u32[]{:S(2)}) copy-start(f32[65]{0:T(128)} %param.18) | copy-start | bytes 784
  37.4 19.0 %copy-start.4 = (bf16[36,1152]{1,0:T(8,128)(2,1)S(1)}, bf16[36,1152]{1,0:T(8,128)(2,1)}, u32[]{:S(2)}) copy-start(bf16[36,1152]{1,0:T(8,128)(2,1)} %param.20) | copy-start | bytes 248836
  43.7 13.2 %all-to-all-start.1 = ((bf16[16,72,160]{2,1,0:T(8,128)(2,1)}), bf16[16,72,160]{2,1,0:T(8,128)(2,1)S(1)}, u32[]{:S(2)}, u32[]{:S(2)}) async-start(bf16[16,72,160]{2,1,0:T(8,128)(2,1)} %shard_map.141), calls=%async_computation.1 | async-start | bytes 1179648 | tf_op jit(solution)/shard_map/all_to_all | solution.py:252
  56.9 1.4 copy-start.2
  58.3 38.2 %all-to-all-start.2 = ((bf16[16,40,1152]{2,1,0:T(8,128)(2,1)}), bf16[16,40,1152]{2,1,0:T(8,128)(2,1)S(1)}, u32[]{:S(2)}, u32[]{:S(2)}) async-start(bf16[16,40,1152]{2,1,0:T(8,128)(2,1)} %broadcast_in_dim.4), calls=%async_computation.2 | async-start | bytes 2949120 | tf_op jit(solution)/shard_map/all_to_all | solution.py:211
  96.4 1.2 copy-start
  97.6 12.1 %copy-start.7 = (bf16[4,72,16]{1,2,0:T(8,128)(2,1)S(1)}, bf16[4,72,16]{1,2,0:T(8,128)(2,1)}, u32[]{:S(2)}) copy-start(bf16[4,72,16]{1,2,0:T(8,128)(2,1)} %param.16) | copy-start | bytes 27652
  97.6 28.3 %copy-start.5 = (bf16[36,1152]{1,0:T(8,128)(2,1)S(1)}, bf16[36,1152]{1,0:T(8,128)(2,1)}, u32[]{:S(2)}) copy-start(bf16[36,1152]{1,0:T(8,128)(2,1)} %param.24) | copy-start | bytes 248836
  101.8 7.9 %collective-permute-start = (bf16[4,16,72]{2,1,0:T(8,128)(2,1)}, bf16[4,16,72]{2,1,0:T(8,128)(2,1)S(1)}, u32[]{:S(2)}, u32[]{:S(2)}) collective-permute-start(bf16[4,16,72]{2,1,0:T(8,128)(2,1)} %shard_map.142), channel_id=1, source_target_pairs={{32,0},{64,32},{96,64},{128,96},{160,128},{192,160},{224,192},{256... | collective-permute-start | bytes 27656 | tf_op jit(solution)/shard_map/ppermute | solution.py:279
  109.7 34.6 %copy-start.6 = (bf16[4,16,72]{2,1,0:T(8,128)(2,1)}, bf16[4,16,72]{2,1,0:T(8,128)(2,1)S(1)}, u32[]{:S(2)}) copy-start(bf16[4,16,72]{2,1,0:T(8,128)(2,1)S(1)} %bitcast_select_fusion.lat_ref) | copy-start | bytes 27652
  110.4 32.6 %all-to-all-start.3 = ((bf16[32,16,72]{2,1,0:T(8,128)(2,1)}), bf16[32,16,72]{2,1,0:T(8,128)(2,1)S(1)}, u32[]{:S(2)}, u32[]{:S(2)}) async-start(bf16[32,16,72]{2,1,0:T(8,128)(2,1)} %bitcast.14), calls=%async_computation.3 | async-start | bytes 262144 | tf_op jit(solution)/shard_map/all_to_all | solution.py:282
  143.0 1.3 copy-start.3
  144.3 50.3 %all-to-all-start.5 = ((bf16[16,40,1152]{2,1,0:T(8,128)(2,1)}), bf16[16,40,1152]{2,1,0:T(8,128)(2,1)S(1)}, u32[]{:S(2)}, u32[]{:S(2)}) async-start(bf16[16,40,1152]{2,1,0:T(8,128)(2,1)} %broadcast_in_dim.5), calls=%async_computation.5 | async-start | bytes 2949120 | tf_op jit(solution)/shard_map/all_to_all | solution.py:211
  194.6 11.4 %copy-start.1 = (bf16[16,40,1152]{2,1,0:T(8,128)(2,1)}, bf16[16,40,1152]{2,1,0:T(8,128)(2,1)S(1)}, u32[]{:S(2)}) copy-start(bf16[16,40,1152]{2,1,0:T(8,128)(2,1)S(1)} %all-to-all-done.5) | copy-start | bytes 4423684
Sparse Core Ops, SparseCore 0:
  11.1 85.5 all-gather.1
where the time goes:
time: 218 us; the launch traced here: 216 us
  Pallas kernels  54.9 us (25%)
  waiting for transfers between devices  45.4 us (21%)
  starting transfers between devices  36 us (17%)
  blocking collectives  35.3 us (16%)
  between operations  21.6 us (10%)
  local copies, waits for them, and re-layouts  18.3 us (8%)
  other arithmetic  5.07 us (2%)
    pallas_call x5, Pallas kernels, call(): pl.pallas_call(kernel, out_shape=out_shape, in_specs=in_specs, out_specs=...  54.9 us
    all_to_all x2, waiting for transfers between devices, spread(): return lax.all_to_all(copies, axis, split_axis=0, concat_axis=0, tiled=True)  25.8 us
    all_to_all x1, blocking collectives, shards(): lax.all_to_all(packed, 'queue', split_axis=0, concat_axis=0, tiled=True)  23.9 us
    all_to_all x1, starting transfers between devices, shards(): lax.all_to_all(jnp.tile(queued, (seqs // videos, 1, 1)), 'seq', split_axi...  15.4 us
    all_to_all x1, waiting for transfers between devices, shards(): lax.all_to_all(jnp.tile(queued, (seqs // videos, 1, 1)), 'seq', split_axi...  14.5 us
    all_to_all x2, starting transfers between devices, spread(): return lax.all_to_all(copies, axis, split_axis=0, concat_axis=0, tiled=True)  12.4 us
    all_to_all x1, blocking collectives, shards(): lax.all_to_all(spatial, 'seq', split_axis=0, concat_axis=0, tiled=True, a...  11.4 us
    all_to_all x1, starting transfers between devices, shards(): lax.all_to_all(attended, 'queue', split_axis=0, concat_axis=0, tiled=True)  5.37 us
  transfers between devices with their start and end apart: 6, of which 4 were waited for; matrix products, arithmetic and copies ran while one was open for 9% of the time, Pallas kernels for 24%

commit v1 on v0

v1 whole, which is shorter than its diff:
```python
import math

import jax
import jax.numpy as jnp
import numpy as np
from jax import lax
from jax.experimental import pallas as pl
from jax.experimental.pallas import tpu as pltpu
from jax.sharding import PartitionSpec as P

HEADS = 8
HDIM = 72
HALF = HDIM // 2
SLOT = 80
PADDED = HEADS * SLOT
SCORE_SCALE = 1.0 / math.sqrt(HDIM)
LOG2E = math.log2(math.e)
F32 = jnp.float32
BF16 = jnp.bfloat16
VMEM_LIMIT = 56 * 1024 * 1024


def mm(a, b):
    return jnp.dot(a, b, preferred_element_type=F32)


def mm_nt(a, b):
    return lax.dot_general(a, b, (((1,), (1,)), ((), ())), preferred_element_type=F32)


def call(kernel, out_shape, args, scratch=(), smem=(), hbm=(), flops=0, grid=None, in_specs=None, out_specs=None):
    moved = sum(a.size * a.dtype.itemsize for a in args)
    if in_specs is None:
        in_specs = [
            pl.BlockSpec(memory_space=pltpu.SMEM if i in smem else pl.ANY if i in hbm else pltpu.VMEM)
            for i in range(len(args))
        ]
        out_specs = jax.tree.map(lambda _: pl.BlockSpec(memory_space=pltpu.VMEM), out_shape)
    return pl.pallas_call(
        kernel,
        out_shape=out_shape,
        in_specs=in_specs,
        out_specs=out_specs,
        scratch_shapes=list(scratch),
        compiler_params=pltpu.CompilerParams(vmem_limit_bytes=VMEM_LIMIT),
        cost_estimate=pl.CostEstimate(flops=flops, bytes_accessed=moved, transcendentals=0),
        **({"grid": grid} if grid else {}),
    )(*args)


def layer_norm(values):
    center = values - jnp.mean(values, axis=-1, keepdims=True)
    spread = jnp.mean(center * center, axis=-1, keepdims=True)
    return center * lax.rsqrt(spread + 1e-06)


def pack_kernel(x_ref, w_ref, o_ref):
    width = x_ref.shape[-1] // o_ref.shape[0]
    weight = w_ref[...]
    for part in range(o_ref.shape[0]):
        o_ref[part, :, :width] = x_ref[0, :, part * width : (part + 1) * width]
        o_ref[part, :, width:] = weight


def temporal_columns():
    pick = np.zeros((6 * HDIM, 1024), np.float32)
    for head in range(2):
        base = 3 * HDIM * head
        for i in range(HDIM):
            pick[base + i, 256 * head + i] = 1.0
            pick[base + HDIM + i, 256 * head + 128 + i] = 1.0
            pick[base + 2 * HDIM + i, 512 + 256 * head + SLOT * head + i] = 1.0
    return pick


def weight_rows():
    pick = np.zeros((2 * SLOT, 2 * HDIM), np.float32)
    for shard in range(2):
        for i in range(HALF):
            pick[HALF * shard + i, HDIM * shard + i] = 1.0
            pick[SLOT + HALF * shard + i, HDIM * shard + HALF + i] = 1.0
    return pick


def temporal_kernel(x_ref, pick_ref, rows_ref, o_ref, w_ref, parts, total):
    frames, tokens, _ = x_ref.shape
    pick = pick_ref[...]
    for f in range(frames):
        parts[f] = mm(x_ref[f, :, : 6 * HDIM], pick)
    rows = frames * 8
    same = (
        lax.broadcasted_iota(jnp.int32, (rows, rows), 0) % 8
        == lax.broadcasted_iota(jnp.int32, (rows, rows), 1) % 8
    )
    for block in range(tokens // 8):
        piece = parts[:, 8 * block : 8 * block + 8, :].reshape(rows, 1024).astype(BF16)
        out = None
        for head in range(2):
            q = piece[:, 256 * head : 256 * head + 128]
            k = piece[:, 256 * head + 128 : 256 * head + 256]
            v = piece[:, 512 + 256 * head : 512 + 256 * head + 2 * SLOT]
            scores = jnp.where(same, mm_nt(q, k) * SCORE_SCALE, -jnp.inf)
            top = jnp.max(scores, axis=-1, keepdims=True)
            raised = jnp.exp(scores - top)
            weights = (raised / jnp.sum(raised, axis=-1, keepdims=True)).astype(BF16)
            found = mm(weights, v)
            out = found if out is None else out + found
        total[:, 8 * block : 8 * block + 8, :] = out.reshape(frames, 8, 2 * SLOT)
    o_ref[...] = total[...].astype(BF16)
    for h in range(frames // 2):
        pair = x_ref[2 * h : 2 * h + 2, :, 6 * HDIM :].astype(F32).reshape(2 * tokens, -1).astype(BF16)
        both = mm(rows_ref[...], pair)
        w_ref[SLOT * h : SLOT * (h + 1), :] = jnp.concatenate(
            [both[:SLOT], both[SLOT:]], axis=-1
        ).astype(BF16)


def step_kernel(coef_ref, core_ref, att_ref, hid_ref, lat_ref, mine_ref, other_ref, wf_ref, mod_ref, o_ref):
    videos, tokens, width = hid_ref.shape
    rows = videos * tokens
    pairs = att_ref.shape[0] // videos
    att = att_ref[...].astype(F32).reshape(videos, pairs, tokens, 2 * SLOT)
    own = far = None
    for p in range(pairs):
        part = att[:, p].reshape(rows, 2 * SLOT).astype(BF16)
        at = slice(2 * SLOT * p, 2 * SLOT * (p + 1))
        own_term, far_term = mm(part, mine_ref[at, :]), mm(part, other_ref[at, :])
        own = own_term if own is None else own + own_term
        far = far_term if far is None else far + far_term
    low = core_ref[0] == 0
    proj = jnp.concatenate([jnp.where(low, own, far), jnp.where(low, far, own)], axis=-1)
    residual = hid_ref[...].astype(F32).reshape(rows, width) + mod_ref[0:1, :] * proj
    final_in = (layer_norm(residual) * (1.0 + mod_ref[2:3, :]) + mod_ref[1:2, :]).astype(BF16)
    predicted = mm_nt(wf_ref[...], final_in)
    for v in range(videos):
        pred = predicted[:, tokens * v : tokens * (v + 1)]
        clean = (lat_ref[v].astype(F32) - coef_ref[0] * pred) * coef_ref[1]
        o_ref[v] = (coef_ref[2] * clean + coef_ref[3] * pred).astype(BF16)


def spatial_kernel(
    group_ref, lat_ref, wemb_ref, ua_ref, va_ref, cb_ref, sb_ref, mod_ref, w_ref,
    o_ref, even, odd, own, keys, vals, ws, sem,
):
    chunks, _, tokens = lat_ref.shape
    members = o_ref.shape[0]
    block = members * tokens
    blocks = chunks // members
    copy = pltpu.make_async_copy(w_ref.at[:, : 3 * PADDED], ws, sem)
    copy.start()
    wemb = wemb_ref[...]
    gain = 1.0 + mod_ref[4:5, :]
    shift = mod_ref[3:4, :]
    lane = lax.broadcasted_iota(jnp.int32, (1, PADDED), 1)
    ones = jnp.where(lane % SLOT == HDIM, 1.0, 0.0)

    def build(index, x_ref):
        made = []
        for i in range(members):
            c = index * members + i
            latent = lat_ref[c].astype(F32).T.astype(BF16)
            place = ua_ref[pl.ds(c, 1), :] * cb_ref[...] + va_ref[pl.ds(c, 1), :] * sb_ref[...]
            embedded = mm(latent, wemb) + place
            made.append(layer_norm(embedded) * gain + shift)
            if i % 2:
                x_ref[tokens * (i - 1) : tokens * (i + 1), :] = jnp.concatenate(made, axis=0).astype(BF16)
                made = []

    def project(index, x_ref):
        start = pl.multiple_of(index * block, block)
        x = x_ref[...]
        keys[pl.ds(start, block), :] = mm(x, ws[:, :PADDED]).astype(BF16)
        vals[pl.ds(start, block), :] = (mm(x, ws[:, PADDED : 2 * PADDED]) + ones).astype(BF16)

    def keep(index, x_ref):
        @pl.when(index == group_ref[0])
        def _():
            own[...] = x_ref[...]

    build(0, even)
    copy.wait()

    def two(step, carry):
        project(2 * step, even)
        build(2 * step + 1, odd)
        keep(2 * step, even)
        project(2 * step + 1, odd)
        build(jnp.minimum(2 * step + 2, blocks - 1), even)
        keep(2 * step + 1, odd)
        return carry

    lax.fori_loop(0, blocks // 2, two, 0)

    q_all = mm(own[...], ws[:, 2 * PADDED :])
    merged = [None] * (PADDED // 128)
    for h in range(HEADS):
        first = SLOT * h // 128
        last = (SLOT * h + HDIM) // 128
        here = slice(128 * first, 128 * (last + 1))
        inside = (lane >= SLOT * h) & (lane < SLOT * h + HDIM)
        inside = inside[:, here]
        q = jnp.where(inside, q_all[:, here], 0.0).astype(BF16)
        scores = mm_nt(q, keys[:, here])
        top = jnp.max(scores, axis=-1, keepdims=True)
        raised = jnp.exp2((scores - top) * (SCORE_SCALE * LOG2E)).astype(BF16)
        found = mm(raised, vals[:, here])
        at = SLOT * h + HDIM - 128 * first
        found = jnp.where(inside, found * (1.0 / found[:, at : at + 1]), 0.0)
        for tile in range(first, last + 1):
            piece = found[:, 128 * (tile - first) : 128 * (tile - first + 1)]
            merged[tile] = piece if merged[tile] is None else merged[tile] + piece
    o_ref[...] = jnp.concatenate(merged, axis=-1).reshape(members, tokens, PADDED).astype(BF16)


def finish_kernel(
    seq_ref, att_ref, lat_ref, wemb_ref, ua_ref, va_ref, cb_ref, sb_ref, mod_ref, rows_ref, w_ref,
    o_ref, raw, left, right, sem,
):
    videos, tokens, width = o_ref.shape
    copy = pltpu.make_async_copy(w_ref.at[:, 3 * PADDED :], raw, sem)
    copy.start()
    s = seq_ref[0]
    place = ua_ref[pl.ds(s, 1), :] * cb_ref[...] + va_ref[pl.ds(s, 1), :] * sb_ref[...]
    att = att_ref[...].astype(F32).reshape(videos * tokens, PADDED).astype(BF16)
    copy.wait()
    for h in range(HEADS):
        both = mm(rows_ref[...], raw[2 * HDIM * h : 2 * HDIM * (h + 1), :]).astype(BF16)
        left[SLOT * h : SLOT * (h + 1), :] = both[:SLOT]
        right[SLOT * h : SLOT * (h + 1), :] = both[SLOT:]
    half = width // 2
    proj = jnp.concatenate([mm(att, left[...])[:, :half], mm(att, right[...])[:, :half]], axis=-1)
    gated = proj * mod_ref[5:6, :]
    for v in range(videos):
        latent = lat_ref[v].astype(F32).T.astype(BF16)
        embedded = mm(latent, wemb_ref[...]) + place
        o_ref[v] = (embedded + gated[tokens * v : tokens * (v + 1), :]).astype(BF16)


def position_factors(chunks, tokens, width):
    half = width // 2
    frequency = jnp.exp(jnp.arange(half, dtype=F32) * (-math.log(10000.0) / half))
    start = (jnp.arange(chunks, dtype=F32) * tokens)[:, None] * frequency[None, :]
    inner = jnp.arange(tokens, dtype=F32)[:, None] * frequency[None, :]
    sin_a, cos_a, sin_b, cos_b = jnp.sin(start), jnp.cos(start), jnp.sin(inner), jnp.cos(inner)
    ua = jnp.concatenate([sin_a, cos_a], axis=-1)
    va = jnp.concatenate([cos_a, -sin_a], axis=-1)
    cb = jnp.concatenate([cos_b, cos_b], axis=-1)
    sb = jnp.concatenate([sin_b, sin_b], axis=-1)
    return ua, va, cb, sb


def stack_halves(weight):
    half = weight.shape[-1] // 2
    return jnp.concatenate([weight[:, :half], weight[:, half:]], axis=0)


def pad_heads(columns):
    return jnp.pad(columns, ((0, 0), (0, 0), (0, SLOT - HDIM))).reshape(-1, PADDED)


def shards(
    t_qkv, hidden, latents, fresh, levels, alpha_bar, modulation, w_tout, w_final, w_embed, w_sqkv, w_sout,
):
    frames = lax.axis_size("queue")
    seqs = lax.axis_size("seq")
    queue_pos = lax.axis_index("queue")
    seq_pos = lax.axis_index("seq")
    videos, _, tokens, width = hidden.shape
    top_level = alpha_bar.shape[0] - 1
    pairs = frames // videos

    by_head = w_sqkv.reshape(-1, HEADS, 3, HDIM)
    sout = jnp.pad(stack_halves(w_sout), ((0, 0), (0, PADDED - width // 2)))
    w_shard = jnp.concatenate([pad_heads(by_head[:, :, i]) for i in (1, 2, 0)] + [sout], axis=-1)
    w_spatial = lax.all_gather(w_shard, "queue", axis=0, tiled=True)

    core = seq_pos % 2
    half = width // 2
    tout = stack_halves(lax.dynamic_slice_in_dim(w_tout, core * half, half, axis=1))
    width_part = t_qkv.shape[-1] // pairs
    sent = width_part + tout.shape[-1]
    packed = call(
        pack_kernel,
        jax.ShapeDtypeStruct((frames, tokens, sent), BF16),
        (t_qkv.reshape(videos, tokens, -1), tout),
        grid=(videos,),
        in_specs=[
            pl.BlockSpec((1, tokens, t_qkv.shape[-1]), lambda v: (v, 0, 0)),
            pl.BlockSpec(tout.shape, lambda v: (0, 0)),
        ],
        out_specs=pl.BlockSpec((pairs, tokens, sent), lambda v: (v, 0, 0)),
    )
    arrived = lax.all_to_all(packed, "queue", split_axis=0, concat_axis=0, tiled=True)
    row_pick = jnp.asarray(weight_rows(), BF16)

    attended, w_mine = call(
        temporal_kernel,
        (
            jax.ShapeDtypeStruct((frames, tokens, 2 * SLOT), BF16),
            jax.ShapeDtypeStruct((PADDED, half), BF16),
        ),
        (arrived, jnp.asarray(temporal_columns(), BF16), row_pick),
        scratch=[pltpu.VMEM((frames, tokens, 1024), F32), pltpu.VMEM((frames, tokens, 2 * SLOT), F32)],
        flops=4_000_000_000,
    )
    w_other = lax.ppermute(w_mine, "seq", [(i, i ^ 1) for i in range(seqs)])
    returned = lax.all_to_all(attended, "queue", split_axis=0, concat_axis=0, tiled=True)

    level = lax.dynamic_index_in_dim(levels, queue_pos, 0, keepdims=False)
    following = lax.dynamic_index_in_dim(
        jnp.concatenate([levels[1:], jnp.full((1,), top_level + 1, levels.dtype)]), queue_pos, 0, keepdims=False
    )
    mods = lax.dynamic_index_in_dim(modulation, level, 0, keepdims=False).astype(F32)
    new_mods = lax.dynamic_index_in_dim(modulation, following - 1, 0, keepdims=False).astype(F32)
    a = lax.dynamic_index_in_dim(alpha_bar, level, 0, keepdims=False)
    b = lax.dynamic_index_in_dim(alpha_bar, level - 1, 0, keepdims=False)
    coef = jnp.stack([jnp.sqrt(1.0 - a), 1.0 / jnp.sqrt(a), jnp.sqrt(b), jnp.sqrt(1.0 - b)])

    stepped = call(
        step_kernel,
        jax.ShapeDtypeStruct((videos, latents.shape[-1], tokens), BF16),
        (
            coef,
            core.reshape(1),
            returned,
            hidden.reshape(videos, tokens, width),
            latents.reshape(videos, tokens, -1).transpose(0, 2, 1),
            w_mine,
            w_other,
            w_final.T,
            mods,
        ),
        smem=(0, 1),
        flops=1_000_000_000,
    )
    arriving = lax.ppermute(stepped, "queue", [(f, f - 1) for f in range(1, frames)])
    queued = jnp.where(queue_pos == frames - 1, fresh.transpose(0, 2, 1), arriving)

    everyone = lax.all_to_all(
        jnp.tile(queued, (seqs // videos, 1, 1)), "seq", split_axis=0, concat_axis=0, tiled=True
    )
    ua, va, cb, sb = position_factors(seqs, tokens, width)
    groups = [[videos * g + i for i in range(videos)] for g in range(seqs // videos)]
    rows = seqs * tokens
    own_rows = videos * tokens
    spatial = call(
        spatial_kernel,
        jax.ShapeDtypeStruct((videos, tokens, PADDED), BF16),
        ((seq_pos // videos).reshape(1), everyone, w_embed, ua, va, cb, sb, new_mods, w_spatial),
        scratch=[
            pltpu.VMEM((own_rows, width), BF16),
            pltpu.VMEM((own_rows, width), BF16),
            pltpu.VMEM((own_rows, width), BF16),
            pltpu.VMEM((rows, PADDED), BF16),
            pltpu.VMEM((rows, PADDED), BF16),
            pltpu.VMEM((width, 3 * PADDED), BF16),
            pltpu.SemaphoreType.DMA,
        ],
        smem=(0,),
        hbm=(8,),
        flops=20_000_000_000,
    )
    heads_out = lax.all_to_all(
        spatial, "seq", split_axis=0, concat_axis=0, tiled=True, axis_index_groups=groups
    )
    block_out = call(
        finish_kernel,
        jax.ShapeDtypeStruct((videos, tokens, width), BF16),
        (seq_pos.reshape(1), heads_out, queued, w_embed, ua, va, cb, sb, new_mods, row_pick, w_spatial),
        scratch=[
            pltpu.VMEM((width, PADDED), BF16),
            pltpu.VMEM((PADDED, PADDED), BF16),
            pltpu.VMEM((PADDED, PADDED), BF16),
            pltpu.SemaphoreType.DMA,
        ],
        smem=(0,),
        hbm=(10,),
        flops=1_000_000_000,
    )
    return (
        queued.transpose(0, 2, 1).reshape(videos, 1, tokens, -1),
        block_out.reshape(videos, 1, tokens, width),
    )


def solution(mesh):
    in_specs = (
        P(None, "queue", "seq", None),
        P(None, "queue", "seq", None),
        P(None, "queue", "seq", None),
        P(None, "seq", None),
        P(),
        P(),
        P(),
        P("queue", None),
        P(),
        P(),
        P("queue", None),
        P("queue", None),
    )
    out_specs = (P(None, "queue", "seq", None), P(None, "queue", "seq", None))
    return jax.shard_map(shards, mesh=mesh, in_specs=in_specs, out_specs=out_specs, check_vma=False)
```

time: 218 us -> 183 us (0.84)
  blocking collectives: 35.3 us -> 11.4 us
  Pallas kernels: 54.9 us -> 46.8 us
  local copies, waits for them, and re-layouts: 18.3 us -> 10.9 us
  waiting for transfers between devices: 45.4 us -> 48.8 us
    all_to_all x1 -> x0, blocking collectives: 23.9 us -> none  [shards(): lax.all_to_all(packed, 'queue', split_axis=0, concat_axis=0, tiled=True)]
    all_to_all x1, waiting for transfers between devices: 0.36 us -> 13.2 us  [shards(): lax.all_to_all(attended, 'queue', split_axis=0, concat_axis=0, tiled=True)]
    all_to_all x2 -> x1, waiting for transfers between devices: 25.8 us -> 15.5 us  [shards(): lax.all_to_all(packed, 'queue', split_axis=0, concat_axis=0, tiled=True)]
    pallas_call x5, Pallas kernels: 54.9 us -> 46.8 us  [call(): pl.pallas_call(kernel, out_shape=out_shape, in_specs=in_specs, out_specs=...]
    slice x4 -> x2, local copies, waits for them, and re-layouts: 7.6 us -> 0.18 us  [stack_halves(): return jnp.concatenate([weight[:, :half], weight[:, half:]], axis=0)]
    all_to_all x2 -> x1, starting transfers between devices: 12.4 us -> 9.24 us  [shards(): lax.all_to_all(packed, 'queue', split_axis=0, concat_axis=0, tiled=True)]
    broadcast_in_dim x2 -> x0, local copies, waits for them, and re-layouts: 2.67 us -> none  [spread(): copies = jnp.broadcast_to(value[None], (count,) + value.shape)]
  transfers between devices with their start and end apart: 6 -> 6, of which waited for: 4 -> 4; matrix products, arithmetic and copies ran while one was open for 9% -> 7% of each run, Pallas kernels for 24% -> 8%
where the time goes in v1:
time: 183 us; the launch traced here: 182 us
  waiting for transfers between devices  48.8 us (27%)
  Pallas kernels  46.8 us (26%)
  starting transfers between devices  36.7 us (20%)
  between operations  21.6 us (12%)
  blocking collectives  11.4 us (6%)
  local copies, waits for them, and re-layouts  10.9 us (6%)
  other arithmetic  6.34 us (3%)
    pallas_call x5, Pallas kernels, call(): pl.pallas_call(kernel, out_shape=out_shape, in_specs=in_specs, out_specs=...  46.8 us
    all_to_all x1, starting transfers between devices, shards(): lax.all_to_all(jnp.tile(queued, (seqs // videos, 1, 1)), 'seq', split_axi...  17.2 us
    all_to_all x1, waiting for transfers between devices, shards(): lax.all_to_all(packed, 'queue', split_axis=0, concat_axis=0, tiled=True)  15.5 us
    all_to_all x1, waiting for transfers between devices, shards(): lax.all_to_all(jnp.tile(queued, (seqs // videos, 1, 1)), 'seq', split_axi...  15.3 us
    all_to_all x1, waiting for transfers between devices, shards(): lax.all_to_all(attended, 'queue', split_axis=0, concat_axis=0, tiled=True)  13.2 us
    all_to_all x1, blocking collectives, shards(): lax.all_to_all(spatial, 'seq', split_axis=0, concat_axis=0, tiled=True, a...  11.4 us
    all_to_all x1, starting transfers between devices, shards(): lax.all_to_all(packed, 'queue', split_axis=0, concat_axis=0, tiled=True)  9.24 us
    all_to_all x1, starting transfers between devices, shards(): lax.all_to_all(attended, 'queue', split_axis=0, concat_axis=0, tiled=True)  5.62 us
  transfers between devices with their start and end apart: 6, of which 4 were waited for; matrix products, arithmetic and copies ran while one was open for 7% of the time, Pallas kernels for 8%

profile of v1, /device:TPU:24, one launch (start us, length us, event | category | flops | bytes accessed | tf_op | source)
XLA Modules:
  0.0 182.4 jit_solution(8698805870255966247)
XLA Ops:
  7.2 0.0 copy-start.4
  7.2 0.0 all-gather.2.cloned.1.call-start
  7.2 1.2 copy.35
  8.5 0.0 copy-start.5
  8.5 0.1 copy.41
  8.7 0.1 copy.42
  8.9 0.1 copy.43
  9.1 0.1 fusion.8
  9.2 0.8 pad_maximum_fusion
  10.0 0.0 all-gather.2.cloned.1.call-update
  10.0 0.1 constant_dynamic-slice_fusion
  10.1 0.6 pad_maximum_fusion.5.w_ref
  10.8 3.8 %shard_map.149 = bf16[16,72,720]{2,1,0:T(8,128)(2,1)} custom-call(bf16[4,72,1728]{2,1,0:T(8,128)(2,1)} %bitcast.44, bf16[72,288]{1,0:T(8,128)(2,1)} %pad_maximum_fusion.5.w_ref), custom_call_target="tpu_custom_call" | custom-call | bytes 1036800 | tf_op jit(solution)/shard_map/pallas_call | solution.py:39
  14.5 9.2 %all-to-all-start = ((bf16[16,72,720]{2,1,0:T(8,128)(2,1)}), bf16[16,72,720]{2,1,0:T(8,128)(2,1)S(1)}, u32[]{:S(2)}, u32[]{:S(2)}) async-start(bf16[16,72,720]{2,1,0:T(8,128)(2,1)} %shard_map.149), calls=%async_computation | async-start | bytes 3538944 | tf_op jit(solution)/shard_map/all_to_all | solution.py:293
  23.8 0.6 dynamic_slice.24
  27.6 0.6 fusion.9
  30.9 0.1 slice.26
  31.1 0.1 pad_add_fusion
  31.1 0.6 dynamic_slice.29
  33.1 1.0 constant_dynamic-slice_fusion.1
  34.1 0.6 fusion.7.mod_ref
  34.7 15.5 %all-to-all-done.x_ref = bf16[16,72,720]{2,1,0:T(8,128)(2,1)S(1)} async-done(((bf16[16,72,720]{2,1,0:T(8,128)(2,1)}), bf16[16,72,720]{2,1,0:T(8,128)(2,1)S(1)}, u32[]{:S(2)}, u32[]{:S(2)}) %all-to-all-start) | async-done | bytes 1658912 | tf_op jit(solution)/shard_map/all_to_all | solution.py:293
  50.2 1.2 copy-done
  51.4 6.8 %shard_map.150 = (bf16[16,72,160]{2,1,0:T(8,128)(2,1)}, bf16[640,576]{1,0:T(8,128)(2,1)}) custom-call(bf16[16,72,720]{2,1,0:T(8,128)(2,1)} %copy-done, bf16[432,1024]{1,0:T(8,128)(2,1)} %constant.89.clone.pick_ref, bf16[160,144]{1,0:T(8,128)(2,1)} %constant.88.clone.rows_ref), custom_call_target="tpu_custom_call" | custom-call | flops 4000000000 | bytes 2589696 | tf_op jit(solution)/shard_map/pallas_call | solution.py:39
  58.2 1.5 copy.31
  59.7 1.9 %collective-permute-start = (bf16[640,576]{0,1:T(8,128)(2,1)S(1)}, bf16[640,576]{0,1:T(8,128)(2,1)S(1)}, u32[]{:S(2)}, u32[]{:S(2)}) collective-permute-start(bf16[640,576]{0,1:T(8,128)(2,1)S(1)} %copy.31), channel_id=1, source_target_pairs={{0,1},{1,0},{2,3},{3,2},{4,5},{5,4},{6,7},{7,6},{8,9},{9,8},{10,11... | collective-permute-start | bytes 2211848 | tf_op jit(solution)/shard_map/ppermute | solution.py:306
  61.6 0.7 pad_maximum_fusion.6.coef_ref
  62.3 0.4 fusion.5
  62.7 5.6 %all-to-all-start.1 = ((bf16[16,72,160]{2,1,0:T(8,128)(2,1)}), bf16[16,72,160]{2,1,0:T(8,128)(2,1)S(1)}, u32[]{:S(2)}, u32[]{:S(2)}) async-start(bf16[16,72,160]{2,1,0:T(8,128)(2,1)} %get-tuple-element.4), calls=%async_computation.1 | async-start | bytes 1179648 | tf_op jit(solution)/shard_map/all_to_all | solution.py:307
  68.3 0.6 fusion.6.mod_ref
  68.9 0.0 collective-permute-done
  68.9 1.2 copy.33.other_ref
  70.1 13.2 %all-to-all-done.1.att_ref = bf16[16,72,160]{2,1,0:T(8,128)(2,1)S(1)} async-done(((bf16[16,72,160]{2,1,0:T(8,128)(2,1)}), bf16[16,72,160]{2,1,0:T(8,128)(2,1)S(1)}, u32[]{:S(2)}, u32[]{:S(2)}) %all-to-all-start.1) | async-done | bytes 368672 | tf_op jit(solution)/shard_map/all_to_all | solution.py:307
  83.4 0.8 copy-done.1
  84.2 4.4 %shard_map.151 = bf16[4,16,72]{2,1,0:T(8,128)(2,1)} custom-call(f32[4]{0:T(128)} %pad_maximum_fusion.6.coef_ref, s32[1]{0:T(128)} %bitcast.2.core_ref, bf16[16,72,160]{2,1,0:T(8,128)(2,1)} %copy-done.1, bf16[4,72,1152]{2,1,0:T(8,128)(2,1)} %bitcast.50, bf16[4,16,72]{2,1,0:T(8,128)(2,1)} %bitcast.52, bf16[640,576]{1,0:T(8,128)(2,1)} %get-tuple-element.5.mine_ref, ...), custom_call_target="tpu_custom_call" | custom-call | flops 1000000000 | bytes 2580500 | tf_op jit(solution)/shard_map/pallas_call | solution.py:39
  88.6 2.7 %collective-permute-start.1 = (bf16[4,16,72]{2,1,0:T(8,128)(2,1)}, bf16[4,16,72]{2,1,0:T(8,128)(2,1)S(1)}, u32[]{:S(2)}, u32[]{:S(2)}) collective-permute-start(bf16[4,16,72]{2,1,0:T(8,128)(2,1)} %shard_map.151), channel_id=1, source_target_pairs={{32,0},{64,32},{96,64},{128,96},{160,128},{192,160},{224,192},{256... | collective-permute-start | bytes 27656 | tf_op jit(solution)/shard_map/ppermute | solution.py:336
  91.3 0.8 pad_maximum_fusion.4
  92.2 4.7 %collective-permute-done.1 = bf16[4,16,72]{2,1,0:T(8,128)(2,1)S(1)} collective-permute-done((bf16[4,16,72]{2,1,0:T(8,128)(2,1)}, bf16[4,16,72]{2,1,0:T(8,128)(2,1)S(1)}, u32[]{:S(2)}, u32[]{:S(2)}) %collective-permute-start.1) | collective-permute-done | bytes 9248 | tf_op jit(solution)/shard_map/ppermute | solution.py:336
  96.9 0.0 copy-start.2
  96.9 0.7 tile.4
  97.6 17.2 %all-to-all-start.2 = ((bf16[32,16,72]{2,1,0:T(8,128)(2,1)}), bf16[32,16,72]{2,1,0:T(8,128)(2,1)S(1)}, u32[]{:S(2)}, u32[]{:S(2)}) async-start(bf16[32,16,72]{2,1,0:T(8,128)(2,1)} %bitcast.14), calls=%async_computation.2 | async-start | bytes 262144 | tf_op jit(solution)/shard_map/all_to_all | solution.py:339
  114.7 0.7 fusion.2
  115.4 1.0 pad_maximum_fusion.1
  116.5 15.3 %all-to-all-done.2.lat_ref = bf16[32,16,72]{2,1,0:T(8,128)(2,1)S(1)} async-done(((bf16[32,16,72]{2,1,0:T(8,128)(2,1)}), bf16[32,16,72]{2,1,0:T(8,128)(2,1)S(1)}, u32[]{:S(2)}, u32[]{:S(2)}) %all-to-all-start.2) | async-done | bytes 73760 | tf_op jit(solution)/shard_map/all_to_all | solution.py:339
  131.8 0.6 copy-done.3
  132.4 26.6 %shard_map.152 = bf16[4,72,640]{2,1,0:T(8,128)(2,1)} custom-call(s32[1]{0:T(128)} %bitcast.13.group_ref, bf16[32,16,72]{2,1,0:T(8,128)(2,1)} %copy-done.3, bf16[16,1152]{1,0:T(8,128)(2,1)} %wemb_ref.3, f32[32,1152]{1,0:T(8,128)} %get-tuple-element.22.ua_ref, f32[32,1152]{1,0:T(8,128)} %get-tuple-element.21.va_ref, f32[72,1152]{1,0:T(8,128)} %get-tuple-element.30.cb_ref, ...), custom_call_target="tpu_custom_call" | custom-call | flops 20000000000 | bytes 6994948 | tf_op jit(solution)/shard_map/pallas_call | solution.py:39
  159.1 11.4 %all_to_all.20.att_ref = bf16[4,72,640]{2,1,0:T(8,128)(2,1)} all-to-all(bf16[4,72,640]{2,1,0:T(8,128)(2,1)} %shard_map.152), channel_id=1, replica_groups={{0,1,2,3},{4,5,6,7},{8,9,10,11},{12,13,14,15},{16,17,18,19},{20,21,22,2..., dimensions={0} | all-to-all | bytes 737280 | tf_op jit(solution)/shard_map/all_to_all | solution.py:363
  170.5 5.1 %shard_map.153 = bf16[4,72,1152]{2,1,0:T(8,128)(2,1)} custom-call(s32[1]{0:T(128)} %bitcast.12.seq_ref, bf16[4,72,640]{2,1,0:T(8,128)(2,1)} %all_to_all.20.att_ref, bf16[4,16,72]{2,1,0:T(8,128)(2,1)} %copy-done.2, bf16[16,1152]{1,0:T(8,128)(2,1)} %wemb_ref.3, f32[32,1152]{1,0:T(8,128)} %get-tuple-element.22.ua_ref, f32[32,1152]{1,0:T(8,128)} %get-tuple-element.21.va_ref, ...), custom_call_target="tpu_custom_call" | custom-call | flops 1000000000 | bytes 7345156 | tf_op jit(solution)/shard_map/pallas_call | solution.py:39
  (21 shorter events, 0.2 us)
Async XLA Ops:
  7.2 1.9 %copy-start.4 = (bf16[36,1152]{1,0:T(8,128)(2,1)S(1)}, bf16[36,1152]{1,0:T(8,128)(2,1)}, u32[]{:S(2)}) copy-start(bf16[36,1152]{1,0:T(8,128)(2,1)} %param.25) | copy-start | bytes 248836
  7.2 124.6 %all-gather.2.cloned.1.call-start = ((), (), s32[]{:S(2)}) async-start(), calls=%async_computation.4 | async-start | bytes 6266880 | tf_op jit(solution)/shard_map/all_gather | solution.py:275
  8.5 1.6 copy-start.5
  14.5 9.2 %copy-start.8 = (s32[16]{0:T(128)S(1)}, s32[16]{0:T(128)}, u32[]{:S(2)}) copy-start(s32[16]{0:T(128)} %param.18) | copy-start | bytes 196
  14.5 13.1 %copy-start.7 = (f32[65]{0:T(128)S(1)}, f32[65]{0:T(128)}, u32[]{:S(2)}) copy-start(f32[65]{0:T(128)} %param.19) | copy-start | bytes 784
  14.5 35.6 %all-to-all-start = ((bf16[16,72,720]{2,1,0:T(8,128)(2,1)}), bf16[16,72,720]{2,1,0:T(8,128)(2,1)S(1)}, u32[]{:S(2)}, u32[]{:S(2)}) async-start(bf16[16,72,720]{2,1,0:T(8,128)(2,1)} %shard_map.149), calls=%async_computation | async-start | bytes 3538944 | tf_op jit(solution)/shard_map/all_to_all | solution.py:293
  50.2 1.2 copy-start
  59.7 9.2 %collective-permute-start = (bf16[640,576]{0,1:T(8,128)(2,1)S(1)}, bf16[640,576]{0,1:T(8,128)(2,1)S(1)}, u32[]{:S(2)}, u32[]{:S(2)}) collective-permute-start(bf16[640,576]{0,1:T(8,128)(2,1)S(1)} %copy.31), channel_id=1, source_target_pairs={{0,1},{1,0},{2,3},{3,2},{4,5},{5,4},{6,7},{7,6},{8,9},{9,8},{10,11... | collective-permute-start | bytes 2211848 | tf_op jit(solution)/shard_map/ppermute | solution.py:306
  62.7 20.7 %all-to-all-start.1 = ((bf16[16,72,160]{2,1,0:T(8,128)(2,1)}), bf16[16,72,160]{2,1,0:T(8,128)(2,1)S(1)}, u32[]{:S(2)}, u32[]{:S(2)}) async-start(bf16[16,72,160]{2,1,0:T(8,128)(2,1)} %get-tuple-element.4), calls=%async_computation.1 | async-start | bytes 1179648 | tf_op jit(solution)/shard_map/all_to_all | solution.py:307
  83.4 0.8 copy-start.1
  84.2 12.7 %copy-start.6 = (bf16[4,72,16]{1,2,0:T(8,128)(2,1)S(1)}, bf16[4,72,16]{1,2,0:T(8,128)(2,1)}, u32[]{:S(2)}) copy-start(bf16[4,72,16]{1,2,0:T(8,128)(2,1)} %param.17) | copy-start | bytes 27652
  88.6 8.3 %collective-permute-start.1 = (bf16[4,16,72]{2,1,0:T(8,128)(2,1)}, bf16[4,16,72]{2,1,0:T(8,128)(2,1)S(1)}, u32[]{:S(2)}, u32[]{:S(2)}) collective-permute-start(bf16[4,16,72]{2,1,0:T(8,128)(2,1)} %shard_map.151), channel_id=1, source_target_pairs={{32,0},{64,32},{96,64},{128,96},{160,128},{192,160},{224,192},{256... | collective-permute-start | bytes 27656 | tf_op jit(solution)/shard_map/ppermute | solution.py:336
  96.9 62.2 %copy-start.2 = (bf16[4,16,72]{2,1,0:T(8,128)(2,1)}, bf16[4,16,72]{2,1,0:T(8,128)(2,1)S(1)}, u32[]{:S(2)}) copy-start(bf16[4,16,72]{2,1,0:T(8,128)(2,1)S(1)} %bitcast_select_fusion.lat_ref) | copy-start | bytes 27652
  97.6 34.2 %all-to-all-start.2 = ((bf16[32,16,72]{2,1,0:T(8,128)(2,1)}), bf16[32,16,72]{2,1,0:T(8,128)(2,1)S(1)}, u32[]{:S(2)}, u32[]{:S(2)}) async-start(bf16[32,16,72]{2,1,0:T(8,128)(2,1)} %bitcast.14), calls=%async_computation.2 | async-start | bytes 262144 | tf_op jit(solution)/shard_map/all_to_all | solution.py:339
  131.8 0.6 copy-start.3
Sparse Core Ops, SparseCore 0:
  11.1 91.3 all-gather.1

commit v2 on v1

--- a/solution.py
+++ b/solution.py
@@ -82,7 +82,7 @@
     return pick
 
 
-def temporal_kernel(x_ref, pick_ref, rows_ref, o_ref, w_ref, parts, total):
+def temporal_kernel(x_ref, pick_ref, o_ref, parts, total):
     frames, tokens, _ = x_ref.shape
     pick = pick_ref[...]
     for f in range(frames):
@@ -107,8 +107,13 @@
             out = found if out is None else out + found
         total[:, 8 * block : 8 * block + 8, :] = out.reshape(frames, 8, 2 * SLOT)
     o_ref[...] = total[...].astype(BF16)
-    for h in range(frames // 2):
-        pair = x_ref[2 * h : 2 * h + 2, :, 6 * HDIM :].astype(F32).reshape(2 * tokens, -1).astype(BF16)
+
+
+def unstack_kernel(x_ref, rows_ref, w_ref):
+    shards, rows, width = x_ref.shape
+    start = width - w_ref.shape[-1] // 2
+    for h in range(shards // 2):
+        pair = x_ref[2 * h : 2 * h + 2, :, start:].astype(F32).reshape(2 * rows, -1).astype(BF16)
         both = mm(rows_ref[...], pair)
         w_ref[SLOT * h : SLOT * (h + 1), :] = jnp.concatenate(
             [both[:SLOT], both[SLOT:]], axis=-1
@@ -138,60 +143,89 @@
         o_ref[v] = (coef_ref[2] * clean + coef_ref[3] * pred).astype(BF16)
 
 
+def place_kernel(mod_ref, ua_ref, va_ref, cb_ref, sb_ref, o_ref):
+    tokens = cb_ref.shape[0]
+    members = o_ref.shape[0] // tokens
+    gain = 1.0 + mod_ref[4:5, :]
+    made = []
+    for i in range(members):
+        c = pl.program_id(0) * members + i
+        place = ua_ref[pl.ds(c, 1), :] * cb_ref[...] + va_ref[pl.ds(c, 1), :] * sb_ref[...]
+        made.append((place - jnp.mean(place, axis=-1, keepdims=True)) * gain)
+    o_ref[...] = jnp.concatenate(made, axis=0).astype(BF16)
+
+
+def prepare_kernel(group_ref, few_ref, p_ref, w_ref, few_out, q_out, kv_out):
+    kv_out[...] = mm(p_ref[...], w_ref[:, : 2 * PADDED])
+
+    @pl.when(pl.program_id(0) == group_ref[0])
+    def _():
+        q_out[...] = mm(p_ref[...], w_ref[:, 2 * PADDED :])
+
+    @pl.when(pl.program_id(0) == 0)
+    def _():
+        few_out[...] = mm(few_ref[...], w_ref[...])
+
+
 def spatial_kernel(
-    group_ref, lat_ref, wemb_ref, ua_ref, va_ref, cb_ref, sb_ref, mod_ref, w_ref,
-    o_ref, even, odd, own, keys, vals, ws, sem,
+    group_ref, lat_ref, wemb_ref, ua_ref, va_ref, cb_ref, sb_ref, few_ref, pq_ref, pkv_ref,
+    o_ref, held, keys, vals, qs, sem,
 ):
-    chunks, _, tokens = lat_ref.shape
+    chunks, patch, tokens = lat_ref.shape
     members = o_ref.shape[0]
     block = members * tokens
     blocks = chunks // members
-    copy = pltpu.make_async_copy(w_ref.at[:, : 3 * PADDED], ws, sem)
-    copy.start()
     wemb = wemb_ref[...]
-    gain = 1.0 + mod_ref[4:5, :]
-    shift = mod_ref[3:4, :]
-    lane = lax.broadcasted_iota(jnp.int32, (1, PADDED), 1)
-    ones = jnp.where(lane % SLOT == HDIM, 1.0, 0.0)
-
-    def build(index, x_ref):
-        made = []
+    lane = lax.broadcasted_iota(jnp.int32, (1, 2 * PADDED), 1)
+    ones = jnp.where((lane >= PADDED) & (lane % SLOT == HDIM), 1.0, 0.0)
+    few = few_ref[...]
+    mix = few[:patch] + few[patch : 2 * patch]
+    offset = few[2 * patch : 2 * patch + 1] + few[2 * patch + 8 : 2 * patch + 9]
+    high = mix.astype(BF16).astype(F32)
+    mix = jnp.concatenate([high, mix - high], axis=0).astype(BF16)
+    kv_mix, q_mix = mix[:, : 2 * PADDED], mix[:, 2 * PADDED :]
+    kv_offset, q_offset = offset[:, : 2 * PADDED] + ones, offset[:, 2 * PADDED :]
+
+    def fetch(index):
+        start = pl.multiple_of(index * block, block)
+        slot = index % 2
+        return pltpu.make_async_copy(pkv_ref.at[pl.ds(start, block), :], held.at[slot], sem.at[slot])
+
+    fetch(0).start()
+
+    def one(index, carry):
+        @pl.when(index + 1 < blocks)
+        def _():
+            fetch(index + 1).start()
+
+        latents, scales = [], []
         for i in range(members):
             c = index * members + i
-            latent = lat_ref[c].astype(F32).T.astype(BF16)
+            once = lat_ref[c].astype(F32)
+            latent = jnp.concatenate([once, once], axis=0).T
             place = ua_ref[pl.ds(c, 1), :] * cb_ref[...] + va_ref[pl.ds(c, 1), :] * sb_ref[...]
-            embedded = mm(latent, wemb) + place
-            made.append(layer_norm(embedded) * gain + shift)
-            if i % 2:
-                x_ref[tokens * (i - 1) : tokens * (i + 1), :] = jnp.concatenate(made, axis=0).astype(BF16)
-                made = []
-
-    def project(index, x_ref):
+            embedded = mm(latent.astype(BF16), wemb) + place
+            center = embedded - jnp.mean(embedded, axis=-1, keepdims=True)
+            scales.append(lax.rsqrt(jnp.mean(center * center, axis=-1, keepdims=True) + 1e-06))
+            latents.append(latent)
+        latent = jnp.concatenate(latents, axis=0).astype(BF16)
+        scale = jnp.concatenate(scales, axis=0)
+        fetch(index).wait()
         start = pl.multiple_of(index * block, block)
-        x = x_ref[...]
-        keys[pl.ds(start, block), :] = mm(x, ws[:, :PADDED]).astype(BF16)
-        vals[pl.ds(start, block), :] = (mm(x, ws[:, PADDED : 2 * PADDED]) + ones).astype(BF16)
-
-    def keep(index, x_ref):
+        kv = (mm(latent, kv_mix) + held[index % 2]) * scale + kv_offset
+        keys[pl.ds(start, block), :] = kv[:, :PADDED].astype(BF16)
+        vals[pl.ds(start, block), :] = kv[:, PADDED:].astype(BF16)
+
         @pl.when(index == group_ref[0])
         def _():
-            own[...] = x_ref[...]
-
-    build(0, even)
-    copy.wait()
-
-    def two(step, carry):
-        project(2 * step, even)
-        build(2 * step + 1, odd)
-        keep(2 * step, even)
-        project(2 * step + 1, odd)
-        build(jnp.minimum(2 * step + 2, blocks - 1), even)
-        keep(2 * step + 1, odd)
+            qs[...] = ((mm(latent, q_mix) + pq_ref[...]) * scale + q_offset).astype(BF16)
+
         return carry
 
-    lax.fori_loop(0, blocks // 2, two, 0)
-
-    q_all = mm(own[...], ws[:, 2 * PADDED :])
+    lax.fori_loop(0, blocks, one, 0)
+
+    lane = lane[:, :PADDED]
+    q_all = qs[...].astype(F32)
     merged = [None] * (PADDED // 128)
     for h in range(HEADS):
         first = SLOT * h // 128
@@ -212,28 +246,32 @@
     o_ref[...] = jnp.concatenate(merged, axis=-1).reshape(members, tokens, PADDED).astype(BF16)
 
 
-def finish_kernel(
-    seq_ref, att_ref, lat_ref, wemb_ref, ua_ref, va_ref, cb_ref, sb_ref, mod_ref, rows_ref, w_ref,
-    o_ref, raw, left, right, sem,
+def residual_kernel(
+    seq_ref, lat_ref, wemb_ref, ua_ref, va_ref, cb_ref, sb_ref, rows_ref, w_ref, emb_out, w_out, raw, sem
 ):
-    videos, tokens, width = o_ref.shape
+    videos, tokens, width = emb_out.shape
     copy = pltpu.make_async_copy(w_ref.at[:, 3 * PADDED :], raw, sem)
     copy.start()
     s = seq_ref[0]
     place = ua_ref[pl.ds(s, 1), :] * cb_ref[...] + va_ref[pl.ds(s, 1), :] * sb_ref[...]
-    att = att_ref[...].astype(F32).reshape(videos * tokens, PADDED).astype(BF16)
-    copy.wait()
-    for h in range(HEADS):
-        both = mm(rows_ref[...], raw[2 * HDIM * h : 2 * HDIM * (h + 1), :]).astype(BF16)
-        left[SLOT * h : SLOT * (h + 1), :] = both[:SLOT]
-        right[SLOT * h : SLOT * (h + 1), :] = both[SLOT:]
-    half = width // 2
-    proj = jnp.concatenate([mm(att, left[...])[:, :half], mm(att, right[...])[:, :half]], axis=-1)
-    gated = proj * mod_ref[5:6, :]
     for v in range(videos):
         latent = lat_ref[v].astype(F32).T.astype(BF16)
-        embedded = mm(latent, wemb_ref[...]) + place
-        o_ref[v] = (embedded + gated[tokens * v : tokens * (v + 1), :]).astype(BF16)
+        emb_out[v] = mm(latent, wemb_ref[...]) + place
+    copy.wait()
+    half = width // 2
+    for h in range(HEADS):
+        both = mm(rows_ref[...], raw[2 * HDIM * h : 2 * HDIM * (h + 1), :])
+        w_out[SLOT * h : SLOT * (h + 1), :] = jnp.concatenate(
+            [both[:SLOT, :half], both[SLOT:, :half]], axis=-1
+        ).astype(BF16)
+
+
+def finish_kernel(att_ref, emb_ref, mod_ref, w_ref, o_ref):
+    videos, tokens, width = o_ref.shape
+    att = att_ref[...].astype(F32).reshape(videos * tokens, PADDED).astype(BF16)
+    gated = mm(att, w_ref[...]) * mod_ref[5:6, :]
+    for v in range(videos):
+        o_ref[v] = (emb_ref[v] + gated[tokens * v : tokens * (v + 1), :]).astype(BF16)
 
 
 def position_factors(chunks, tokens, width):
@@ -254,6 +292,10 @@
     return jnp.concatenate([weight[:, :half], weight[:, half:]], axis=0)
 
 
+def rounding_rest(values):
+    return values - lax.reduce_precision(values, 8, 7)
+
+
 def pad_heads(columns):
     return jnp.pad(columns, ((0, 0), (0, 0), (0, SLOT - HDIM))).reshape(-1, PADDED)
 
@@ -268,11 +310,6 @@
     videos, _, tokens, width = hidden.shape
     top_level = alpha_bar.shape[0] - 1
     pairs = frames // videos
-
-    by_head = w_sqkv.reshape(-1, HEADS, 3, HDIM)
-    sout = jnp.pad(stack_halves(w_sout), ((0, 0), (0, PADDED - width // 2)))
-    w_shard = jnp.concatenate([pad_heads(by_head[:, :, i]) for i in (1, 2, 0)] + [sout], axis=-1)
-    w_spatial = lax.all_gather(w_shard, "queue", axis=0, tiled=True)
 
     core = seq_pos % 2
     half = width // 2
@@ -290,18 +327,27 @@
         ],
         out_specs=pl.BlockSpec((pairs, tokens, sent), lambda v: (v, 0, 0)),
     )
+    w_sqkv, w_sout, packed = lax.optimization_barrier((w_sqkv, w_sout, packed))
+    by_head = w_sqkv.reshape(-1, HEADS, 3, HDIM)
+    sout = jnp.pad(stack_halves(w_sout), ((0, 0), (0, PADDED - width // 2)))
+    w_shard = jnp.concatenate([pad_heads(by_head[:, :, i]) for i in (1, 2, 0)] + [sout], axis=-1)
+    w_spatial = lax.all_gather(w_shard, "queue", axis=0, tiled=True)
+
     arrived = lax.all_to_all(packed, "queue", split_axis=0, concat_axis=0, tiled=True)
     row_pick = jnp.asarray(weight_rows(), BF16)
 
-    attended, w_mine = call(
+    attended = call(
         temporal_kernel,
-        (
-            jax.ShapeDtypeStruct((frames, tokens, 2 * SLOT), BF16),
-            jax.ShapeDtypeStruct((PADDED, half), BF16),
-        ),
-        (arrived, jnp.asarray(temporal_columns(), BF16), row_pick),
+        jax.ShapeDtypeStruct((frames, tokens, 2 * SLOT), BF16),
+        (arrived, jnp.asarray(temporal_columns(), BF16)),
         scratch=[pltpu.VMEM((frames, tokens, 1024), F32), pltpu.VMEM((frames, tokens, 2 * SLOT), F32)],
         flops=4_000_000_000,
+    )
+    w_mine = call(
+        unstack_kernel,
+        jax.ShapeDtypeStruct((PADDED, half), BF16),
+        (arrived, row_pick),
+        flops=1_000_000_000,
     )
     w_other = lax.ppermute(w_mine, "seq", [(i, i ^ 1) for i in range(seqs)])
     returned = lax.all_to_all(attended, "queue", split_axis=0, concat_axis=0, tiled=True)
@@ -343,38 +389,80 @@
     groups = [[videos * g + i for i in range(videos)] for g in range(seqs // videos)]
     rows = seqs * tokens
     own_rows = videos * tokens
+    group = (seq_pos // videos).reshape(1)
+    placed = call(
+        place_kernel,
+        jax.ShapeDtypeStruct((rows, width), BF16),
+        (new_mods, ua, va, cb, sb),
+        grid=(rows // own_rows,),
+        in_specs=[pl.BlockSpec(a.shape, lambda i: (0, 0)) for a in (new_mods, ua, va, cb, sb)],
+        out_specs=pl.BlockSpec((own_rows, width), lambda i: (i, 0)),
+        flops=100_000_000,
+    )
+    gain, shift = 1.0 + new_mods[4:5], new_mods[3:4]
+    emb_f32 = w_embed.astype(F32)
+    centered = (emb_f32 - jnp.mean(emb_f32, axis=-1, keepdims=True)) * gain
+    eight = jnp.zeros((7, width), F32)
+    few = [centered, rounding_rest(centered), shift, eight, rounding_rest(shift), eight]
+    few = jnp.concatenate(few, axis=0).astype(BF16)
+    few_out, pq, pkv = call(
+        prepare_kernel,
+        (
+            jax.ShapeDtypeStruct((few.shape[0], 3 * PADDED), F32),
+            jax.ShapeDtypeStruct((own_rows, PADDED), F32),
+            jax.ShapeDtypeStruct((rows, 2 * PADDED), F32),
+        ),
+        (group, few, placed, w_spatial),
+        grid=(rows // own_rows,),
+        in_specs=[
+            pl.BlockSpec(memory_space=pltpu.SMEM),
+            pl.BlockSpec(few.shape, lambda i: (0, 0)),
+            pl.BlockSpec((own_rows, width), lambda i: (i, 0)),
+            pl.BlockSpec((width, 3 * PADDED), lambda i: (0, 0)),
+        ],
+        out_specs=(
+            pl.BlockSpec((few.shape[0], 3 * PADDED), lambda i: (0, 0)),
+            pl.BlockSpec((own_rows, PADDED), lambda i: (0, 0)),
+            pl.BlockSpec((own_rows, 2 * PADDED), lambda i: (i, 0)),
+        ),
+        flops=8_000_000_000,
+    )
+    wemb_twice = jnp.concatenate([w_embed, jnp.zeros_like(w_embed)], axis=0)
     spatial = call(
         spatial_kernel,
         jax.ShapeDtypeStruct((videos, tokens, PADDED), BF16),
-        ((seq_pos // videos).reshape(1), everyone, w_embed, ua, va, cb, sb, new_mods, w_spatial),
+        (group, everyone, wemb_twice, ua, va, cb, sb, few_out, pq, pkv),
         scratch=[
-            pltpu.VMEM((own_rows, width), BF16),
-            pltpu.VMEM((own_rows, width), BF16),
-            pltpu.VMEM((own_rows, width), BF16),
+            pltpu.VMEM((2, own_rows, 2 * PADDED), F32),
             pltpu.VMEM((rows, PADDED), BF16),
             pltpu.VMEM((rows, PADDED), BF16),
-            pltpu.VMEM((width, 3 * PADDED), BF16),
-            pltpu.SemaphoreType.DMA,
+            pltpu.VMEM((own_rows, PADDED), BF16),
+            pltpu.SemaphoreType.DMA((2,)),
         ],
         smem=(0,),
-        hbm=(8,),
+        hbm=(9,),
         flops=20_000_000_000,
     )
     heads_out = lax.all_to_all(
         spatial, "seq", split_axis=0, concat_axis=0, tiled=True, axis_index_groups=groups
+    )
+    late, _ = lax.optimization_barrier((w_spatial, spatial))
+    embedded, w_s = call(
+        residual_kernel,
+        (
+            jax.ShapeDtypeStruct((videos, tokens, width), F32),
+            jax.ShapeDtypeStruct((PADDED, width), BF16),
+        ),
+        (seq_pos.reshape(1), queued, w_embed, ua, va, cb, sb, row_pick, late),
+        scratch=[pltpu.VMEM((width, PADDED), BF16), pltpu.SemaphoreType.DMA],
+        smem=(0,),
+        hbm=(8,),
+        flops=1_000_000_000,
     )
     block_out = call(
         finish_kernel,
         jax.ShapeDtypeStruct((videos, tokens, width), BF16),
-        (seq_pos.reshape(1), heads_out, queued, w_embed, ua, va, cb, sb, new_mods, row_pick, w_spatial),
-        scratch=[
-            pltpu.VMEM((width, PADDED), BF16),
-            pltpu.VMEM((PADDED, PADDED), BF16),
-            pltpu.VMEM((PADDED, PADDED), BF16),
-            pltpu.SemaphoreType.DMA,
-        ],
-        smem=(0,),
-        hbm=(10,),
+        (heads_out, embedded, new_mods, w_s),
         flops=1_000_000_000,
     )
     return (

time: 183 us -> 178 us (0.973); the launches traced: 182 us -> 175 us
  waiting for transfers between devices: 48.8 us -> 25.3 us
  Pallas kernels: 46.8 us -> 66.7 us
  blocking collectives: 11.4 us -> 0 us
  local copies, waits for them, and re-layouts: 10.9 us -> 14.8 us
  starting transfers between devices: 36.7 us -> 39.6 us
    pallas_call x5 -> x9, Pallas kernels: 46.8 us -> 66.7 us  [call(): pl.pallas_call(kernel, out_shape=out_shape, in_specs=in_specs, out_specs=...]
    all_to_all x1, waiting for transfers between devices: 15.3 us -> 0.86 us  [shards(): lax.all_to_all(jnp.tile(queued, (seqs // videos, 1, 1)), 'seq', split_axi...]
    all_to_all x1 -> x0, blocking collectives: 11.4 us -> none  [shards(): lax.all_to_all(spatial, 'seq', split_axis=0, concat_axis=0, tiled=True, a...]
    all_to_all x1, waiting for transfers between devices: 15.5 us -> 7.95 us  [shards(): lax.all_to_all(packed, 'queue', split_axis=0, concat_axis=0, tiled=True)]
    ppermute x1, waiting for transfers between devices: 4.71 us -> 0.01 us  [shards(): lax.ppermute(stepped, 'queue', [(f, f - 1) for f in range(1, frames)])]
    all_to_all x1, starting transfers between devices: 17.2 us -> 13.6 us  [shards(): lax.all_to_all(jnp.tile(queued, (seqs // videos, 1, 1)), 'seq', split_axi...]
    all_to_all x0 -> x1, starting transfers between devices: none -> 3.47 us  [shards(): lax.all_to_all(spatial, 'seq', split_axis=0, concat_axis=0, tiled=True, a...]
    concatenate x0 -> x2, local copies, waits for them, and re-layouts: none -> 3.12 us  [the longest x1 2.49 us: shards(): few = jnp.concatenate(few, axis=0).astype(BF16)]
  transfers between devices with their start and end apart: 6 -> 7, of which waited for: 4 -> 4; matrix products, arithmetic and copies ran while one was open for 7% -> 8% of each run, Pallas kernels for 8% -> 23%
where the time goes in v2:
time: 178 us; the launch traced here: 175 us
  Pallas kernels  66.7 us (37%)
  starting transfers between devices  39.6 us (22%)
  waiting for transfers between devices  25.3 us (14%)
  between operations  21.6 us (12%)
  local copies, waits for them, and re-layouts  14.8 us (8%)
  other arithmetic  6.58 us (4%)
    pallas_call x9, Pallas kernels, call(): pl.pallas_call(kernel, out_shape=out_shape, in_specs=in_specs, out_specs=...  66.7 us
    all_to_all x1, waiting for transfers between devices, shards(): lax.all_to_all(attended, 'queue', split_axis=0, concat_axis=0, tiled=True)  13.8 us
    all_to_all x1, starting transfers between devices, shards(): lax.all_to_all(jnp.tile(queued, (seqs // videos, 1, 1)), 'seq', split_axi...  13.6 us
    all_to_all x1, starting transfers between devices, shards(): lax.all_to_all(packed, 'queue', split_axis=0, concat_axis=0, tiled=True)  9.25 us
    all_to_all x1, starting transfers between devices, shards(): lax.all_to_all(attended, 'queue', split_axis=0, concat_axis=0, tiled=True)  8.62 us
    all_to_all x1, waiting for transfers between devices, shards(): lax.all_to_all(packed, 'queue', split_axis=0, concat_axis=0, tiled=True)  7.95 us
  transfers between devices with their start and end apart: 7, of which 4 were waited for; matrix products, arithmetic and copies ran while one was open for 8% of the time, Pallas kernels for 23%

profile of v2, /device:TPU:24, one launch (start us, length us, event | category | flops | bytes accessed | tf_op | source)
XLA Modules:
  0.0 174.6 jit_solution(7355623074700140280)
XLA Ops:
  7.2 1.0 constant_dynamic-slice_fusion
  8.2 0.6 pad_maximum_fusion.5.w_ref
  8.9 3.8 %shard_map.149 = bf16[16,72,720]{2,1,0:T(8,128)(2,1)} custom-call(bf16[4,72,1728]{2,1,0:T(8,128)(2,1)} %bitcast.47, bf16[72,288]{1,0:T(8,128)(2,1)} %pad_maximum_fusion.5.w_ref), custom_call_target="tpu_custom_call" | custom-call | bytes 1036800 | tf_op jit(solution)/shard_map/pallas_call | solution.py:39
  12.7 0.3 copy.35
  13.1 0.1 copy.41
  13.3 0.1 copy.43
  13.5 0.1 copy.42
  13.6 0.8 pad_maximum_fusion
  14.5 9.3 %all-to-all-start = ((bf16[16,72,720]{2,1,0:T(8,128)(2,1)}), bf16[16,72,720]{2,1,0:T(8,128)(2,1)S(1)}, u32[]{:S(2)}, u32[]{:S(2)}) async-start(bf16[16,72,720]{2,1,0:T(8,128)(2,1)} %shard_map.149), calls=%async_computation | async-start | bytes 3538944 | tf_op jit(solution)/shard_map/all_to_all | solution.py:336
  23.8 0.6 dynamic_slice.24
  25.8 0.6 dynamic_slice.29
  28.3 0.1 convert_reduce_fusion
  28.4 1.0 constant_dynamic-slice_fusion.1
  29.5 0.6 fusion.13
  30.1 0.1 fusion.7
  31.5 0.6 fusion.15
  34.8 0.6 concatenate.32.wemb_ref
  35.6 2.5 %concatenate.38.few_ref = bf16[48,1152]{1,0:T(8,128)(2,1)} concatenate(bf16[16,1152]{1,0:T(8,128)(2,1)S(1)} %get-tuple-element.38, bf16[16,1152]{1,0:T(8,128)(2,1)S(1)} %get-tuple-element.37, bf16[1,1152]{1,0:T(2,128)(2,1)S(1)} %fusion.12, bf16[7,1152]{1,0:T(8,128)(2,1)S(1)} %broadcast_in_dim.2, bf16[1,1152]{1,0:T(2,128)(2,1)S(1)} %fusion.10, bf16[7,1152]{1,0:T(8,128)(2,1)S(1)} %broadcast_in_dim.2), dimensions={0} | concatenate | bytes 221184 | tf_op jit(solution)/shard_map/concatenate | solution.py:407
  38.1 0.4 fusion.8
  38.4 0.7 fusion.2
  39.1 0.9 pad_maximum_fusion.4
  40.0 0.6 fusion.9.mod_ref
  40.6 8.0 %all-to-all-done.x_ref = bf16[16,72,720]{2,1,0:T(8,128)(2,1)S(1)} async-done(((bf16[16,72,720]{2,1,0:T(8,128)(2,1)}), bf16[16,72,720]{2,1,0:T(8,128)(2,1)S(1)}, u32[]{:S(2)}, u32[]{:S(2)}) %all-to-all-start) | async-done | bytes 1658912 | tf_op jit(solution)/shard_map/all_to_all | solution.py:336
  48.5 1.2 copy-done
  49.8 3.0 %shard_map.151.mine_ref = bf16[640,576]{1,0:T(8,128)(2,1)} custom-call(bf16[16,72,720]{2,1,0:T(8,128)(2,1)} %copy-done, bf16[160,144]{1,0:T(8,128)(2,1)} %constant.98.clone.rows_ref), custom_call_target="tpu_custom_call" | custom-call | flops 1000000000 | bytes 1704960 | tf_op jit(solution)/shard_map/pallas_call | solution.py:39
  52.8 1.5 copy.31
  54.3 1.9 %collective-permute-start = (bf16[640,576]{0,1:T(8,128)(2,1)S(1)}, bf16[640,576]{0,1:T(8,128)(2,1)S(1)}, u32[]{:S(2)}, u32[]{:S(2)}) collective-permute-start(bf16[640,576]{0,1:T(8,128)(2,1)S(1)} %copy.31), channel_id=1, source_target_pairs={{0,1},{1,0},{2,3},{3,2},{4,5},{5,4},{6,7},{7,6},{8,9},{9,8},{10,11... | collective-permute-start | bytes 2211848 | tf_op jit(solution)/shard_map/ppermute | solution.py:352
  56.2 6.4 %shard_map.150 = bf16[16,72,160]{2,1,0:T(8,128)(2,1)} custom-call(bf16[16,72,720]{2,1,0:T(8,128)(2,1)} %copy-done, bf16[432,1024]{1,0:T(8,128)(2,1)} %constant.99.clone.pick_ref), custom_call_target="tpu_custom_call" | custom-call | flops 4000000000 | bytes 2543616 | tf_op jit(solution)/shard_map/pallas_call | solution.py:39
  62.6 8.6 %all-to-all-start.1 = ((bf16[16,72,160]{2,1,0:T(8,128)(2,1)}), bf16[16,72,160]{2,1,0:T(8,128)(2,1)S(1)}, u32[]{:S(2)}, u32[]{:S(2)}) async-start(bf16[16,72,160]{2,1,0:T(8,128)(2,1)} %shard_map.150), calls=%async_computation.1 | async-start | bytes 1179648 | tf_op jit(solution)/shard_map/all_to_all | solution.py:353
  71.2 0.7 pad_maximum_fusion.6.coef_ref
  71.9 1.0 pad_maximum_fusion.1
  72.9 1.2 copy.33.other_ref
  74.1 13.8 %all-to-all-done.1.att_ref = bf16[16,72,160]{2,1,0:T(8,128)(2,1)S(1)} async-done(((bf16[16,72,160]{2,1,0:T(8,128)(2,1)}), bf16[16,72,160]{2,1,0:T(8,128)(2,1)S(1)}, u32[]{:S(2)}, u32[]{:S(2)}) %all-to-all-start.1) | async-done | bytes 368672 | tf_op jit(solution)/shard_map/all_to_all | solution.py:353
  87.9 0.8 copy-done.3
  88.8 4.4 %shard_map.152 = bf16[4,16,72]{2,1,0:T(8,128)(2,1)} custom-call(f32[4]{0:T(128)} %pad_maximum_fusion.6.coef_ref, s32[1]{0:T(128)} %bitcast.2.core_ref, bf16[16,72,160]{2,1,0:T(8,128)(2,1)} %copy-done.3, bf16[4,72,1152]{2,1,0:T(8,128)(2,1)} %bitcast.53, bf16[4,16,72]{2,1,0:T(8,128)(2,1)} %bitcast.55, bf16[640,576]{1,0:T(8,128)(2,1)} %shard_map.151.mine_ref, ...), custom_call_target="tpu_custom_call" | custom-call | flops 1000000000 | bytes 2580500 | tf_op jit(solution)/shard_map/pallas_call | solution.py:39
  93.1 2.8 %collective-permute-start.1 = (bf16[4,16,72]{2,1,0:T(8,128)(2,1)}, bf16[4,16,72]{2,1,0:T(8,128)(2,1)S(1)}, u32[]{:S(2)}, u32[]{:S(2)}) collective-permute-start(bf16[4,16,72]{2,1,0:T(8,128)(2,1)} %shard_map.152), channel_id=1, source_target_pairs={{32,0},{64,32},{96,64},{128,96},{160,128},{192,160},{224,192},{256... | collective-permute-start | bytes 27656 | tf_op jit(solution)/shard_map/ppermute | solution.py:382
  95.9 6.5 %shard_map.153.p_ref = bf16[2304,1152]{1,0:T(8,128)(2,1)} custom-call(f32[6,1152]{1,0:T(8,128)} %get-tuple-element.39.mod_ref, f32[32,1152]{1,0:T(8,128)} %get-tuple-element.36.ua_ref, f32[32,1152]{1,0:T(8,128)} %get-tuple-element.35.va_ref, f32[72,1152]{1,0:T(8,128)} %get-tuple-element.48.cb_ref, f32[72,1152]{1,0:T(8,128)} %get-tuple-element.49.sb_ref), custom_call_target="tpu_custom_call" | custom-call | flops 100000000 | bytes 986112 | tf_op jit(solution)/shard_map/pallas_call | solution.py:39
  102.4 0.7 tile.4
  103.1 13.6 %all-to-all-start.2 = ((bf16[32,16,72]{2,1,0:T(8,128)(2,1)}), bf16[32,16,72]{2,1,0:T(8,128)(2,1)S(1)}, u32[]{:S(2)}, u32[]{:S(2)}) async-start(bf16[32,16,72]{2,1,0:T(8,128)(2,1)} %bitcast.13), calls=%async_computation.2 | async-start | bytes 262144 | tf_op jit(solution)/shard_map/all_to_all | solution.py:385
  116.7 16.1 %shard_map.154 = (f32[48,1920]{1,0:T(8,128)}, f32[288,640]{1,0:T(8,128)}, f32[2304,1280]{1,0:T(8,128)}) custom-call(s32[1]{0:T(128)} %bitcast.12.group_ref, bf16[48,1152]{1,0:T(8,128)(2,1)} %concatenate.38.few_ref, bf16[2304,1152]{1,0:T(8,128)(2,1)} %shard_map.153.p_ref, bf16[1152,2560]{1,0:T(8,128)(2,1)} %all-gather.2.cloned.1.call-done.w_ref), custom_call_target="tpu_custom_call" | custom-call | flops 8000000000 | bytes 11317252 | tf_op jit(solution)/shard_map/pallas_call | solution.py:39
  132.9 0.9 all-to-all-done.2.lat_ref
  133.7 0.6 copy-done.6
  134.4 18.6 %shard_map.155 = bf16[4,72,640]{2,1,0:T(8,128)(2,1)} custom-call(s32[1]{0:T(128)} %bitcast.12.group_ref, bf16[32,16,72]{2,1,0:T(8,128)(2,1)} %copy-done.6, bf16[32,1152]{1,0:T(8,128)(2,1)} %concatenate.32.wemb_ref, f32[32,1152]{1,0:T(8,128)} %get-tuple-element.36.ua_ref, f32[32,1152]{1,0:T(8,128)} %get-tuple-element.35.va_ref, ...), custom_call_target="tpu_custom_call" | custom-call | flops 20000000000 | bytes 14008324 | tf_op jit(solution)/shard_map/pallas_call | solution.py:39
  152.9 3.5 %all-to-all-start.3 = ((bf16[4,72,640]{2,1,0:T(8,128)(2,1)}), bf16[4,72,640]{2,1,0:T(8,128)(2,1)S(1)}, u32[]{:S(2)}, u32[]{:S(2)}) async-start(bf16[4,72,640]{2,1,0:T(8,128)(2,1)} %shard_map.155), calls=%async_computation.3 | async-start | bytes 737280 | tf_op jit(solution)/shard_map/all_to_all | solution.py:446
  156.4 4.5 %shard_map.156 = (f32[4,72,1152]{2,1,0:T(8,128)}, bf16[640,1152]{1,0:T(8,128)(2,1)}) custom-call(s32[1]{0:T(128)} %bitcast.25.seq_ref, bf16[4,16,72]{2,1,0:T(8,128)(2,1)} %copy-done.5, bf16[16,1152]{1,0:T(8,128)(2,1)} %wemb_ref.1, f32[32,1152]{1,0:T(8,128)} %get-tuple-element.36.ua_ref, f32[32,1152]{1,0:T(8,128)} %get-tuple-element.35.va_ref, ...), custom_call_target="tpu_custom_call" | custom-call | flops 1000000000 | bytes 6948868 | tf_op jit(solution)/shard_map/pallas_call | solution.py:39
  160.9 2.6 %all-to-all-done.3.att_ref = bf16[4,72,640]{2,1,0:T(8,128)(2,1)S(1)} async-done(((bf16[4,72,640]{2,1,0:T(8,128)(2,1)}), bf16[4,72,640]{2,1,0:T(8,128)(2,1)S(1)}, u32[]{:S(2)}, u32[]{:S(2)}) %all-to-all-start.3) | async-done | bytes 368672 | tf_op jit(solution)/shard_map/all_to_all | solution.py:446
  163.6 0.7 copy-done.1
  164.3 3.5 %shard_map.157 = bf16[4,72,1152]{2,1,0:T(8,128)(2,1)} custom-call(bf16[4,72,640]{2,1,0:T(8,128)(2,1)} %copy-done.1, f32[4,72,1152]{2,1,0:T(8,128)} %get-tuple-element.18.emb_ref, f32[6,1152]{1,0:T(8,128)} %get-tuple-element.39.mod_ref, bf16[640,1152]{1,0:T(8,128)(2,1)} %get-tuple-element.19.w_ref), custom_call_target="tpu_custom_call" | custom-call | flops 1000000000 | bytes 3197952 | tf_op jit(solution)/shard_map/pallas_call | solution.py:39
  (39 shorter events, 0.6 us)
Async XLA Ops:
  7.2 5.5 %copy-start.7 = (bf16[36,1152]{1,0:T(8,128)(2,1)S(1)}, bf16[36,1152]{1,0:T(8,128)(2,1)}, u32[]{:S(2)}) copy-start(bf16[36,1152]{1,0:T(8,128)(2,1)} %param.25) | copy-start | bytes 248836
  7.2 5.5 %copy-start.4 = (bf16[72,1728]{1,0:T(8,128)(2,1)S(1)}, bf16[72,1728]{1,0:T(8,128)(2,1)}, u32[]{:S(2)}) copy-start(bf16[72,1728]{1,0:T(8,128)(2,1)} %param.24) | copy-start | bytes 746500
  7.2 109.5 %all-gather.2.cloned.1.call-start = ((), (), s32[]{:S(2)}) async-start(), calls=%async_computation.4 | async-start | bytes 6266880 | tf_op jit(solution)/shard_map/all_gather | solution.py:334
  14.4 9.3 %copy-start.10 = (s32[16]{0:T(128)S(1)}, s32[16]{0:T(128)}, u32[]{:S(2)}) copy-start(s32[16]{0:T(128)} %param.18) | copy-start | bytes 196
  14.4 13.8 %copy-start.2 = (bf16[16,1152]{1,0:T(8,128)(2,1)S(1)}, bf16[16,1152]{1,0:T(8,128)(2,1)}, u32[]{:S(2)}) copy-start(bf16[16,1152]{1,0:T(8,128)(2,1)} %wemb_ref.1) | copy-start | bytes 110596
  14.5 17.1 %copy-start.9 = (f32[65]{0:T(128)S(1)}, f32[65]{0:T(128)}, u32[]{:S(2)}) copy-start(f32[65]{0:T(128)} %param.19) | copy-start | bytes 784
  14.5 34.1 %all-to-all-start = ((bf16[16,72,720]{2,1,0:T(8,128)(2,1)}), bf16[16,72,720]{2,1,0:T(8,128)(2,1)S(1)}, u32[]{:S(2)}, u32[]{:S(2)}) async-start(bf16[16,72,720]{2,1,0:T(8,128)(2,1)} %shard_map.149), calls=%async_computation | async-start | bytes 3538944 | tf_op jit(solution)/shard_map/all_to_all | solution.py:336
  48.5 1.2 copy-start
  54.3 18.6 %collective-permute-start = (bf16[640,576]{0,1:T(8,128)(2,1)S(1)}, bf16[640,576]{0,1:T(8,128)(2,1)S(1)}, u32[]{:S(2)}, u32[]{:S(2)}) collective-permute-start(bf16[640,576]{0,1:T(8,128)(2,1)S(1)} %copy.31), channel_id=1, source_target_pairs={{0,1},{1,0},{2,3},{3,2},{4,5},{5,4},{6,7},{7,6},{8,9},{9,8},{10,11... | collective-permute-start | bytes 2211848 | tf_op jit(solution)/shard_map/ppermute | solution.py:352
  62.6 25.3 %all-to-all-start.1 = ((bf16[16,72,160]{2,1,0:T(8,128)(2,1)}), bf16[16,72,160]{2,1,0:T(8,128)(2,1)S(1)}, u32[]{:S(2)}, u32[]{:S(2)}) async-start(bf16[16,72,160]{2,1,0:T(8,128)(2,1)} %shard_map.150), calls=%async_computation.1 | async-start | bytes 1179648 | tf_op jit(solution)/shard_map/all_to_all | solution.py:353
  87.9 0.8 copy-start.3
  93.1 9.3 %collective-permute-start.1 = (bf16[4,16,72]{2,1,0:T(8,128)(2,1)}, bf16[4,16,72]{2,1,0:T(8,128)(2,1)S(1)}, u32[]{:S(2)}, u32[]{:S(2)}) collective-permute-start(bf16[4,16,72]{2,1,0:T(8,128)(2,1)} %shard_map.152), channel_id=1, source_target_pairs={{32,0},{64,32},{96,64},{128,96},{160,128},{192,160},{224,192},{256... | collective-permute-start | bytes 27656 | tf_op jit(solution)/shard_map/ppermute | solution.py:382
  95.9 6.5 %copy-start.8 = (bf16[4,72,16]{1,2,0:T(8,128)(2,1)S(1)}, bf16[4,72,16]{1,2,0:T(8,128)(2,1)}, u32[]{:S(2)}) copy-start(bf16[4,72,16]{1,2,0:T(8,128)(2,1)} %param.17) | copy-start | bytes 27652
  102.4 30.5 %copy-start.5 = (bf16[4,16,72]{2,1,0:T(8,128)(2,1)}, bf16[4,16,72]{2,1,0:T(8,128)(2,1)S(1)}, u32[]{:S(2)}) copy-start(bf16[4,16,72]{2,1,0:T(8,128)(2,1)S(1)} %bitcast_select_fusion.lat_ref) | copy-start | bytes 27652
  103.1 30.6 %all-to-all-start.2 = ((bf16[32,16,72]{2,1,0:T(8,128)(2,1)}), bf16[32,16,72]{2,1,0:T(8,128)(2,1)S(1)}, u32[]{:S(2)}, u32[]{:S(2)}) async-start(bf16[32,16,72]{2,1,0:T(8,128)(2,1)} %bitcast.13), calls=%async_computation.2 | async-start | bytes 262144 | tf_op jit(solution)/shard_map/all_to_all | solution.py:385
  133.7 0.6 copy-start.6
  152.9 10.6 %all-to-all-start.3 = ((bf16[4,72,640]{2,1,0:T(8,128)(2,1)}), bf16[4,72,640]{2,1,0:T(8,128)(2,1)S(1)}, u32[]{:S(2)}, u32[]{:S(2)}) async-start(bf16[4,72,640]{2,1,0:T(8,128)(2,1)} %shard_map.155), calls=%async_computation.3 | async-start | bytes 737280 | tf_op jit(solution)/shard_map/all_to_all | solution.py:446
  163.6 0.7 copy-start.1
Sparse Core Ops, SparseCore 0:
  14.5 90.6 all-gather.1

commit v3 on v2

v3 whole, which is shorter than its diff:
```python
import math

import jax
import jax.numpy as jnp
import numpy as np
from jax import lax
from jax.experimental import pallas as pl
from jax.experimental.pallas import tpu as pltpu
from jax.sharding import PartitionSpec as P

HEADS = 8
HDIM = 72
HALF = HDIM // 2
SLOT = 80
PADDED = HEADS * SLOT
SCORE_SCALE = 1.0 / math.sqrt(HDIM)
LOG2E = math.log2(math.e)
F32 = jnp.float32
BF16 = jnp.bfloat16
MIB = 1024 * 1024


def mm(a, b):
    return jnp.dot(a, b, preferred_element_type=F32)


def mm_nt(a, b):
    return lax.dot_general(a, b, (((1,), (1,)), ((), ())), preferred_element_type=F32)


def call(kernel, out_shape, args, scratch=(), smem=(), hbm=(), hbm_out=(), flops=0, vmem=24, grid=None, in_specs=None, out_specs=None):
    moved = sum(a.size * a.dtype.itemsize for a in args)
    if in_specs is None:
        in_specs = [
            pl.BlockSpec(memory_space=pltpu.SMEM if i in smem else pl.ANY if i in hbm else pltpu.VMEM)
            for i in range(len(args))
        ]
        if isinstance(out_shape, tuple):
            out_specs = tuple(
                pl.BlockSpec(memory_space=pl.ANY if i in hbm_out else pltpu.VMEM) for i in range(len(out_shape))
            )
        else:
            out_specs = pl.BlockSpec(memory_space=pltpu.VMEM)
    return pl.pallas_call(
        kernel,
        out_shape=out_shape,
        in_specs=in_specs,
        out_specs=out_specs,
        scratch_shapes=list(scratch),
        compiler_params=pltpu.CompilerParams(vmem_limit_bytes=vmem * MIB),
        cost_estimate=pl.CostEstimate(flops=flops, bytes_accessed=moved, transcendentals=0),
        **({"grid": grid} if grid else {}),
    )(*args)


def layer_norm(values):
    center = values - jnp.mean(values, axis=-1, keepdims=True)
    spread = jnp.mean(center * center, axis=-1, keepdims=True)
    return center * lax.rsqrt(spread + 1e-06)


def pack_kernel(core_ref, x_ref, w_ref, o_ref):
    width = x_ref.shape[-1] // o_ref.shape[0]
    shard = w_ref[...].astype(F32)
    half = shard.shape[-1] // 2
    shard = jnp.where(core_ref[0] == 0, shard[:, :half], shard[:, half:])
    weight = jnp.concatenate([shard[:, : half // 2], shard[:, half // 2 :]], axis=0).astype(BF16)
    for part in range(o_ref.shape[0]):
        o_ref[part, :, :width] = x_ref[0, :, part * width : (part + 1) * width]
        o_ref[part, :, width:] = weight


def gather_kernel(w_ref, sout_ref, o_ref):
    rows = o_ref.shape[0]
    blank = jnp.zeros((rows, SLOT - HDIM), BF16)
    for i, part in enumerate((1, 2, 0)):
        pieces = []
        for h in range(HEADS):
            at = HDIM * (3 * h + part)
            pieces += [w_ref[:, at : at + HDIM], blank]
        o_ref[:, PADDED * i : PADDED * (i + 1)] = jnp.concatenate(pieces, axis=-1)
    sout = sout_ref[...].astype(F32)
    half = sout.shape[-1] // 2
    sout = jnp.concatenate([sout[:, :half], sout[:, half:]], axis=0)
    sout = jnp.concatenate([sout, jnp.zeros((rows, PADDED - half), F32)], axis=-1)
    o_ref[:, 3 * PADDED :] = sout.astype(BF16)


def temporal_columns():
    pick = np.zeros((6 * HDIM, 768), np.float32)
    for head in range(2):
        base = 3 * HDIM * head
        for i in range(HDIM):
            pick[base + i, 256 * head + i] = 1.0
            pick[base + HDIM + i, 256 * head + 128 + i] = 1.0
            pick[base + 2 * HDIM + i, 512 + SLOT * head + i] = 1.0
    return pick


def weight_rows():
    pick = np.zeros((2 * SLOT, 256), np.float32)
    for shard in range(2):
        for i in range(HALF):
            pick[HALF * shard + i, HDIM * shard + i] = 1.0
            pick[SLOT + HALF * shard + i, HDIM * shard + HALF + i] = 1.0
    return pick


def temporal_kernel(x_ref, pick_ref, o_ref, parts, total):
    frames, tokens, _ = x_ref.shape
    flat = x_ref[:, :, : 6 * HDIM].astype(F32).reshape(frames * tokens, 6 * HDIM).astype(BF16)
    parts[...] = mm(flat, pick_ref[...]).reshape(frames, tokens, -1)
    rows = frames * 8
    first = lax.broadcasted_iota(jnp.int32, (1, 2 * SLOT), 1) < SLOT
    same = (
        lax.broadcasted_iota(jnp.int32, (rows, rows), 0) % 8
        == lax.broadcasted_iota(jnp.int32, (rows, rows), 1) % 8
    )
    for block in range(tokens // 8):
        piece = parts[:, 8 * block : 8 * block + 8, :].reshape(rows, -1).astype(BF16)
        v = piece[:, 512 : 512 + 2 * SLOT]
        out = None
        for head in range(2):
            q = piece[:, 256 * head : 256 * head + 128]
            k = piece[:, 256 * head + 128 : 256 * head + 256]
            scores = jnp.where(same, mm_nt(q, k) * SCORE_SCALE, -jnp.inf)
            top = jnp.max(scores, axis=-1, keepdims=True)
            raised = jnp.exp(scores - top)
            weights = (raised / jnp.sum(raised, axis=-1, keepdims=True)).astype(BF16)
            found = mm(weights, v)
            out = found if out is None else jnp.where(first, out, found)
        total[:, 8 * block : 8 * block + 8, :] = out.reshape(frames, 8, 2 * SLOT)
    o_ref[...] = total[...].astype(BF16)


def unstack_kernel(x_ref, rows_ref, w_ref):
    shards, rows, width = x_ref.shape
    start = 6 * HDIM
    blank = jnp.zeros((SLOT, w_ref.shape[-1] - 2 * (width - start)), F32)
    for h in range(shards // 2):
        pair = x_ref[2 * h : 2 * h + 2, :, start:].astype(F32).reshape(2 * rows, -1).astype(BF16)
        both = mm(rows_ref[:, : 2 * rows], pair)
        w_ref[SLOT * h : SLOT * (h + 1), :] = jnp.concatenate(
            [both[:SLOT], both[SLOT:], blank], axis=-1
        ).astype(BF16)


def step_kernel(coef_ref, core_ref, att_ref, hid_ref, lat_ref, mine_ref, other_ref, wf_ref, mod_ref, o_ref):
    videos, tokens, width = hid_ref.shape
    rows = videos * tokens
    pairs = att_ref.shape[0] // videos
    att = att_ref[...].astype(F32).reshape(videos, pairs, tokens, 2 * SLOT)
    own = far = None
    for p in range(pairs):
        part = att[:, p].reshape(rows, 2 * SLOT).astype(BF16)
        at = slice(2 * SLOT * p, 2 * SLOT * (p + 1))
        own_term, far_term = mm(part, mine_ref[at, :]), mm(part, other_ref[at, :])
        own = own_term if own is None else own + own_term
        far = far_term if far is None else far + far_term
    low = core_ref[0] == 0
    half = width // 2
    proj = jnp.concatenate([jnp.where(low, own, far)[:, :half], jnp.where(low, far, own)[:, :half]], axis=-1)
    residual = hid_ref[...].astype(F32).reshape(rows, width) + mod_ref[0:1, :] * proj
    final_in = (layer_norm(residual) * (1.0 + mod_ref[2:3, :]) + mod_ref[1:2, :]).astype(BF16)
    predicted = mm_nt(wf_ref[...], final_in)
    for v in range(videos):
        pred = predicted[:, tokens * v : tokens * (v + 1)]
        clean = (lat_ref[v].astype(F32) - coef_ref[0] * pred) * coef_ref[1]
        o_ref[v] = (coef_ref[2] * clean + coef_ref[3] * pred).astype(BF16)


def place_kernel(mod_ref, wemb_ref, ua_ref, va_ref, cb_ref, sb_ref, o_ref, sums_ref):
    tokens, width = cb_ref.shape
    members = o_ref.shape[0] // tokens
    gain = 1.0 + mod_ref[4:5, :]
    made = []
    for i in range(members):
        c = pl.program_id(0) * members + i
        place = ua_ref[pl.ds(c, 1), :] * cb_ref[...] + va_ref[pl.ds(c, 1), :] * sb_ref[...]
        center = place - jnp.mean(place, axis=-1, keepdims=True)
        made.append(center * gain)
        high = center.astype(BF16)
        low = (center - high.astype(F32)).astype(BF16)
        cross = (mm_nt(high, wemb_ref[...]) + mm_nt(low, wemb_ref[...])) * (2.0 / width)
        square = jnp.mean(center * center, axis=-1, keepdims=True)
        blank = jnp.zeros((tokens, 7), F32)
        sums_ref[i] = jnp.concatenate([cross, square, blank], axis=-1).T
    o_ref[...] = jnp.concatenate(made, axis=0).astype(BF16)


def prepare_kernel(group_ref, few_ref, p_ref, w_ref, few_out, q_out, kv_out, p, w, made, p_sem, w_sem, out_sem):
    rows = q_out.shape[0]
    steps = made.shape[0] // 2
    step = made.shape[1]

    def load_w(part):
        at = slice(PADDED * part, PADDED * (part + 1))
        return pltpu.make_async_copy(w_ref.at[:, at], w.at[:, at], w_sem.at[part])

    def load_p(part):
        at = slice(step * part, step * (part + 1))
        return pltpu.make_async_copy(p_ref.at[at, :], p.at[at, :], p_sem.at[part])

    def store(part, i):
        at = kv_out.at[step * i : step * (i + 1), PADDED * part : PADDED * (part + 1)]
        slot = steps * part + i
        return pltpu.make_async_copy(made.at[slot], at, out_sem.at[slot])

    load_w(0).start()
    for i in range(steps):
        load_p(i).start()
    load_w(1).start()
    load_w(2).start()
    for part in range(2):
        load_w(part).wait()
        for i in range(steps):
            if part == 0:
                load_p(i).wait()
            here = slice(step * i, step * (i + 1))
            made[steps * part + i] = mm(p[here, :], w[:, PADDED * part : PADDED * (part + 1)]).astype(BF16)
            store(part, i).start()
    load_w(2).wait()
    start = pl.multiple_of(group_ref[0] * rows, rows)
    q_out[...] = mm(p[pl.ds(start, rows), :], w[:, 2 * PADDED :])
    few_out[...] = mm(few_ref[...], w[...])
    for part in range(2):
        for i in range(steps):
            store(part, i).wait()


def spatial_kernel(
    group_ref, lat_ref, gram_ref, sums_ref, few_ref, pq_ref, pkv_ref,
    o_ref, held, columns, keys, vals, sem,
):
    chunks, patch, tokens = lat_ref.shape
    members = o_ref.shape[0]
    block = members * tokens
    blocks = chunks // members

    def fetch(index):
        start = pl.multiple_of(index * block, block)
        return pltpu.make_async_copy(pkv_ref.at[pl.ds(start, block), :], held.at[index], sem.at[index])

    for i in range(blocks):
        fetch(i).start()

    gram = gram_ref[...]
    for c in range(chunks):
        once = lat_ref[c].astype(F32)
        twice = jnp.concatenate([once, once], axis=0)
        sums = sums_ref[c]
        mixed = mm(gram, twice.astype(BF16)) + sums[:patch]
        variance = jnp.sum(mixed * once, axis=0, keepdims=True) + sums[patch : patch + 1]
        scale = lax.rsqrt(jnp.maximum(variance, 0.0) + 1e-06)
        rows = jnp.concatenate([twice, jnp.broadcast_to(scale, (8, tokens))], axis=0)
        columns[tokens * c : tokens * (c + 1), :] = rows.T

    lane = lax.broadcasted_iota(jnp.int32, (1, 2 * PADDED), 1)
    ones = jnp.where((lane >= PADDED) & (lane % SLOT == HDIM), 1.0, 0.0)
    few = few_ref[...]
    mix = few[:patch] + few[patch : 2 * patch]
    offset = few[2 * patch : 2 * patch + 1] + few[2 * patch + 8 : 2 * patch + 9]
    high = mix.astype(BF16).astype(F32)
    mix = jnp.concatenate([high, mix - high], axis=0).astype(BF16)
    kv_mix, q_mix = mix[:, : 2 * PADDED], mix[:, 2 * PADDED :]
    kv_offset, q_offset = offset[:, : 2 * PADDED] + ones, offset[:, 2 * PADDED :]

    def one(index, carry):
        start = pl.multiple_of(index * block, block)
        column = columns[pl.ds(start, block), :]
        latent, scale = column[:, : 2 * patch].astype(BF16), column[:, 2 * patch : 2 * patch + 1]
        mixed = mm(latent, kv_mix)
        fetch(index).wait()
        kv = (mixed + held[index].astype(F32)) * scale + kv_offset
        keys[pl.ds(start, block), :] = kv[:, :PADDED].astype(BF16)
        vals[pl.ds(start, block), :] = kv[:, PADDED:].astype(BF16)
        return carry

    lax.fori_loop(0, blocks, one, 0)

    column = columns[pl.ds(pl.multiple_of(group_ref[0] * block, block), block), :]
    latent, scale = column[:, : 2 * patch].astype(BF16), column[:, 2 * patch : 2 * patch + 1]
    q_all = (mm(latent, q_mix) + pq_ref[...]) * scale + q_offset
    q_all = q_all.astype(BF16).astype(F32)
    lane = lane[:, :PADDED]
    merged = [None] * (PADDED // 128)

    def window(h):
        first = SLOT * h // 128
        last = (SLOT * h + HDIM) // 128
        here = slice(128 * first, 128 * (last + 1))
        inside = (lane >= SLOT * h) & (lane < SLOT * h + HDIM)
        return first, last, here, inside[:, here]

    def score(h):
        _, _, here, inside = window(h)
        return mm_nt(jnp.where(inside, q_all[:, here], 0.0).astype(BF16), keys[:, here])

    def weigh(scores):
        top = jnp.max(scores, axis=-1, keepdims=True)
        return jnp.exp2((scores - top) * (SCORE_SCALE * LOG2E)).astype(BF16)

    def blend(h, raised):
        first, last, here, inside = window(h)
        found = mm(raised, vals[:, here])
        at = SLOT * h + HDIM - 128 * first
        found = jnp.where(inside, found * (1.0 / found[:, at : at + 1]), 0.0)
        for tile in range(first, last + 1):
            piece = found[:, 128 * (tile - first) : 128 * (tile - first + 1)]
            merged[tile] = piece if merged[tile] is None else merged[tile] + piece

    scores = score(0)
    raised = None
    for h in range(HEADS):
        following = score(h + 1) if h + 1 < HEADS else None
        if raised is not None:
            blend(h - 1, raised)
        raised = weigh(scores)
        scores = following
    blend(HEADS - 1, raised)
    o_ref[...] = jnp.concatenate(merged, axis=-1).reshape(members, tokens, PADDED).astype(BF16)


def projection_kernel(rows_ref, w_ref, w_out, raw, sem):
    copy = pltpu.make_async_copy(w_ref.at[:, 3 * PADDED :], raw, sem)
    copy.start()
    copy.wait()
    half = w_out.shape[-1] // 2
    for h in range(HEADS):
        both = mm(rows_ref[:, : 2 * HDIM], raw[2 * HDIM * h : 2 * HDIM * (h + 1), :])
        w_out[SLOT * h : SLOT * (h + 1), :] = jnp.concatenate(
            [both[:SLOT, :half], both[SLOT:, :half]], axis=-1
        ).astype(BF16)


def finish_kernel(
    seq_ref, att_ref, lat_ref, wemb_ref, ua_ref, va_ref, cb_ref, sb_ref, mod_ref, w_ref, o_ref
):
    videos, tokens, width = o_ref.shape
    s = seq_ref[0]
    place = ua_ref[pl.ds(s, 1), :] * cb_ref[...] + va_ref[pl.ds(s, 1), :] * sb_ref[...]
    gate = mod_ref[5:6, :]
    att = att_ref[...].astype(F32).reshape(videos * tokens, PADDED).astype(BF16)
    embedded = [mm(lat_ref[v].astype(F32).T.astype(BF16), wemb_ref[...]) + place for v in range(videos)]
    gated = mm(att, w_ref[...]) * gate
    for v in range(videos):
        o_ref[v] = (embedded[v] + gated[tokens * v : tokens * (v + 1), :]).astype(BF16)


def position_factors(chunks, tokens, width):
    half = width // 2
    frequency = jnp.exp(jnp.arange(half, dtype=F32) * (-math.log(10000.0) / half))
    start = (jnp.arange(chunks, dtype=F32) * tokens)[:, None] * frequency[None, :]
    inner = jnp.arange(tokens, dtype=F32)[:, None] * frequency[None, :]
    sin_a, cos_a, sin_b, cos_b = jnp.sin(start), jnp.cos(start), jnp.sin(inner), jnp.cos(inner)
    ua = jnp.concatenate([sin_a, cos_a], axis=-1)
    va = jnp.concatenate([cos_a, -sin_a], axis=-1)
    cb = jnp.concatenate([cos_b, cos_b], axis=-1)
    sb = jnp.concatenate([sin_b, sin_b], axis=-1)
    return ua, va, cb, sb


def rounding_rest(values):
    return values - lax.reduce_precision(values, 8, 7)


def shards(
    t_qkv, hidden, latents, fresh, levels, alpha_bar, modulation, w_tout, w_final, w_embed, w_sqkv, w_sout,
):
    frames = lax.axis_size("queue")
    seqs = lax.axis_size("seq")
    queue_pos = lax.axis_index("queue")
    seq_pos = lax.axis_index("seq")
    videos, _, tokens, width = hidden.shape
    top_level = alpha_bar.shape[0] - 1
    pairs = frames // videos

    core = seq_pos % 2
    half = width // 2
    width_part = t_qkv.shape[-1] // pairs
    sent = width_part + half // 2
    packed = call(
        pack_kernel,
        jax.ShapeDtypeStruct((frames, tokens, sent), BF16),
        (core.reshape(1), t_qkv.reshape(videos, tokens, -1), w_tout),
        grid=(videos,),
        in_specs=[
            pl.BlockSpec(memory_space=pltpu.SMEM),
            pl.BlockSpec((1, tokens, t_qkv.shape[-1]), lambda v: (v, 0, 0)),
            pl.BlockSpec(w_tout.shape, lambda v: (0, 0)),
        ],
        out_specs=pl.BlockSpec((pairs, tokens, sent), lambda v: (v, 0, 0)),
    )
    w_sqkv, w_sout, packed = lax.optimization_barrier((w_sqkv, w_sout, packed))
    w_shard = call(
        gather_kernel,
        jax.ShapeDtypeStruct((w_sqkv.shape[0], 4 * PADDED), BF16),
        (w_sqkv, w_sout),
    )
    w_spatial = lax.all_gather(w_shard, "queue", axis=0, tiled=True)

    arrived = lax.all_to_all(packed, "queue", split_axis=0, concat_axis=0, tiled=True)
    row_pick = jnp.asarray(weight_rows(), BF16)

    level = lax.dynamic_index_in_dim(levels, queue_pos, 0, keepdims=False)
    following = lax.dynamic_index_in_dim(
        jnp.concatenate([levels[1:], jnp.full((1,), top_level + 1, levels.dtype)]), queue_pos, 0, keepdims=False
    )
    mods = lax.dynamic_index_in_dim(modulation, level, 0, keepdims=False).astype(F32)
    new_mods = lax.dynamic_index_in_dim(modulation, following - 1, 0, keepdims=False).astype(F32)
    a = lax.dynamic_index_in_dim(alpha_bar, level, 0, keepdims=False)
    b = lax.dynamic_index_in_dim(alpha_bar, level - 1, 0, keepdims=False)
    coef = jnp.stack([jnp.sqrt(1.0 - a), 1.0 / jnp.sqrt(a), jnp.sqrt(b), jnp.sqrt(1.0 - b)])

    ua, va, cb, sb = position_factors(seqs, tokens, width)
    rows = seqs * tokens
    own_rows = videos * tokens
    placed, sums = call(
        place_kernel,
        (
            jax.ShapeDtypeStruct((rows, width), BF16),
            jax.ShapeDtypeStruct((seqs, 24, tokens), F32),
        ),
        (new_mods, w_embed, ua, va, cb, sb),
        grid=(rows // own_rows,),
        in_specs=[pl.BlockSpec(a.shape, lambda i: (0, 0)) for a in (new_mods, w_embed, ua, va, cb, sb)],
        out_specs=(
            pl.BlockSpec((own_rows, width), lambda i: (i, 0)),
            pl.BlockSpec((videos, 24, tokens), lambda i: (i, 0, 0)),
        ),
        flops=100_000_000,
    )
    gain, shift = 1.0 + new_mods[4:5], new_mods[3:4]
    emb_f32 = w_embed.astype(F32)
    centered = emb_f32 - jnp.mean(emb_f32, axis=-1, keepdims=True)
    gram = jnp.dot(centered, centered.T, precision=lax.Precision.HIGHEST) * (1.0 / width)
    gram = jnp.concatenate([gram, rounding_rest(gram)], axis=-1).astype(BF16)
    centered = centered * gain
    eight = jnp.zeros((7, width), F32)
    few = [centered, rounding_rest(centered), shift, eight, rounding_rest(shift), eight]
    few = jnp.concatenate(few, axis=0).astype(BF16)
    latents_t = latents.reshape(videos, tokens, -1).transpose(0, 2, 1)
    fresh_t = fresh.transpose(0, 2, 1)
    w_final_t = w_final.T
    early = (arrived, placed, sums, few, gram, mods, new_mods, coef, latents_t, fresh_t, w_final_t)
    early = lax.optimization_barrier(early)
    arrived, placed, sums, few, gram, mods, new_mods, coef, latents_t, fresh_t, w_final_t = early

    attended = call(
        temporal_kernel,
        jax.ShapeDtypeStruct((frames, tokens, 2 * SLOT), BF16),
        (arrived, jnp.asarray(temporal_columns(), BF16)),
        scratch=[pltpu.VMEM((frames, tokens, 768), F32), pltpu.VMEM((frames, tokens, 2 * SLOT), F32)],
        flops=4_000_000_000,
    )
    stacked, attended = lax.optimization_barrier((arrived, attended))
    w_mine = call(
        unstack_kernel,
        jax.ShapeDtypeStruct((PADDED, PADDED), BF16),
        (stacked, row_pick),
        flops=20_000_000_000,
    )
    w_other = lax.ppermute(w_mine, "seq", [(i, i ^ 1) for i in range(seqs)])
    returned = lax.all_to_all(attended, "queue", split_axis=0, concat_axis=0, tiled=True)

    stepped = call(
        step_kernel,
        jax.ShapeDtypeStruct((videos, latents.shape[-1], tokens), BF16),
        (
            coef,
            core.reshape(1),
            returned,
            hidden.reshape(videos, tokens, width),
            latents_t,
            w_mine,
            w_other,
            w_final_t,
            mods,
        ),
        smem=(0, 1),
        flops=1_000_000_000,
    )
    arriving = lax.ppermute(stepped, "queue", [(f, f - 1) for f in range(1, frames)])
    queued = jnp.where(queue_pos == frames - 1, fresh_t, arriving)

    everyone = lax.all_to_all(
        jnp.tile(queued, (seqs // videos, 1, 1)), "seq", split_axis=0, concat_axis=0, tiled=True
    )
    groups = [[videos * g + i for i in range(videos)] for g in range(seqs // videos)]
    group = (seq_pos // videos).reshape(1)
    few_out, pq, pkv = call(
        prepare_kernel,
        (
            jax.ShapeDtypeStruct((few.shape[0], 3 * PADDED), F32),
            jax.ShapeDtypeStruct((own_rows, PADDED), F32),
            jax.ShapeDtypeStruct((rows, 2 * PADDED), BF16),
        ),
        (group, few, placed, w_spatial),
        scratch=[
            pltpu.VMEM((rows, width), BF16),
            pltpu.VMEM((width, 3 * PADDED), BF16),
            pltpu.VMEM((8, rows // 4, PADDED), BF16),
            pltpu.SemaphoreType.DMA((4,)),
            pltpu.SemaphoreType.DMA((3,)),
            pltpu.SemaphoreType.DMA((8,)),
        ],
        smem=(0,),
        hbm=(2, 3),
        hbm_out=(2,),
        flops=8_000_000_000,
        vmem=56,
    )
    spatial = call(
        spatial_kernel,
        jax.ShapeDtypeStruct((videos, tokens, PADDED), BF16),
        (group, everyone, gram, sums, few_out, pq, pkv),
        scratch=[
            pltpu.VMEM((rows // own_rows, own_rows, 2 * PADDED), BF16),
            pltpu.VMEM((rows, 2 * latents.shape[-1] + 8), F32),
            pltpu.VMEM((rows, PADDED), BF16),
            pltpu.VMEM((rows, PADDED), BF16),
            pltpu.SemaphoreType.DMA((rows // own_rows,)),
        ],
        smem=(0,),
        hbm=(6,),
        flops=20_000_000_000,
        vmem=56,
    )
    heads_out = lax.all_to_all(
        spatial, "seq", split_axis=0, concat_axis=0, tiled=True, axis_index_groups=groups
    )
    late, _ = lax.optimization_barrier((w_spatial, spatial))
    w_s = call(
        projection_kernel,
        jax.ShapeDtypeStruct((PADDED, width), BF16),
        (row_pick, late),
        scratch=[pltpu.VMEM((width, PADDED), BF16), pltpu.SemaphoreType.DMA],
        hbm=(1,),
        flops=20_000_000_000,
        vmem=56,
    )
    block_out = call(
        finish_kernel,
        jax.ShapeDtypeStruct((videos, tokens, width), BF16),
        (seq_pos.reshape(1), heads_out, queued, w_embed, ua, va, cb, sb, new_mods, w_s),
        smem=(0,),
        flops=1_000_000_000,
    )
    return (
        queued.transpose(0, 2, 1).reshape(videos, 1, tokens, -1),
        block_out.reshape(videos, 1, tokens, width),
    )


def solution(mesh):
    in_specs = (
        P(None, "queue", "seq", None),
        P(None, "queue", "seq", None),
        P(None, "queue", "seq", None),
        P(None, "seq", None),
        P(),
        P(),
        P(),
        P("queue", None),
        P(),
        P(),
        P("queue", None),
        P("queue", None),
    )
    out_specs = (P(None, "queue", "seq", None), P(None, "queue", "seq", None))
    return jax.shard_map(shards, mesh=mesh, in_specs=in_specs, out_specs=out_specs, check_vma=False)
```

time: 178 us -> 156 us (0.88); the launches traced: 175 us -> 155 us
  blocking collectives: 0 us -> 18.9 us
  waiting for transfers between devices: 25.3 us -> 9.42 us
  Pallas kernels: 66.7 us -> 55.1 us
  starting transfers between devices: 39.6 us -> 32 us
  other arithmetic: 6.58 us -> 2.41 us
    all_to_all x0 -> x1, blocking collectives: none -> 18.9 us  [shards(): lax.all_to_all(attended, 'queue', split_axis=0, concat_axis=0, tiled=True)]
    all_to_all x1 -> x0, waiting for transfers between devices: 13.8 us -> none  [shards(): lax.all_to_all(attended, 'queue', split_axis=0, concat_axis=0, tiled=True)]
    pallas_call x9 -> x10, Pallas kernels: 66.7 us -> 55.1 us  [call(): pl.pallas_call(kernel, out_shape=out_shape, in_specs=in_specs, out_specs=...]
    all_to_all x1 -> x0, starting transfers between devices: 8.62 us -> none  [shards(): lax.all_to_all(attended, 'queue', split_axis=0, concat_axis=0, tiled=True)]
    all_to_all x1, waiting for transfers between devices: 7.95 us -> 0.01 us  [shards(): lax.all_to_all(packed, 'queue', split_axis=0, concat_axis=0, tiled=True)]
    unnamed x22 -> x36, local copies, waits for them, and re-layouts: 3.46 us -> 9.05 us
    ppermute x1, waiting for transfers between devices: 0.01 us -> 5.26 us  [shards(): lax.ppermute(stepped, 'queue', [(f, f - 1) for f in range(1, frames)])]
  transfers between devices with their start and end apart: 7 -> 6, of which waited for: 4 -> 3; matrix products, arithmetic and copies ran while one was open for 8% -> 6% of each run, Pallas kernels for 23% -> 24%
where the time goes in v3:
time: 156 us; the launch traced here: 155 us
  Pallas kernels  55.1 us (35%)
  starting transfers between devices  32 us (21%)
  between operations  21.7 us (14%)
  blocking collectives  18.9 us (12%)
  local copies, waits for them, and re-layouts  15.1 us (10%)
  waiting for transfers between devices  9.42 us (6%)
  other arithmetic  2.41 us (2%)
    pallas_call x10, Pallas kernels, call(): pl.pallas_call(kernel, out_shape=out_shape, in_specs=in_specs, out_specs=...  55.1 us
    all_to_all x1, blocking collectives, shards(): lax.all_to_all(attended, 'queue', split_axis=0, concat_axis=0, tiled=True)  18.9 us
    all_to_all x1, starting transfers between devices, shards(): lax.all_to_all(jnp.tile(queued, (seqs // videos, 1, 1)), 'seq', split_axi...  14.7 us
    all_to_all x1, starting transfers between devices, shards(): lax.all_to_all(packed, 'queue', split_axis=0, concat_axis=0, tiled=True)  9.12 us
    unnamed x36, local copies, waits for them, and re-layouts  9.05 us
    ppermute x1, waiting for transfers between devices, shards(): lax.ppermute(stepped, 'queue', [(f, f - 1) for f in range(1, frames)])  5.26 us
    all_to_all x1, starting transfers between devices, shards(): lax.all_to_all(spatial, 'seq', split_axis=0, concat_axis=0, tiled=True, a...  3.47 us
  transfers between devices with their start and end apart: 6, of which 3 were waited for; matrix products, arithmetic and copies ran while one was open for 6% of the time, Pallas kernels for 24%

profile of v3, /device:TPU:24, one launch (start us, length us, event | category | flops | bytes accessed | tf_op | source)
XLA Modules:
  0.0 154.8 jit_solution(1038327633628861171)
XLA Ops:
  7.2 0.0 all-gather.2.cloned.1.call-start
  7.3 1.2 copy-done
  8.5 0.9 copy-done.4
  9.4 2.3 %shard_map.149 = bf16[16,72,720]{2,1,0:T(8,128)(2,1)} custom-call(s32[1]{0:T(128)} %bitcast.core_ref, bf16[4,72,1728]{2,1,0:T(8,128)(2,1)S(1)} %bitcast.35, bf16[36,1152]{1,0:T(8,128)(2,1)S(1)} %copy-done.4), custom_call_target="tpu_custom_call" | custom-call | bytes 1078276 | tf_op jit(solution)/shard_map/pallas_call | solution.py:44
  11.6 0.9 copy-done.2
  12.6 0.9 copy-done.3
  13.5 1.0 shard_map.154
  14.5 0.0 all-gather.2.cloned.1.call-update
  14.6 9.1 %all-to-all-start = ((bf16[16,72,720]{2,1,0:T(8,128)(2,1)}), bf16[16,72,720]{2,1,0:T(8,128)(2,1)S(1)}, u32[]{:S(2)}, u32[]{:S(2)}) async-start(bf16[16,72,720]{2,1,0:T(8,128)(2,1)} %shard_map.149), calls=%async_computation | async-start | bytes 3538944 | tf_op jit(solution)/shard_map/all_to_all | solution.py:402
  23.7 0.1 slice.13
  23.8 0.6 dynamic_slice.23
  27.6 0.6 fusion.14
  30.9 0.1 pad_add_fusion
  30.9 0.6 dynamic_slice.21
  32.9 0.1 convert_reduce_fusion
  33.0 1.0 constant_dynamic-slice_fusion
  34.1 0.1 fusion.4
  34.2 2.5 %concatenate.28.few_ref = bf16[48,1152]{1,0:T(8,128)(2,1)} concatenate(bf16[16,1152]{1,0:T(8,128)(2,1)S(1)} %get-tuple-element.53, bf16[16,1152]{1,0:T(8,128)(2,1)S(1)} %get-tuple-element.52, bf16[1,1152]{1,0:T(2,128)(2,1)S(1)} %fusion.11, bf16[7,1152]{1,0:T(8,128)(2,1)S(1)} %broadcast_in_dim.2, bf16[1,1152]{1,0:T(2,128)(2,1)S(1)} %fusion.9, bf16[7,1152]{1,0:T(8,128)(2,1)S(1)} %broadcast_in_dim.2), dimensions={0} | concatenate | bytes 221184 | tf_op jit(solution)/shard_map/concatenate | solution.py:441
  36.8 0.7 fusion
  37.4 0.4 fusion.6
  37.8 0.1 pad_maximum_fusion.3
  37.9 0.2 pad_maximum_fusion
  38.1 8.0 %shard_map.150 = (bf16[2304,1152]{1,0:T(8,128)(2,1)S(1)}, f32[32,24,72]{2,1,0:T(8,128)S(1)}) custom-call(f32[6,1152]{1,0:T(8,128)S(1)} %get-tuple-element.44.mod_ref, bf16[16,1152]{1,0:T(8,128)(2,1)S(1)} %copy-done.1, f32[32,1152]{1,0:T(8,128)S(1)} %get-tuple-element.51.ua_ref, f32[32,1152]{1,0:T(8,128)S(1)} %get-tuple-element.50.va_ref, ...), custom_call_target="tpu_custom_call" | custom-call | flops 100000000 | bytes 1022976 | tf_op jit(solution)/shard_map/pallas_call | solution.py:44
  46.0 2.3 %copy-done.6 = bf16[2304,1152]{1,0:T(8,128)(2,1)} copy-done((bf16[2304,1152]{1,0:T(8,128)(2,1)}, bf16[2304,1152]{1,0:T(8,128)(2,1)S(1)}, u32[]{:S(2)}) %copy-start.6) | copy-done | bytes 5308440
  48.3 0.7 copy-done.8
  49.1 0.1 pad_maximum_fusion.5.coef_ref
  49.2 0.3 fusion.13
  49.5 0.7 pad_maximum_fusion.4.gram_ref
  50.2 0.0 copy-start.12
  50.2 5.5 %shard_map.151 = bf16[16,72,160]{2,1,0:T(8,128)(2,1)S(1)} custom-call(bf16[16,72,720]{2,1,0:T(8,128)(2,1)S(1)} %all-to-all-done.x_ref, bf16[432,768]{1,0:T(8,128)(2,1)S(1)} %copy-done.11), custom_call_target="tpu_custom_call" | custom-call | flops 4000000000 | bytes 2322432 | tf_op jit(solution)/shard_map/pallas_call | solution.py:44
  55.7 0.7 shard_map.152.mine_ref
  56.4 1.9 %collective-permute-start = (bf16[640,640]{1,0:T(8,128)(2,1)S(1)}, bf16[640,640]{1,0:T(8,128)(2,1)S(1)}, u32[]{:S(2)}, u32[]{:S(2)}) collective-permute-start(bf16[640,640]{1,0:T(8,128)(2,1)S(1)} %shard_map.152.mine_ref), channel_id=1, source_target_pairs={{0,1},{1,0},{2,3},{3,2},{4,5},{5,4},{6,7},{7,6},{8,9},{9,8},{10,11... | collective-permute-start | bytes 2457608 | tf_op jit(solution)/shard_map/ppermute | solution.py:463
  58.3 18.9 %all_to_all.20.att_ref = bf16[16,72,160]{2,1,0:T(8,128)(2,1)S(1)} all-to-all(bf16[16,72,160]{2,1,0:T(8,128)(2,1)S(1)} %shard_map.151), channel_id=1, replica_groups=mesh['queue'=16,'seq'=32] {'queue'}, dimensions={0} | all-to-all | bytes 737280 | tf_op jit(solution)/shard_map/all_to_all | solution.py:464
  77.2 2.5 %shard_map.153 = bf16[4,16,72]{2,1,0:T(8,128)(2,1)S(1)} custom-call(f32[4]{0:T(128)S(1)} %pad_maximum_fusion.5.coef_ref, s32[1]{0:T(128)} %bitcast.core_ref, bf16[16,72,160]{2,1,0:T(8,128)(2,1)S(1)} %all_to_all.20.att_ref, bf16[4,72,1152]{2,1,0:T(8,128)(2,1)S(1)} %bitcast.37, bf16[4,16,72]{2,1,0:T(8,128)(2,1)S(1)} %bitcast.39, ...), custom_call_target="tpu_custom_call" | custom-call | flops 1000000000 | bytes 2744340 | tf_op jit(solution)/shard_map/pallas_call | solution.py:44
  79.8 2.8 %collective-permute-start.1 = (bf16[4,16,72]{2,1,0:T(8,128)(2,1)S(1)}, bf16[4,16,72]{2,1,0:T(8,128)(2,1)S(1)}, u32[]{:S(2)}, u32[]{:S(2)}) collective-permute-start(bf16[4,16,72]{2,1,0:T(8,128)(2,1)S(1)} %shard_map.153), channel_id=1, source_target_pairs={{32,0},{64,32},{96,64},{128,96},{160,128},{192,160},{224,192},{256... | collective-permute-start | bytes 27656 | tf_op jit(solution)/shard_map/ppermute | solution.py:483
  82.6 5.3 %collective-permute-done.1 = bf16[4,16,72]{2,1,0:T(8,128)(2,1)S(1)} collective-permute-done((bf16[4,16,72]{2,1,0:T(8,128)(2,1)S(1)}, bf16[4,16,72]{2,1,0:T(8,128)(2,1)S(1)}, u32[]{:S(2)}, u32[]{:S(2)}) %collective-permute-start.1) | collective-permute-done | bytes 9248 | tf_op jit(solution)/shard_map/ppermute | solution.py:483
  87.9 0.7 tile.4
  88.5 14.7 %all-to-all-start.2 = ((bf16[32,16,72]{2,1,0:T(8,128)(2,1)}), bf16[32,16,72]{2,1,0:T(8,128)(2,1)S(1)}, u32[]{:S(2)}, u32[]{:S(2)}) async-start(bf16[32,16,72]{2,1,0:T(8,128)(2,1)} %bitcast.18), calls=%async_computation.2 | async-start | bytes 262144 | tf_op jit(solution)/shard_map/all_to_all | solution.py:486
  103.2 0.0 all-gather.2.cloned.1.call-done.w_ref
  103.2 15.9 %shard_map.155 = (f32[48,1920]{1,0:T(8,128)}, f32[288,640]{1,0:T(8,128)}, bf16[2304,1280]{1,0:T(8,128)(2,1)}) custom-call(s32[1]{0:T(128)} %bitcast.17.group_ref, bf16[48,1152]{1,0:T(8,128)(2,1)} %concatenate.28.few_ref, bf16[2304,1152]{1,0:T(8,128)(2,1)} %copy-done.6, bf16[1152,2560]{1,0:T(8,128)(2,1)} %all-gather.2.cloned.1.call-done.w_ref), custom_call_target="tpu_custom_call" | custom-call | flops 8000000000 | bytes 11317252 | tf_op jit(solution)/shard_map/pallas_call | solution.py:44
  119.1 1.1 all-to-all-done.2.lat_ref
  120.2 0.6 copy-done.14
  120.9 13.1 %shard_map.156 = bf16[4,72,640]{2,1,0:T(8,128)(2,1)} custom-call(s32[1]{0:T(128)} %bitcast.17.group_ref, bf16[32,16,72]{2,1,0:T(8,128)(2,1)} %copy-done.14, bf16[16,32]{1,0:T(8,128)(2,1)} %pad_maximum_fusion.4.gram_ref, f32[32,24,72]{2,1,0:T(8,128)} %copy-done.8, f32[48,1920]{1,0:T(8,128)} %get-tuple-element.41.few_ref, ...), custom_call_target="tpu_custom_call" | custom-call | flops 20000000000 | bytes 7300100 | tf_op jit(solution)/shard_map/pallas_call | solution.py:44
  134.0 3.5 %all-to-all-start.3 = ((bf16[4,72,640]{2,1,0:T(8,128)(2,1)}), bf16[4,72,640]{2,1,0:T(8,128)(2,1)S(1)}, u32[]{:S(2)}, u32[]{:S(2)}) async-start(bf16[4,72,640]{2,1,0:T(8,128)(2,1)} %shard_map.156), calls=%async_computation.3 | async-start | bytes 737280 | tf_op jit(solution)/shard_map/all_to_all | solution.py:529
  137.5 4.1 %shard_map.157.w_ref = bf16[640,1152]{1,0:T(8,128)(2,1)} custom-call(bf16[160,256]{1,0:T(8,128)(2,1)} %constant.92.clone.rows_ref, bf16[1152,2560]{1,0:T(8,128)(2,1)} %all-gather.2.cloned.1.call-done.w_ref), custom_call_target="tpu_custom_call" | custom-call | flops 20000000000 | bytes 5980160 | tf_op jit(solution)/shard_map/pallas_call | solution.py:44
  141.6 3.0 %all-to-all-done.3.att_ref = bf16[4,72,640]{2,1,0:T(8,128)(2,1)S(1)} async-done(((bf16[4,72,640]{2,1,0:T(8,128)(2,1)}), bf16[4,72,640]{2,1,0:T(8,128)(2,1)S(1)}, u32[]{:S(2)}, u32[]{:S(2)}) %all-to-all-start.3) | async-done | bytes 368672 | tf_op jit(solution)/shard_map/all_to_all | solution.py:529
  144.7 1.4 copy-done.13
  146.0 1.9 %shard_map.158 = bf16[4,72,1152]{2,1,0:T(8,128)(2,1)} custom-call(s32[1]{0:T(128)} %bitcast.16.seq_ref, bf16[4,72,640]{2,1,0:T(8,128)(2,1)S(1)} %all-to-all-done.3.att_ref, bf16[4,16,72]{2,1,0:T(8,128)(2,1)S(1)} %broadcast_select_fusion.lat_ref, bf16[16,1152]{1,0:T(8,128)(2,1)S(1)} %copy-done.1, f32[32,1152]{1,0:T(8,128)S(1)} %get-tuple-element.51.ua_ref, ...), custom_call_target="tpu_custom_call" | custom-call | flops 1000000000 | bytes 2875396 | tf_op jit(solution)/shard_map/pallas_call | solution.py:44
  (39 shorter events, 0.2 us)
Async XLA Ops:
  7.2 16.5 %copy-start.17 = (s32[16]{0:T(128)S(1)}, s32[16]{0:T(128)}, u32[]{:S(2)}) copy-start(s32[16]{0:T(128)} %param.18) | copy-start | bytes 196
  7.2 20.4 %copy-start.16 = (f32[65]{0:T(128)S(1)}, f32[65]{0:T(128)}, u32[]{:S(2)}) copy-start(f32[65]{0:T(128)} %param.19) | copy-start | bytes 784
  7.2 96.0 %all-gather.2.cloned.1.call-start = ((), (), s32[]{:S(2)}) async-start(), calls=%async_computation.4 | async-start | bytes 6266880 | tf_op jit(solution)/shard_map/all_gather | solution.py:400
  7.2 1.2 copy-start
  8.5 0.9 copy-start.4
  9.4 23.6 %copy-start.1 = (bf16[16,1152]{1,0:T(8,128)(2,1)S(1)}, bf16[16,1152]{1,0:T(8,128)(2,1)}, u32[]{:S(2)}) copy-start(bf16[16,1152]{1,0:T(8,128)(2,1)} %wemb_ref.3) | copy-start | bytes 110596
  9.4 40.8 %copy-start.11 = (bf16[432,768]{1,0:T(8,128)(2,1)S(1)}, bf16[432,768]{1,0:T(8,128)(2,1)}, u32[]{:S(2)}) copy-start(bf16[432,768]{1,0:T(8,128)(2,1)} %constant.93.clone.pick_ref) | copy-start | bytes 1990660
  11.6 0.9 copy-start.2
  12.6 0.9 copy-start.3
  14.6 35.6 %all-to-all-start = ((bf16[16,72,720]{2,1,0:T(8,128)(2,1)}), bf16[16,72,720]{2,1,0:T(8,128)(2,1)S(1)}, u32[]{:S(2)}, u32[]{:S(2)}) async-start(bf16[16,72,720]{2,1,0:T(8,128)(2,1)} %shard_map.149), calls=%async_computation | async-start | bytes 3538944 | tf_op jit(solution)/shard_map/all_to_all | solution.py:402
  46.0 2.3 %copy-start.6 = (bf16[2304,1152]{1,0:T(8,128)(2,1)}, bf16[2304,1152]{1,0:T(8,128)(2,1)S(1)}, u32[]{:S(2)}) copy-start(bf16[2304,1152]{1,0:T(8,128)(2,1)S(1)} %get-tuple-element.38.p_ref) | copy-start | bytes 15925252
  48.3 0.7 copy-start.8
  50.2 5.5 %copy-start.12 = (bf16[160,256]{1,0:T(8,128)(2,1)S(1)}, bf16[160,256]{1,0:T(8,128)(2,1)}, u32[]{:S(2)}) copy-start(bf16[160,256]{1,0:T(8,128)(2,1)} %constant.92.clone.rows_ref) | copy-start | bytes 245764
  55.7 21.6 %copy-start.7 = (bf16[4,1,72,1152]{3,2,1,0:T(8,128)(2,1)S(1)}, bf16[4,1,72,1152]{3,2,1,0:T(8,128)(2,1)}, u32[]{:S(2)}) copy-start(bf16[4,1,72,1152]{3,2,1,0:T(8,128)(2,1)} %param.15) | copy-start | bytes 1990660
  55.7 21.5 %copy-start.9 = (bf16[1152,16]{0,1:T(8,128)(2,1)S(1)}, bf16[1152,16]{0,1:T(8,128)(2,1)}, u32[]{:S(2)}) copy-start(bf16[1152,16]{0,1:T(8,128)(2,1)} %param.22) | copy-start | bytes 110596
  55.7 21.5 %copy-start.10 = (bf16[4,1,72,16]{2,3,1,0:T(8,128)(2,1)S(1)}, bf16[4,1,72,16]{2,3,1,0:T(8,128)(2,1)}, u32[]{:S(2)}) copy-start(bf16[4,1,72,16]{2,3,1,0:T(8,128)(2,1)} %param.16) | copy-start | bytes 27652
  55.7 32.2 %copy-start.15 = (bf16[4,72,16]{1,2,0:T(8,128)(2,1)S(1)}, bf16[4,72,16]{1,2,0:T(8,128)(2,1)}, u32[]{:S(2)}) copy-start(bf16[4,72,16]{1,2,0:T(8,128)(2,1)} %param.17) | copy-start | bytes 27652
  56.4 20.8 %collective-permute-start = (bf16[640,640]{1,0:T(8,128)(2,1)S(1)}, bf16[640,640]{1,0:T(8,128)(2,1)S(1)}, u32[]{:S(2)}, u32[]{:S(2)}) collective-permute-start(bf16[640,640]{1,0:T(8,128)(2,1)S(1)} %shard_map.152.mine_ref), channel_id=1, source_target_pairs={{0,1},{1,0},{2,3},{3,2},{4,5},{5,4},{6,7},{7,6},{8,9},{9,8},{10,11... | collective-permute-start | bytes 2457608 | tf_op jit(solution)/shard_map/ppermute | solution.py:463
  79.8 8.1 %collective-permute-start.1 = (bf16[4,16,72]{2,1,0:T(8,128)(2,1)S(1)}, bf16[4,16,72]{2,1,0:T(8,128)(2,1)S(1)}, u32[]{:S(2)}, u32[]{:S(2)}) collective-permute-start(bf16[4,16,72]{2,1,0:T(8,128)(2,1)S(1)} %shard_map.153), channel_id=1, source_target_pairs={{32,0},{64,32},{96,64},{128,96},{160,128},{192,160},{224,192},{256... | collective-permute-start | bytes 27656 | tf_op jit(solution)/shard_map/ppermute | solution.py:483
  87.9 56.8 %copy-start.5 = (bf16[4,16,72]{2,1,0:T(8,128)(2,1)}, bf16[4,16,72]{2,1,0:T(8,128)(2,1)S(1)}, u32[]{:S(2)}) copy-start(bf16[4,16,72]{2,1,0:T(8,128)(2,1)S(1)} %broadcast_select_fusion.lat_ref) | copy-start | bytes 27652
  88.5 31.7 %all-to-all-start.2 = ((bf16[32,16,72]{2,1,0:T(8,128)(2,1)}), bf16[32,16,72]{2,1,0:T(8,128)(2,1)S(1)}, u32[]{:S(2)}, u32[]{:S(2)}) async-start(bf16[32,16,72]{2,1,0:T(8,128)(2,1)} %bitcast.18), calls=%async_computation.2 | async-start | bytes 262144 | tf_op jit(solution)/shard_map/all_to_all | solution.py:486
  120.2 0.6 copy-start.14
  134.0 10.6 %all-to-all-start.3 = ((bf16[4,72,640]{2,1,0:T(8,128)(2,1)}), bf16[4,72,640]{2,1,0:T(8,128)(2,1)S(1)}, u32[]{:S(2)}, u32[]{:S(2)}) async-start(bf16[4,72,640]{2,1,0:T(8,128)(2,1)} %shard_map.156), calls=%async_computation.3 | async-start | bytes 737280 | tf_op jit(solution)/shard_map/all_to_all | solution.py:529
  144.7 1.4 copy-start.13
Sparse Core Ops, SparseCore 0:
  14.7 85.2 all-gather.1

commit v4 on v3

--- a/solution.py
+++ b/solution.py
@@ -59,31 +59,68 @@
     return center * lax.rsqrt(spread + 1e-06)
 
 
-def pack_kernel(core_ref, x_ref, w_ref, o_ref):
-    width = x_ref.shape[-1] // o_ref.shape[0]
-    shard = w_ref[...].astype(F32)
-    half = shard.shape[-1] // 2
-    shard = jnp.where(core_ref[0] == 0, shard[:, :half], shard[:, half:])
-    weight = jnp.concatenate([shard[:, : half // 2], shard[:, half // 2 :]], axis=0).astype(BF16)
-    for part in range(o_ref.shape[0]):
-        o_ref[part, :, :width] = x_ref[0, :, part * width : (part + 1) * width]
-        o_ref[part, :, width:] = weight
-
-
-def gather_kernel(w_ref, sout_ref, o_ref):
-    rows = o_ref.shape[0]
-    blank = jnp.zeros((rows, SLOT - HDIM), BF16)
+def pack_kernel(
+    core_ref, x_ref, tout_ref, sqkv_ref, sout_ref, o_ref, shard_ref,
+    x, tout, sqkv, sout, packed, shard, x_sem, w_sem, o_sem,
+):
+    videos, tokens, columns = x.shape
+    pairs = packed.shape[0] // videos
+    width = columns // pairs
+
+    def load(v):
+        return pltpu.make_async_copy(x_ref.at[v], x.at[v], x_sem.at[v])
+
+    weights = [
+        pltpu.make_async_copy(source, target, w_sem.at[i])
+        for i, (source, target) in enumerate(((tout_ref, tout), (sqkv_ref, sqkv), (sout_ref, sout)))
+    ]
+
+    def store(v):
+        at = slice(pairs * v, pairs * (v + 1))
+        return pltpu.make_async_copy(packed.at[at], o_ref.at[at], o_sem.at[v])
+
+    weights[0].start()
+    load(0).start()
+    weights[1].start()
+    weights[2].start()
+    for v in range(1, videos):
+        load(v).start()
+
+    weights[0].wait()
+    half = tout.shape[-1] // 2
+    left, right = tout[:, :half].astype(F32), tout[:, half:].astype(F32)
+    own = jnp.where(core_ref[0] == 0, left, right)
+    weight = jnp.concatenate([own[:, : half // 2], own[:, half // 2 :]], axis=0).astype(BF16)
+    load(0).wait()
+    for part in range(pairs):
+        packed[part, :, :width] = x[0, :, part * width : (part + 1) * width]
+        packed[part, :, width:] = weight
+    store(0).start()
+
+    weights[1].wait()
+    weights[2].wait()
+    blank = jnp.zeros((tokens, SLOT - HDIM), BF16)
     for i, part in enumerate((1, 2, 0)):
         pieces = []
         for h in range(HEADS):
             at = HDIM * (3 * h + part)
-            pieces += [w_ref[:, at : at + HDIM], blank]
-        o_ref[:, PADDED * i : PADDED * (i + 1)] = jnp.concatenate(pieces, axis=-1)
-    sout = sout_ref[...].astype(F32)
-    half = sout.shape[-1] // 2
-    sout = jnp.concatenate([sout[:, :half], sout[:, half:]], axis=0)
-    sout = jnp.concatenate([sout, jnp.zeros((rows, PADDED - half), F32)], axis=-1)
-    o_ref[:, 3 * PADDED :] = sout.astype(BF16)
+            pieces += [sqkv[:, at : at + HDIM], blank]
+        shard[:, PADDED * i : PADDED * (i + 1)] = jnp.concatenate(pieces, axis=-1)
+    ends = jnp.concatenate([sout[:, :half].astype(F32), sout[:, half:].astype(F32)], axis=0)
+    ends = jnp.concatenate([ends, jnp.zeros((tokens, PADDED - half), F32)], axis=-1)
+    shard[:, 3 * PADDED :] = ends.astype(BF16)
+    last = pltpu.make_async_copy(shard, shard_ref, w_sem.at[3])
+    last.start()
+
+    for v in range(1, videos):
+        load(v).wait()
+        for part in range(pairs):
+            packed[pairs * v + part, :, :width] = x[v, :, part * width : (part + 1) * width]
+            packed[pairs * v + part, :, width:] = weight
+        store(v).start()
+    last.wait()
+    for v in range(videos):
+        store(v).wait()
 
 
 def temporal_columns():
@@ -116,21 +153,26 @@
         lax.broadcasted_iota(jnp.int32, (rows, rows), 0) % 8
         == lax.broadcasted_iota(jnp.int32, (rows, rows), 1) % 8
     )
-    for block in range(tokens // 8):
-        piece = parts[:, 8 * block : 8 * block + 8, :].reshape(rows, -1).astype(BF16)
-        v = piece[:, 512 : 512 + 2 * SLOT]
-        out = None
-        for head in range(2):
-            q = piece[:, 256 * head : 256 * head + 128]
-            k = piece[:, 256 * head + 128 : 256 * head + 256]
-            scores = jnp.where(same, mm_nt(q, k) * SCORE_SCALE, -jnp.inf)
-            top = jnp.max(scores, axis=-1, keepdims=True)
-            raised = jnp.exp(scores - top)
-            weights = (raised / jnp.sum(raised, axis=-1, keepdims=True)).astype(BF16)
-            found = mm(weights, v)
-            out = found if out is None else jnp.where(first, out, found)
-        total[:, 8 * block : 8 * block + 8, :] = out.reshape(frames, 8, 2 * SLOT)
-    o_ref[...] = total[...].astype(BF16)
+    blocks = tokens // 8
+    pieces = [parts[:, 8 * i : 8 * i + 8, :].reshape(rows, -1).astype(BF16) for i in range(blocks)]
+    scores = [
+        mm_nt(piece[:, 256 * head : 256 * head + 128], piece[:, 256 * head + 128 : 256 * head + 256])
+        for piece in pieces
+        for head in range(2)
+    ]
+    scores = jnp.concatenate(scores, axis=0).reshape(2 * blocks, rows, rows)
+    scores = jnp.where(same[None], scores * SCORE_SCALE, -jnp.inf)
+    raised = jnp.exp(scores - jnp.max(scores, axis=-1, keepdims=True))
+    weights = (raised / jnp.sum(raised, axis=-1, keepdims=True)).astype(BF16)
+    for i in range(blocks):
+        v = pieces[i][:, 512 : 512 + 2 * SLOT]
+        out = jnp.where(first, mm(weights[2 * i], v), mm(weights[2 * i + 1], v))
+        total[:, 8 * i : 8 * i + 8, :] = out.reshape(frames, 8, 2 * SLOT)
+    side = total[:, :, 128:]
+    third = tokens // 3
+    side = [side[:, third * i : third * (i + 1), :] for i in range(3)] + [jnp.zeros((frames, third, 32), F32)]
+    o_ref[:, :tokens, :] = total[:, :, :128].astype(BF16)
+    o_ref[:, tokens:, :] = jnp.concatenate(side, axis=-1).astype(BF16)
 
 
 def unstack_kernel(x_ref, rows_ref, w_ref):
@@ -149,7 +191,9 @@
     videos, tokens, width = hid_ref.shape
     rows = videos * tokens
     pairs = att_ref.shape[0] // videos
-    att = att_ref[...].astype(F32).reshape(videos, pairs, tokens, 2 * SLOT)
+    att = att_ref[...].astype(F32)
+    side = jnp.concatenate([att[:, tokens:, 32 * i : 32 * (i + 1)] for i in range(3)], axis=1)
+    att = jnp.concatenate([att[:, :tokens, :], side], axis=-1).reshape(videos, pairs, tokens, 2 * SLOT)
     own = far = None
     for p in range(pairs):
         part = att[:, p].reshape(rows, 2 * SLOT).astype(BF16)
@@ -169,55 +213,66 @@
         o_ref[v] = (coef_ref[2] * clean + coef_ref[3] * pred).astype(BF16)
 
 
-def place_kernel(mod_ref, wemb_ref, ua_ref, va_ref, cb_ref, sb_ref, o_ref, sums_ref):
+def centered_place(c, ua_ref, va_ref, cb_ref, sb_ref):
+    place = ua_ref[pl.ds(c, 1), :] * cb_ref[...] + va_ref[pl.ds(c, 1), :] * sb_ref[...]
+    return place - jnp.mean(place, axis=-1, keepdims=True)
+
+
+def place_kernel(wemb_ref, ua_ref, va_ref, cb_ref, sb_ref, sums_ref):
     tokens, width = cb_ref.shape
-    members = o_ref.shape[0] // tokens
+    blank = jnp.zeros((tokens, 7), F32)
+
+    def one(few, carry):
+        for i in range(4):
+            c = 4 * few + i
+            center = centered_place(c, ua_ref, va_ref, cb_ref, sb_ref)
+            high = center.astype(BF16)
+            low = (center - high.astype(F32)).astype(BF16)
+            cross = (mm_nt(high, wemb_ref[...]) + mm_nt(low, wemb_ref[...])) * (2.0 / width)
+            square = jnp.mean(center * center, axis=-1, keepdims=True)
+            sums_ref[c] = jnp.concatenate([cross, square, blank], axis=-1).T
+        return carry
+
+    lax.fori_loop(0, sums_ref.shape[0] // 4, one, 0)
+
+
+def prepare_kernel(
+    group_ref, few_ref, mod_ref, ua_ref, va_ref, cb_ref, sb_ref, w_ref, few_out, q_out, kv_out,
+    p, w, made, w_sem, out_sem,
+):
+    rows = q_out.shape[0]
+    tokens = cb_ref.shape[0]
+    step = 2 * rows
+    steps = made.shape[0] // step
+
+    edges = (0, 512, 2 * PADDED, 3 * PADDED)
+
+    def load_w(part):
+        at = slice(edges[part], edges[part + 1])
+        return pltpu.make_async_copy(w_ref.at[:, at], w.at[:, at], w_sem.at[part])
+
+    def store(part, i):
+        at = (slice(step * i, step * (i + 1)), slice(edges[part], edges[part + 1]))
+        return pltpu.make_async_copy(made.at[at], kv_out.at[at], out_sem.at[steps * part + i])
+
+    for part in range(3):
+        load_w(part).start()
     gain = 1.0 + mod_ref[4:5, :]
-    made = []
-    for i in range(members):
-        c = pl.program_id(0) * members + i
-        place = ua_ref[pl.ds(c, 1), :] * cb_ref[...] + va_ref[pl.ds(c, 1), :] * sb_ref[...]
-        center = place - jnp.mean(place, axis=-1, keepdims=True)
-        made.append(center * gain)
-        high = center.astype(BF16)
-        low = (center - high.astype(F32)).astype(BF16)
-        cross = (mm_nt(high, wemb_ref[...]) + mm_nt(low, wemb_ref[...])) * (2.0 / width)
-        square = jnp.mean(center * center, axis=-1, keepdims=True)
-        blank = jnp.zeros((tokens, 7), F32)
-        sums_ref[i] = jnp.concatenate([cross, square, blank], axis=-1).T
-    o_ref[...] = jnp.concatenate(made, axis=0).astype(BF16)
-
-
-def prepare_kernel(group_ref, few_ref, p_ref, w_ref, few_out, q_out, kv_out, p, w, made, p_sem, w_sem, out_sem):
-    rows = q_out.shape[0]
-    steps = made.shape[0] // 2
-    step = made.shape[1]
-
-    def load_w(part):
-        at = slice(PADDED * part, PADDED * (part + 1))
-        return pltpu.make_async_copy(w_ref.at[:, at], w.at[:, at], w_sem.at[part])
-
-    def load_p(part):
-        at = slice(step * part, step * (part + 1))
-        return pltpu.make_async_copy(p_ref.at[at, :], p.at[at, :], p_sem.at[part])
-
-    def store(part, i):
-        at = kv_out.at[step * i : step * (i + 1), PADDED * part : PADDED * (part + 1)]
-        slot = steps * part + i
-        return pltpu.make_async_copy(made.at[slot], at, out_sem.at[slot])
-
-    load_w(0).start()
-    for i in range(steps):
-        load_p(i).start()
-    load_w(1).start()
-    load_w(2).start()
+
+    def place(i):
+        for c in range(step // tokens * i, step // tokens * (i + 1), 2):
+            two = [centered_place(c + j, ua_ref, va_ref, cb_ref, sb_ref) * gain for j in range(2)]
+            p[tokens * c : tokens * (c + 2), :] = jnp.concatenate(two, axis=0).astype(BF16)
+
+    place(0)
     for part in range(2):
         load_w(part).wait()
         for i in range(steps):
-            if part == 0:
-                load_p(i).wait()
             here = slice(step * i, step * (i + 1))
-            made[steps * part + i] = mm(p[here, :], w[:, PADDED * part : PADDED * (part + 1)]).astype(BF16)
+            columns = slice(edges[part], edges[part + 1])
+            made[here, columns] = mm(p[here, :], w[:, columns]).astype(BF16)
+            if part == 0 and i + 1 < steps:
+                place(i + 1)
             store(part, i).start()
     load_w(2).wait()
     start = pl.multiple_of(group_ref[0] * rows, rows)
@@ -379,23 +434,28 @@
     half = width // 2
     width_part = t_qkv.shape[-1] // pairs
     sent = width_part + half // 2
-    packed = call(
+    packed, w_shard = call(
         pack_kernel,
-        jax.ShapeDtypeStruct((frames, tokens, sent), BF16),
-        (core.reshape(1), t_qkv.reshape(videos, tokens, -1), w_tout),
-        grid=(videos,),
-        in_specs=[
-            pl.BlockSpec(memory_space=pltpu.SMEM),
-            pl.BlockSpec((1, tokens, t_qkv.shape[-1]), lambda v: (v, 0, 0)),
-            pl.BlockSpec(w_tout.shape, lambda v: (0, 0)),
+        (
+            jax.ShapeDtypeStruct((frames, tokens, sent), BF16),
+            jax.ShapeDtypeStruct((w_sqkv.shape[0], 4 * PADDED), BF16),
+        ),
+        (core.reshape(1), t_qkv.reshape(videos, tokens, -1), w_tout, w_sqkv, w_sout),
+        scratch=[
+            pltpu.VMEM((videos, tokens, t_qkv.shape[-1]), BF16),
+            pltpu.VMEM(w_tout.shape, BF16),
+            pltpu.VMEM(w_sqkv.shape, BF16),
+            pltpu.VMEM(w_sout.shape, BF16),
+            pltpu.VMEM((frames, tokens, sent), BF16),
+            pltpu.VMEM((w_sqkv.shape[0], 4 * PADDED), BF16),
+            pltpu.SemaphoreType.DMA((videos,)),
+            pltpu.SemaphoreType.DMA((4,)),
+            pltpu.SemaphoreType.DMA((videos,)),
         ],
-        out_specs=pl.BlockSpec((pairs, tokens, sent), lambda v: (v, 0, 0)),
-    )
-    w_sqkv, w_sout, packed = lax.optimization_barrier((w_sqkv, w_sout, packed))
-    w_shard = call(
-        gather_kernel,
-        jax.ShapeDtypeStruct((w_sqkv.shape[0], 4 * PADDED), BF16),
-        (w_sqkv, w_sout),
+        smem=(0,),
+        hbm=(1, 2, 3, 4),
+        hbm_out=(0, 1),
+        vmem=56,
     )
     w_spatial = lax.all_gather(w_shard, "queue", axis=0, tiled=True)
 
@@ -415,20 +475,12 @@
     ua, va, cb, sb = position_factors(seqs, tokens, width)
     rows = seqs * tokens
     own_rows = videos * tokens
-    placed, sums = call(
+    sums = call(
         place_kernel,
-        (
-            jax.ShapeDtypeStruct((rows, width), BF16),
-            jax.ShapeDtypeStruct((seqs, 24, tokens), F32),
-        ),
-        (new_mods, w_embed, ua, va, cb, sb),
-        grid=(rows // own_rows,),
-        in_specs=[pl.BlockSpec(a.shape, lambda i: (0, 0)) for a in (new_mods, w_embed, ua, va, cb, sb)],
-        out_specs=(
-            pl.BlockSpec((own_rows, width), lambda i: (i, 0)),
-            pl.BlockSpec((videos, 24, tokens), lambda i: (i, 0, 0)),
-        ),
+        jax.ShapeDtypeStruct((seqs, 24, tokens), F32),
+        (w_embed, ua, va, cb, sb),
         flops=100_000_000,
+        vmem=56,
     )
     gain, shift = 1.0 + new_mods[4:5], new_mods[3:4]
     emb_f32 = w_embed.astype(F32)
@@ -442,13 +494,13 @@
     latents_t = latents.reshape(videos, tokens, -1).transpose(0, 2, 1)
     fresh_t = fresh.transpose(0, 2, 1)
     w_final_t = w_final.T
-    early = (arrived, placed, sums, few, gram, mods, new_mods, coef, latents_t, fresh_t, w_final_t)
+    early = (arrived, sums, few, gram, mods, new_mods, coef, latents_t, fresh_t, w_final_t)
     early = lax.optimization_barrier(early)
-    arrived, placed, sums, few, gram, mods, new_mods, coef, latents_t, fresh_t, w_final_t = early
+    arrived, sums, few, gram, mods, new_mods, coef, latents_t, fresh_t, w_final_t = early
 
     attended = call(
         temporal_kernel,
-        jax.ShapeDtypeStruct((frames, tokens, 2 * SLOT), BF16),
+        jax.ShapeDtypeStruct((frames, tokens + tokens // 3, 128), BF16),
         (arrived, jnp.asarray(temporal_columns(), BF16)),
         scratch=[pltpu.VMEM((frames, tokens, 768), F32), pltpu.VMEM((frames, tokens, 2 * SLOT), F32)],
         flops=4_000_000_000,
@@ -495,17 +547,16 @@
             jax.ShapeDtypeStruct((own_rows, PADDED), F32),
             jax.ShapeDtypeStruct((rows, 2 * PADDED), BF16),
         ),
-        (group, few, placed, w_spatial),
+        (group, few, new_mods, ua, va, cb, sb, w_spatial),
         scratch=[
             pltpu.VMEM((rows, width), BF16),
             pltpu.VMEM((width, 3 * PADDED), BF16),
-            pltpu.VMEM((8, rows // 4, PADDED), BF16),
-            pltpu.SemaphoreType.DMA((4,)),
+            pltpu.VMEM((rows, 2 * PADDED), BF16),
             pltpu.SemaphoreType.DMA((3,)),
             pltpu.SemaphoreType.DMA((8,)),
         ],
         smem=(0,),
-        hbm=(2, 3),
+        hbm=(7,),
         hbm_out=(2,),
         flops=8_000_000_000,
         vmem=56,

time: 156 us -> 145 us (0.929)
  local copies, waits for them, and re-layouts: 15.1 us -> 8.14 us
  Pallas kernels: 55.1 us -> 50.7 us
  blocking collectives: 18.9 us -> 15.3 us
  other arithmetic: 2.41 us -> 4.59 us
  waiting for transfers between devices: 9.42 us -> 11.1 us
    unnamed x36, local copies, waits for them, and re-layouts: 9.05 us -> 2.1 us
    pallas_call x10 -> x9, Pallas kernels: 55.1 us -> 50.7 us  [call(): pl.pallas_call(kernel, out_shape=out_shape, in_specs=in_specs, out_specs=...]
    all_to_all x1, blocking collectives: 18.9 us -> 15.3 us  [shards(): lax.all_to_all(attended, 'queue', split_axis=0, concat_axis=0, tiled=True)]
    all_gather x1, waiting for transfers between devices: 0.02 us -> 3.23 us  [shards(): w_spatial = lax.all_gather(w_shard, 'queue', axis=0, tiled=True)]
  transfers between devices with their start and end apart: 6 -> 6, of which waited for: 3 -> 3; matrix products, arithmetic and copies ran while one was open for 6% -> 8% of each run, Pallas kernels for 24% -> 23%
where the time goes in v4:
time: 145 us; the launch traced here: 143 us
  Pallas kernels  50.7 us (35%)
  starting transfers between devices  31.4 us (22%)
  between operations  21.7 us (15%)
  blocking collectives  15.3 us (11%)
  waiting for transfers between devices  11.1 us (8%)
  local copies, waits for them, and re-layouts  8.14 us (6%)
  other arithmetic  4.59 us (3%)
    pallas_call x9, Pallas kernels, call(): pl.pallas_call(kernel, out_shape=out_shape, in_specs=in_specs, out_specs=...  50.7 us
    all_to_all x1, blocking collectives, shards(): lax.all_to_all(attended, 'queue', split_axis=0, concat_axis=0, tiled=True)  15.3 us
    all_to_all x1, starting transfers between devices, shards(): lax.all_to_all(jnp.tile(queued, (seqs // videos, 1, 1)), 'seq', split_axi...  13.7 us
    all_to_all x1, starting transfers between devices, shards(): lax.all_to_all(packed, 'queue', split_axis=0, concat_axis=0, tiled=True)  9.25 us
    ppermute x1, waiting for transfers between devices, shards(): lax.ppermute(stepped, 'queue', [(f, f - 1) for f in range(1, frames)])  4.96 us
    all_to_all x1, starting transfers between devices, shards(): lax.all_to_all(spatial, 'seq', split_axis=0, concat_axis=0, tiled=True, a...  3.47 us
    all_gather x1, waiting for transfers between devices, shards(): w_spatial = lax.all_gather(w_shard, 'queue', axis=0, tiled=True)  3.23 us
    ppermute x1, starting transfers between devices, shards(): lax.ppermute(stepped, 'queue', [(f, f - 1) for f in range(1, frames)])  3.08 us
  transfers between devices with their start and end apart: 6, of which 3 were waited for; matrix products, arithmetic and copies ran while one was open for 8% of the time, Pallas kernels for 23%

profile of v4, /device:TPU:24, one launch (start us, length us, event | category | flops | bytes accessed | tf_op | source)
XLA Modules:
  0.0 143.3 jit_solution(17013146125898052426)
XLA Ops:
  7.2 0.0 all-gather.2.cloned.1.call-start
  7.2 2.9 %shard_map.149 = (bf16[16,72,720]{2,1,0:T(8,128)(2,1)}, bf16[72,2560]{1,0:T(8,128)(2,1)}) custom-call(s32[1]{0:T(128)} %bitcast.core_ref, bf16[4,72,1728]{2,1,0:T(8,128)(2,1)} %bitcast.39, bf16[36,1152]{1,0:T(8,128)(2,1)} %tout_ref.1, bf16[72,1728]{1,0:T(8,128)(2,1)} %sqkv_ref.1, bf16[36,1152]{1,0:T(8,128)(2,1)} %sout_ref.1), custom_call_target="tpu_custom_call" | custom-call | bytes 1410052 | tf_op jit(solution)/shard_map/pallas_call | solution.py:44
  10.1 0.0 all-gather.2.cloned.1.call-update
  10.2 0.0 copy-start.17
  10.2 0.0 copy-start.16
  10.2 0.0 copy-start.4
  10.2 9.3 %all-to-all-start = ((bf16[16,72,720]{2,1,0:T(8,128)(2,1)}), bf16[16,72,720]{2,1,0:T(8,128)(2,1)S(1)}, u32[]{:S(2)}, u32[]{:S(2)}) async-start(bf16[16,72,720]{2,1,0:T(8,128)(2,1)} %get-tuple-element.20), calls=%async_computation | async-start | bytes 3538944 | tf_op jit(solution)/shard_map/all_to_all | solution.py:462
  19.5 0.1 slice.13
  19.5 0.6 dynamic_slice.23
  23.4 0.6 fusion.14
  26.6 0.1 pad_add_fusion
  26.7 0.6 dynamic_slice.21
  28.7 0.1 convert_reduce_fusion
  28.8 1.0 constant_dynamic-slice_fusion
  29.8 0.6 fusion.12
  30.5 0.1 fusion.4
  30.6 2.5 %concatenate.28.few_ref = bf16[48,1152]{1,0:T(8,128)(2,1)} concatenate(bf16[16,1152]{1,0:T(8,128)(2,1)S(1)} %get-tuple-element.45, bf16[16,1152]{1,0:T(8,128)(2,1)S(1)} %get-tuple-element.44, bf16[1,1152]{1,0:T(2,128)(2,1)S(1)} %fusion.11, bf16[7,1152]{1,0:T(8,128)(2,1)S(1)} %broadcast_in_dim.2, bf16[1,1152]{1,0:T(2,128)(2,1)S(1)} %fusion.9, bf16[7,1152]{1,0:T(8,128)(2,1)S(1)} %broadcast_in_dim.2), dimensions={0} | concatenate | bytes 221184 | tf_op jit(solution)/shard_map/concatenate | solution.py:493
  33.2 0.7 fusion
  33.8 0.0 copy-start.11
  33.8 0.4 fusion.6
  34.2 0.8 pad_maximum_fusion.3
  35.0 1.0 pad_maximum_fusion
  36.1 9.1 %shard_map.150.sums_ref = f32[32,24,72]{2,1,0:T(8,128)} custom-call(bf16[16,1152]{1,0:T(8,128)(2,1)} %wemb_ref.3, f32[32,1152]{1,0:T(8,128)} %get-tuple-element.43.ua_ref, f32[32,1152]{1,0:T(8,128)} %get-tuple-element.42.va_ref, f32[72,1152]{1,0:T(8,128)} %get-tuple-element.57.cb_ref, f32[72,1152]{1,0:T(8,128)} %get-tuple-element.58.sb_ref), custom_call_target="tpu_custom_call" | custom-call | flops 100000000 | bytes 995328 | tf_op jit(solution)/shard_map/pallas_call | solution.py:44
  45.2 0.1 pad_maximum_fusion.5.coef_ref
  45.3 0.3 fusion.13
  45.6 0.7 pad_maximum_fusion.4.gram_ref
  46.3 0.0 copy-start.12
  46.3 2.0 %shard_map.151 = bf16[16,96,128]{2,1,0:T(8,128)(2,1)S(1)} custom-call(bf16[16,72,720]{2,1,0:T(8,128)(2,1)S(1)} %all-to-all-done.x_ref, bf16[432,768]{1,0:T(8,128)(2,1)S(1)} %copy-done.11), custom_call_target="tpu_custom_call" | custom-call | flops 4000000000 | bytes 2322432 | tf_op jit(solution)/shard_map/pallas_call | solution.py:44
  48.3 0.0 copy-start.8
  48.4 0.7 shard_map.152.mine_ref
  49.0 1.9 %collective-permute-start = (bf16[640,640]{1,0:T(8,128)(2,1)S(1)}, bf16[640,640]{1,0:T(8,128)(2,1)S(1)}, u32[]{:S(2)}, u32[]{:S(2)}) collective-permute-start(bf16[640,640]{1,0:T(8,128)(2,1)S(1)} %shard_map.152.mine_ref), channel_id=1, source_target_pairs={{0,1},{1,0},{2,3},{3,2},{4,5},{5,4},{6,7},{7,6},{8,9},{9,8},{10,11... | collective-permute-start | bytes 2457608 | tf_op jit(solution)/shard_map/ppermute | solution.py:515
  50.9 15.3 %all_to_all.20.att_ref = bf16[16,96,128]{2,1,0:T(8,128)(2,1)S(1)} all-to-all(bf16[16,96,128]{2,1,0:T(8,128)(2,1)S(1)} %shard_map.151), channel_id=1, replica_groups=mesh['queue'=16,'seq'=32] {'queue'}, dimensions={0} | all-to-all | bytes 786432 | tf_op jit(solution)/shard_map/all_to_all | solution.py:516
  66.3 0.0 copy-start.15
  66.3 2.6 %shard_map.153 = bf16[4,16,72]{2,1,0:T(8,128)(2,1)S(1)} custom-call(f32[4]{0:T(128)S(1)} %pad_maximum_fusion.5.coef_ref, s32[1]{0:T(128)} %bitcast.core_ref, bf16[16,96,128]{2,1,0:T(8,128)(2,1)S(1)} %all_to_all.20.att_ref, bf16[4,72,1152]{2,1,0:T(8,128)(2,1)S(1)} %bitcast.36, bf16[4,16,72]{2,1,0:T(8,128)(2,1)S(1)} %bitcast.38, ...), custom_call_target="tpu_custom_call" | custom-call | flops 1000000000 | bytes 2768916 | tf_op jit(solution)/shard_map/pallas_call | solution.py:44
  68.8 3.1 %collective-permute-start.1 = (bf16[4,16,72]{2,1,0:T(8,128)(2,1)S(1)}, bf16[4,16,72]{2,1,0:T(8,128)(2,1)S(1)}, u32[]{:S(2)}, u32[]{:S(2)}) collective-permute-start(bf16[4,16,72]{2,1,0:T(8,128)(2,1)S(1)} %shard_map.153), channel_id=1, source_target_pairs={{32,0},{64,32},{96,64},{128,96},{160,128},{192,160},{224,192},{256... | collective-permute-start | bytes 27656 | tf_op jit(solution)/shard_map/ppermute | solution.py:535
  71.9 5.0 %collective-permute-done.1 = bf16[4,16,72]{2,1,0:T(8,128)(2,1)S(1)} collective-permute-done((bf16[4,16,72]{2,1,0:T(8,128)(2,1)S(1)}, bf16[4,16,72]{2,1,0:T(8,128)(2,1)S(1)}, u32[]{:S(2)}, u32[]{:S(2)}) %collective-permute-start.1) | collective-permute-done | bytes 9248 | tf_op jit(solution)/shard_map/ppermute | solution.py:535
  76.9 0.0 copy-start.6
  76.9 0.7 tile.4
  77.6 13.7 %all-to-all-start.2 = ((bf16[32,16,72]{2,1,0:T(8,128)(2,1)}), bf16[32,16,72]{2,1,0:T(8,128)(2,1)S(1)}, u32[]{:S(2)}, u32[]{:S(2)}) async-start(bf16[32,16,72]{2,1,0:T(8,128)(2,1)} %bitcast.18), calls=%async_computation.2 | async-start | bytes 262144 | tf_op jit(solution)/shard_map/all_to_all | solution.py:538
  91.3 3.2 %all-gather.2.cloned.1.call-done.w_ref = bf16[1152,2560]{1,0:T(8,128)(2,1)} async-done(((bf16[72,2560]{1,0:T(8,128)(2,1)}), bf16[1152,2560]{1,0:T(8,128)(2,1)}) %all-gather.2.cloned.1.call-update) | async-done | bytes 5898256 | tf_op jit(solution)/shard_map/all_gather | solution.py:460
  94.5 14.2 %shard_map.154 = (f32[48,1920]{1,0:T(8,128)}, f32[288,640]{1,0:T(8,128)}, bf16[2304,1280]{1,0:T(8,128)(2,1)}) custom-call(s32[1]{0:T(128)} %bitcast.17.group_ref, bf16[48,1152]{1,0:T(8,128)(2,1)} %concatenate.28.few_ref, f32[6,1152]{1,0:T(8,128)} %get-tuple-element.32.mod_ref, f32[32,1152]{1,0:T(8,128)} %get-tuple-element.43.ua_ref, ...), custom_call_target="tpu_custom_call" | custom-call | flops 8000000000 | bytes 6994948 | tf_op jit(solution)/shard_map/pallas_call | solution.py:44
  108.8 0.6 copy-done.14
  109.4 13.1 %shard_map.155 = bf16[4,72,640]{2,1,0:T(8,128)(2,1)} custom-call(s32[1]{0:T(128)} %bitcast.17.group_ref, bf16[32,16,72]{2,1,0:T(8,128)(2,1)} %copy-done.14, bf16[16,32]{1,0:T(8,128)(2,1)} %pad_maximum_fusion.4.gram_ref, f32[32,24,72]{2,1,0:T(8,128)} %shard_map.150.sums_ref, f32[48,1920]{1,0:T(8,128)} %get-tuple-element.34.few_ref, ...), custom_call_target="tpu_custom_call" | custom-call | flops 20000000000 | bytes 7300100 | tf_op jit(solution)/shard_map/pallas_call | solution.py:44
  122.5 3.5 %all-to-all-start.3 = ((bf16[4,72,640]{2,1,0:T(8,128)(2,1)}), bf16[4,72,640]{2,1,0:T(8,128)(2,1)S(1)}, u32[]{:S(2)}, u32[]{:S(2)}) async-start(bf16[4,72,640]{2,1,0:T(8,128)(2,1)} %shard_map.155), calls=%async_computation.3 | async-start | bytes 737280 | tf_op jit(solution)/shard_map/all_to_all | solution.py:580
  126.0 4.2 %shard_map.156.w_ref = bf16[640,1152]{1,0:T(8,128)(2,1)} custom-call(bf16[160,256]{1,0:T(8,128)(2,1)} %constant.92.clone.rows_ref, bf16[1152,2560]{1,0:T(8,128)(2,1)} %all-gather.2.cloned.1.call-done.w_ref), custom_call_target="tpu_custom_call" | custom-call | flops 20000000000 | bytes 5980160 | tf_op jit(solution)/shard_map/pallas_call | solution.py:44
  130.2 2.9 %all-to-all-done.3.att_ref = bf16[4,72,640]{2,1,0:T(8,128)(2,1)S(1)} async-done(((bf16[4,72,640]{2,1,0:T(8,128)(2,1)}), bf16[4,72,640]{2,1,0:T(8,128)(2,1)S(1)}, u32[]{:S(2)}, u32[]{:S(2)}) %all-to-all-start.3) | async-done | bytes 368672 | tf_op jit(solution)/shard_map/all_to_all | solution.py:580
  133.2 1.4 copy-done.13
  134.5 1.9 %shard_map.157 = bf16[4,72,1152]{2,1,0:T(8,128)(2,1)} custom-call(s32[1]{0:T(128)} %bitcast.16.seq_ref, bf16[4,72,640]{2,1,0:T(8,128)(2,1)S(1)} %all-to-all-done.3.att_ref, bf16[4,16,72]{2,1,0:T(8,128)(2,1)S(1)} %broadcast_select_fusion.lat_ref, bf16[16,1152]{1,0:T(8,128)(2,1)S(1)} %copy-done.5, f32[32,1152]{1,0:T(8,128)S(1)} %copy-done.3, ...), custom_call_target="tpu_custom_call" | custom-call | flops 1000000000 | bytes 2875396 | tf_op jit(solution)/shard_map/pallas_call | solution.py:44
  (38 shorter events, 0.1 us)
Async XLA Ops:
  7.2 87.3 %all-gather.2.cloned.1.call-start = ((), (), s32[]{:S(2)}) async-start(), calls=%async_computation.4 | async-start | bytes 6266880 | tf_op jit(solution)/shard_map/all_gather | solution.py:460
  10.2 9.3 %copy-start.17 = (s32[16]{0:T(128)S(1)}, s32[16]{0:T(128)}, u32[]{:S(2)}) copy-start(s32[16]{0:T(128)} %param.18) | copy-start | bytes 196
  10.2 13.2 %copy-start.16 = (f32[65]{0:T(128)S(1)}, f32[65]{0:T(128)}, u32[]{:S(2)}) copy-start(f32[65]{0:T(128)} %param.19) | copy-start | bytes 784
  10.2 18.5 %copy-start.4 = (bf16[16,1152]{1,0:T(8,128)(2,1)S(1)}, bf16[16,1152]{1,0:T(8,128)(2,1)}, u32[]{:S(2)}) copy-start(bf16[16,1152]{1,0:T(8,128)(2,1)} %wemb_ref.3) | copy-start | bytes 110596
  10.2 36.0 %all-to-all-start = ((bf16[16,72,720]{2,1,0:T(8,128)(2,1)}), bf16[16,72,720]{2,1,0:T(8,128)(2,1)S(1)}, u32[]{:S(2)}, u32[]{:S(2)}) async-start(bf16[16,72,720]{2,1,0:T(8,128)(2,1)} %get-tuple-element.20), calls=%async_computation | async-start | bytes 3538944 | tf_op jit(solution)/shard_map/all_to_all | solution.py:462
  33.2 12.1 %copy-start.5 = (bf16[16,1152]{1,0:T(8,128)(2,1)S(1)}, bf16[16,1152]{1,0:T(8,128)(2,1)}, u32[]{:S(2)}) copy-start(bf16[16,1152]{1,0:T(8,128)(2,1)} %wemb_ref.3) | copy-start | bytes 110596
  33.8 12.4 %copy-start.11 = (bf16[432,768]{1,0:T(8,128)(2,1)S(1)}, bf16[432,768]{1,0:T(8,128)(2,1)}, u32[]{:S(2)}) copy-start(bf16[432,768]{1,0:T(8,128)(2,1)} %constant.93.clone.pick_ref) | copy-start | bytes 1990660
  46.3 2.0 %copy-start.12 = (bf16[160,256]{1,0:T(8,128)(2,1)S(1)}, bf16[160,256]{1,0:T(8,128)(2,1)}, u32[]{:S(2)}) copy-start(bf16[160,256]{1,0:T(8,128)(2,1)} %constant.92.clone.rows_ref) | copy-start | bytes 245764
  48.3 17.9 %copy-start.8 = (bf16[4,1,72,1152]{3,2,1,0:T(8,128)(2,1)S(1)}, bf16[4,1,72,1152]{3,2,1,0:T(8,128)(2,1)}, u32[]{:S(2)}) copy-start(bf16[4,1,72,1152]{3,2,1,0:T(8,128)(2,1)} %param.15) | copy-start | bytes 1990660
  48.3 17.9 %copy-start.9 = (bf16[1152,16]{0,1:T(8,128)(2,1)S(1)}, bf16[1152,16]{0,1:T(8,128)(2,1)}, u32[]{:S(2)}) copy-start(bf16[1152,16]{0,1:T(8,128)(2,1)} %param.22) | copy-start | bytes 110596
  48.3 17.9 %copy-start.10 = (bf16[4,1,72,16]{2,3,1,0:T(8,128)(2,1)S(1)}, bf16[4,1,72,16]{2,3,1,0:T(8,128)(2,1)}, u32[]{:S(2)}) copy-start(bf16[4,1,72,16]{2,3,1,0:T(8,128)(2,1)} %param.16) | copy-start | bytes 27652
  49.0 17.2 %collective-permute-start = (bf16[640,640]{1,0:T(8,128)(2,1)S(1)}, bf16[640,640]{1,0:T(8,128)(2,1)S(1)}, u32[]{:S(2)}, u32[]{:S(2)}) collective-permute-start(bf16[640,640]{1,0:T(8,128)(2,1)S(1)} %shard_map.152.mine_ref), channel_id=1, source_target_pairs={{0,1},{1,0},{2,3},{3,2},{4,5},{5,4},{6,7},{7,6},{8,9},{9,8},{10,11... | collective-permute-start | bytes 2457608 | tf_op jit(solution)/shard_map/ppermute | solution.py:515
  66.3 10.6 %copy-start.15 = (bf16[4,72,16]{1,2,0:T(8,128)(2,1)S(1)}, bf16[4,72,16]{1,2,0:T(8,128)(2,1)}, u32[]{:S(2)}) copy-start(bf16[4,72,16]{1,2,0:T(8,128)(2,1)} %param.17) | copy-start | bytes 27652
  68.8 8.1 %collective-permute-start.1 = (bf16[4,16,72]{2,1,0:T(8,128)(2,1)S(1)}, bf16[4,16,72]{2,1,0:T(8,128)(2,1)S(1)}, u32[]{:S(2)}, u32[]{:S(2)}) collective-permute-start(bf16[4,16,72]{2,1,0:T(8,128)(2,1)S(1)} %shard_map.153), channel_id=1, source_target_pairs={{32,0},{64,32},{96,64},{128,96},{160,128},{192,160},{224,192},{256... | collective-permute-start | bytes 27656 | tf_op jit(solution)/shard_map/ppermute | solution.py:535
  76.9 56.2 %copy-start.6 = (bf16[4,16,72]{2,1,0:T(8,128)(2,1)}, bf16[4,16,72]{2,1,0:T(8,128)(2,1)S(1)}, u32[]{:S(2)}) copy-start(bf16[4,16,72]{2,1,0:T(8,128)(2,1)S(1)} %broadcast_select_fusion.lat_ref) | copy-start | bytes 27652
  77.6 31.1 %all-to-all-start.2 = ((bf16[32,16,72]{2,1,0:T(8,128)(2,1)}), bf16[32,16,72]{2,1,0:T(8,128)(2,1)S(1)}, u32[]{:S(2)}, u32[]{:S(2)}) async-start(bf16[32,16,72]{2,1,0:T(8,128)(2,1)} %bitcast.18), calls=%async_computation.2 | async-start | bytes 262144 | tf_op jit(solution)/shard_map/all_to_all | solution.py:538
  108.7 0.7 copy-start.14
  122.5 10.6 %all-to-all-start.3 = ((bf16[4,72,640]{2,1,0:T(8,128)(2,1)}), bf16[4,72,640]{2,1,0:T(8,128)(2,1)S(1)}, u32[]{:S(2)}, u32[]{:S(2)}) async-start(bf16[4,72,640]{2,1,0:T(8,128)(2,1)} %shard_map.155), calls=%async_computation.3 | async-start | bytes 737280 | tf_op jit(solution)/shard_map/all_to_all | solution.py:580
  126.0 7.1 %copy-start = (f32[72,1152]{1,0:T(8,128)S(1)}, f32[72,1152]{1,0:T(8,128)}, u32[]{:S(2)}) copy-start(f32[72,1152]{1,0:T(8,128)} %get-tuple-element.57.cb_ref) | copy-start | bytes 995332
  126.0 7.1 %copy-start.1 = (f32[72,1152]{1,0:T(8,128)S(1)}, f32[72,1152]{1,0:T(8,128)}, u32[]{:S(2)}) copy-start(f32[72,1152]{1,0:T(8,128)} %get-tuple-element.58.sb_ref) | copy-start | bytes 995332
  126.0 7.1 %copy-start.2 = (f32[32,1152]{1,0:T(8,128)S(1)}, f32[32,1152]{1,0:T(8,128)}, u32[]{:S(2)}) copy-start(f32[32,1152]{1,0:T(8,128)} %get-tuple-element.42.va_ref) | copy-start | bytes 442372
  126.0 7.1 %copy-start.3 = (f32[32,1152]{1,0:T(8,128)S(1)}, f32[32,1152]{1,0:T(8,128)}, u32[]{:S(2)}) copy-start(f32[32,1152]{1,0:T(8,128)} %get-tuple-element.43.ua_ref) | copy-start | bytes 442372
  126.0 7.1 %copy-start.7 = (f32[6,1152]{1,0:T(8,128)S(1)}, f32[6,1152]{1,0:T(8,128)}, u32[]{:S(2)}) copy-start(f32[6,1152]{1,0:T(8,128)} %get-tuple-element.32.mod_ref) | copy-start | bytes 82948
  133.2 1.4 copy-start.13
Sparse Core Ops, SparseCore 0:
  11.1 83.4 all-gather.1

commit v5 on v4

--- a/solution.py
+++ b/solution.py
@@ -237,7 +237,7 @@
 
 
 def prepare_kernel(
-    group_ref, few_ref, mod_ref, ua_ref, va_ref, cb_ref, sb_ref, w_ref, few_out, q_out, kv_out,
+    group_ref, few_ref, mod_ref, ua_ref, va_ref, cb_ref, sb_ref, w_ref, mix_out, offset_out, q_out, kv_out,
     p, w, made, w_sem, out_sem,
 ):
     rows = q_out.shape[0]
@@ -251,9 +251,9 @@
         at = slice(edges[part], edges[part + 1])
         return pltpu.make_async_copy(w_ref.at[:, at], w.at[:, at], w_sem.at[part])
 
-    def store(part, i):
-        at = (slice(step * i, step * (i + 1)), slice(edges[part], edges[part + 1]))
-        return pltpu.make_async_copy(made.at[at], kv_out.at[at], out_sem.at[steps * part + i])
+    def store(i):
+        at = slice(step * i, step * (i + 1))
+        return pltpu.make_async_copy(made.at[at], kv_out.at[at], out_sem.at[i])
 
     for part in range(3):
         load_w(part).start()
@@ -265,26 +265,31 @@
             p[tokens * c : tokens * (c + 2), :] = jnp.concatenate(two, axis=0).astype(BF16)
 
     place(0)
-    for part in range(2):
-        load_w(part).wait()
-        for i in range(steps):
-            here = slice(step * i, step * (i + 1))
+    for i in range(steps):
+        here = slice(step * i, step * (i + 1))
+        for part in range(2):
+            if i == 0:
+                load_w(part).wait()
             columns = slice(edges[part], edges[part + 1])
             made[here, columns] = mm(p[here, :], w[:, columns]).astype(BF16)
             if part == 0 and i + 1 < steps:
                 place(i + 1)
-            store(part, i).start()
+        store(i).start()
     load_w(2).wait()
     start = pl.multiple_of(group_ref[0] * rows, rows)
-    q_out[...] = mm(p[pl.ds(start, rows), :], w[:, 2 * PADDED :])
-    few_out[...] = mm(few_ref[...], w[...])
-    for part in range(2):
-        for i in range(steps):
-            store(part, i).wait()
+    q_out[...] = mm(p[pl.ds(start, rows), :], w[:, 2 * PADDED :]).astype(BF16)
+    few = mm(few_ref[...], w[...])
+    patch = mix_out.shape[0] // 2
+    mix = few[:patch] + few[patch : 2 * patch]
+    high = mix.astype(BF16).astype(F32)
+    mix_out[...] = jnp.concatenate([high, mix - high], axis=0).astype(BF16)
+    offset_out[...] = few[2 * patch : 2 * patch + 8] + few[2 * patch + 8 :]
+    for i in range(steps):
+        store(i).wait()
 
 
 def spatial_kernel(
-    group_ref, lat_ref, gram_ref, sums_ref, few_ref, pq_ref, pkv_ref,
+    group_ref, lat_ref, gram_ref, sums_ref, mix_ref, offset_ref, pq_ref, pkv_ref,
     o_ref, held, columns, keys, vals, sem,
 ):
     chunks, patch, tokens = lat_ref.shape
@@ -310,15 +315,11 @@
         rows = jnp.concatenate([twice, jnp.broadcast_to(scale, (8, tokens))], axis=0)
         columns[tokens * c : tokens * (c + 1), :] = rows.T
 
-    lane = lax.broadcasted_iota(jnp.int32, (1, 2 * PADDED), 1)
-    ones = jnp.where((lane >= PADDED) & (lane % SLOT == HDIM), 1.0, 0.0)
-    few = few_ref[...]
-    mix = few[:patch] + few[patch : 2 * patch]
-    offset = few[2 * patch : 2 * patch + 1] + few[2 * patch + 8 : 2 * patch + 9]
-    high = mix.astype(BF16).astype(F32)
-    mix = jnp.concatenate([high, mix - high], axis=0).astype(BF16)
-    kv_mix, q_mix = mix[:, : 2 * PADDED], mix[:, 2 * PADDED :]
-    kv_offset, q_offset = offset[:, : 2 * PADDED] + ones, offset[:, 2 * PADDED :]
+    lane = lax.broadcasted_iota(jnp.int32, (1, PADDED), 1)
+    ones = jnp.where(lane % SLOT == HDIM, 1.0, 0.0)
+
+    kv_mix = mix_ref[:, : 2 * PADDED]
+    kv_offset = offset_ref[0:1, : 2 * PADDED] + jnp.concatenate([jnp.zeros_like(ones), ones], axis=-1)
 
     def one(index, carry):
         start = pl.multiple_of(index * block, block)
@@ -335,9 +336,8 @@
 
     column = columns[pl.ds(pl.multiple_of(group_ref[0] * block, block), block), :]
     latent, scale = column[:, : 2 * patch].astype(BF16), column[:, 2 * patch : 2 * patch + 1]
-    q_all = (mm(latent, q_mix) + pq_ref[...]) * scale + q_offset
+    q_all = (mm(latent, mix_ref[:, 2 * PADDED :]) + pq_ref[...].astype(F32)) * scale + offset_ref[0:1, 2 * PADDED :]
     q_all = q_all.astype(BF16).astype(F32)
-    lane = lane[:, :PADDED]
     merged = [None] * (PADDED // 128)
 
     def window(h):
@@ -540,11 +540,12 @@
     )
     groups = [[videos * g + i for i in range(videos)] for g in range(seqs // videos)]
     group = (seq_pos // videos).reshape(1)
-    few_out, pq, pkv = call(
+    mix, offset, pq, pkv = call(
         prepare_kernel,
         (
-            jax.ShapeDtypeStruct((few.shape[0], 3 * PADDED), F32),
-            jax.ShapeDtypeStruct((own_rows, PADDED), F32),
+            jax.ShapeDtypeStruct((2 * w_embed.shape[0], 3 * PADDED), BF16),
+            jax.ShapeDtypeStruct((8, 3 * PADDED), F32),
+            jax.ShapeDtypeStruct((own_rows, PADDED), BF16),
             jax.ShapeDtypeStruct((rows, 2 * PADDED), BF16),
         ),
         (group, few, new_mods, ua, va, cb, sb, w_spatial),
@@ -553,18 +554,18 @@
             pltpu.VMEM((width, 3 * PADDED), BF16),
             pltpu.VMEM((rows, 2 * PADDED), BF16),
             pltpu.SemaphoreType.DMA((3,)),
-            pltpu.SemaphoreType.DMA((8,)),
+            pltpu.SemaphoreType.DMA((4,)),
         ],
         smem=(0,),
         hbm=(7,),
-        hbm_out=(2,),
+        hbm_out=(3,),
         flops=8_000_000_000,
         vmem=56,
     )
     spatial = call(
         spatial_kernel,
         jax.ShapeDtypeStruct((videos, tokens, PADDED), BF16),
-        (group, everyone, gram, sums, few_out, pq, pkv),
+        (group, everyone, gram, sums, mix, offset, pq, pkv),
         scratch=[
             pltpu.VMEM((rows // own_rows, own_rows, 2 * PADDED), BF16),
             pltpu.VMEM((rows, 2 * latents.shape[-1] + 8), F32),
@@ -573,7 +574,7 @@
             pltpu.SemaphoreType.DMA((rows // own_rows,)),
         ],
         smem=(0,),
-        hbm=(6,),
+        hbm=(7,),
         flops=20_000_000_000,
         vmem=56,
     )
@@ -596,6 +597,7 @@
         (seq_pos.reshape(1), heads_out, queued, w_embed, ua, va, cb, sb, new_mods, w_s),
         smem=(0,),
         flops=1_000_000_000,
+        vmem=56,
     )
     return (
         queued.transpose(0, 2, 1).reshape(videos, 1, tokens, -1),

time: 145 us -> 146 us (level)
  no operation moved by 1% of the time
where the time goes in v5:
time: 146 us; the launch traced here: 144 us
  Pallas kernels  52.1 us (36%)
  starting transfers between devices  31.4 us (22%)
  between operations  21.7 us (15%)
  blocking collectives  15.2 us (10%)
  waiting for transfers between devices  11.2 us (8%)
  local copies, waits for them, and re-layouts  7.49 us (5%)
  other arithmetic  4.65 us (3%)
    pallas_call x9, Pallas kernels, call(): pl.pallas_call(kernel, out_shape=out_shape, in_specs=in_specs, out_specs=...  52.1 us
    all_to_all x1, blocking collectives, shards(): lax.all_to_all(attended, 'queue', split_axis=0, concat_axis=0, tiled=True)  15.2 us
    all_to_all x1, starting transfers between devices, shards(): lax.all_to_all(jnp.tile(queued, (seqs // videos, 1, 1)), 'seq', split_axi...  13.7 us
    all_to_all x1, starting transfers between devices, shards(): lax.all_to_all(packed, 'queue', split_axis=0, concat_axis=0, tiled=True)  9.25 us
    ppermute x1, waiting for transfers between devices, shards(): lax.ppermute(stepped, 'queue', [(f, f - 1) for f in range(1, frames)])  4.96 us
    all_to_all x1, starting transfers between devices, shards(): lax.all_to_all(spatial, 'seq', split_axis=0, concat_axis=0, tiled=True, a...  3.47 us
    all_gather x1, waiting for transfers between devices, shards(): w_spatial = lax.all_gather(w_shard, 'queue', axis=0, tiled=True)  3.23 us
    ppermute x1, starting transfers between devices, shards(): lax.ppermute(stepped, 'queue', [(f, f - 1) for f in range(1, frames)])  3.08 us
  transfers between devices with their start and end apart: 6, of which 3 were waited for; matrix products, arithmetic and copies ran while one was open for 8% of the time, Pallas kernels for 23%

profile of v5, /device:TPU:24, one launch (start us, length us, event | category | flops | bytes accessed | tf_op | source)
XLA Modules:
  0.0 144.1 jit_solution(3077866720262944090)
XLA Ops:
  7.2 0.0 all-gather.2.cloned.1.call-start
  7.2 2.9 %shard_map.149 = (bf16[16,72,720]{2,1,0:T(8,128)(2,1)}, bf16[72,2560]{1,0:T(8,128)(2,1)}) custom-call(s32[1]{0:T(128)} %bitcast.core_ref, bf16[4,72,1728]{2,1,0:T(8,128)(2,1)} %bitcast.38, bf16[36,1152]{1,0:T(8,128)(2,1)} %tout_ref.1, bf16[72,1728]{1,0:T(8,128)(2,1)} %sqkv_ref.1, bf16[36,1152]{1,0:T(8,128)(2,1)} %sout_ref.1), custom_call_target="tpu_custom_call" | custom-call | bytes 1410052 | tf_op jit(solution)/shard_map/pallas_call | solution.py:44
  10.2 0.0 all-gather.2.cloned.1.call-update
  10.2 0.0 copy-start.12
  10.2 0.0 copy-start.11
  10.2 0.0 copy-start.6
  10.2 9.3 %all-to-all-start = ((bf16[16,72,720]{2,1,0:T(8,128)(2,1)}), bf16[16,72,720]{2,1,0:T(8,128)(2,1)S(1)}, u32[]{:S(2)}, u32[]{:S(2)}) async-start(bf16[16,72,720]{2,1,0:T(8,128)(2,1)} %get-tuple-element.21), calls=%async_computation | async-start | bytes 3538944 | tf_op jit(solution)/shard_map/all_to_all | solution.py:462
  19.5 0.1 slice.13
  19.5 0.6 dynamic_slice.23
  23.4 0.6 fusion.14
  26.6 0.1 pad_add_fusion
  26.7 0.6 dynamic_slice.21
  28.7 0.1 convert_reduce_fusion
  28.8 1.0 constant_dynamic-slice_fusion
  29.9 0.6 fusion.12
  30.6 0.1 fusion.4
  30.7 2.5 %concatenate.28.few_ref = bf16[48,1152]{1,0:T(8,128)(2,1)} concatenate(bf16[16,1152]{1,0:T(8,128)(2,1)S(1)} %get-tuple-element.47, bf16[16,1152]{1,0:T(8,128)(2,1)S(1)} %get-tuple-element.46, bf16[1,1152]{1,0:T(2,128)(2,1)S(1)} %fusion.11, bf16[7,1152]{1,0:T(8,128)(2,1)S(1)} %broadcast_in_dim.2, bf16[1,1152]{1,0:T(2,128)(2,1)S(1)} %fusion.9, bf16[7,1152]{1,0:T(8,128)(2,1)S(1)} %broadcast_in_dim.2), dimensions={0} | concatenate | bytes 221184 | tf_op jit(solution)/shard_map/concatenate | solution.py:493
  33.2 0.7 fusion
  33.8 0.0 copy-start.3
  33.9 0.4 fusion.6
  34.2 0.8 pad_maximum_fusion.3
  35.1 1.1 pad_maximum_fusion
  36.1 9.1 %shard_map.150.sums_ref = f32[32,24,72]{2,1,0:T(8,128)} custom-call(bf16[16,1152]{1,0:T(8,128)(2,1)} %wemb_ref.3, f32[32,1152]{1,0:T(8,128)} %get-tuple-element.45.ua_ref, f32[32,1152]{1,0:T(8,128)} %get-tuple-element.44.va_ref, f32[72,1152]{1,0:T(8,128)} %get-tuple-element.59.cb_ref, f32[72,1152]{1,0:T(8,128)} %get-tuple-element.60.sb_ref), custom_call_target="tpu_custom_call" | custom-call | flops 100000000 | bytes 995328 | tf_op jit(solution)/shard_map/pallas_call | solution.py:44
  45.3 0.1 pad_maximum_fusion.5.coef_ref
  45.4 0.3 fusion.13
  45.7 0.7 pad_maximum_fusion.4.gram_ref
  46.3 0.0 copy-start.4
  46.4 2.0 %shard_map.151 = bf16[16,96,128]{2,1,0:T(8,128)(2,1)S(1)} custom-call(bf16[16,72,720]{2,1,0:T(8,128)(2,1)S(1)} %all-to-all-done.x_ref, bf16[432,768]{1,0:T(8,128)(2,1)S(1)} %copy-done.3), custom_call_target="tpu_custom_call" | custom-call | flops 4000000000 | bytes 2322432 | tf_op jit(solution)/shard_map/pallas_call | solution.py:44
  48.4 0.0 copy-start.2
  48.4 0.7 shard_map.152.mine_ref
  49.1 1.9 %collective-permute-start = (bf16[640,640]{1,0:T(8,128)(2,1)S(1)}, bf16[640,640]{1,0:T(8,128)(2,1)S(1)}, u32[]{:S(2)}, u32[]{:S(2)}) collective-permute-start(bf16[640,640]{1,0:T(8,128)(2,1)S(1)} %shard_map.152.mine_ref), channel_id=1, source_target_pairs={{0,1},{1,0},{2,3},{3,2},{4,5},{5,4},{6,7},{7,6},{8,9},{9,8},{10,11... | collective-permute-start | bytes 2457608 | tf_op jit(solution)/shard_map/ppermute | solution.py:515
  51.0 15.2 %all_to_all.20.att_ref = bf16[16,96,128]{2,1,0:T(8,128)(2,1)S(1)} all-to-all(bf16[16,96,128]{2,1,0:T(8,128)(2,1)S(1)} %shard_map.151), channel_id=1, replica_groups=mesh['queue'=16,'seq'=32] {'queue'}, dimensions={0} | all-to-all | bytes 786432 | tf_op jit(solution)/shard_map/all_to_all | solution.py:516
  66.3 0.0 copy-start.10
  66.3 2.5 %shard_map.153 = bf16[4,16,72]{2,1,0:T(8,128)(2,1)S(1)} custom-call(f32[4]{0:T(128)S(1)} %pad_maximum_fusion.5.coef_ref, s32[1]{0:T(128)} %bitcast.core_ref, bf16[16,96,128]{2,1,0:T(8,128)(2,1)S(1)} %all_to_all.20.att_ref, bf16[4,72,1152]{2,1,0:T(8,128)(2,1)S(1)} %bitcast.35, bf16[4,16,72]{2,1,0:T(8,128)(2,1)S(1)} %bitcast.37, ...), custom_call_target="tpu_custom_call" | custom-call | flops 1000000000 | bytes 2768916 | tf_op jit(solution)/shard_map/pallas_call | solution.py:44
  68.8 3.1 %collective-permute-start.1 = (bf16[4,16,72]{2,1,0:T(8,128)(2,1)S(1)}, bf16[4,16,72]{2,1,0:T(8,128)(2,1)S(1)}, u32[]{:S(2)}, u32[]{:S(2)}) collective-permute-start(bf16[4,16,72]{2,1,0:T(8,128)(2,1)S(1)} %shard_map.153), channel_id=1, source_target_pairs={{32,0},{64,32},{96,64},{128,96},{160,128},{192,160},{224,192},{256... | collective-permute-start | bytes 27656 | tf_op jit(solution)/shard_map/ppermute | solution.py:535
  72.0 5.0 %collective-permute-done.1 = bf16[4,16,72]{2,1,0:T(8,128)(2,1)S(1)} collective-permute-done((bf16[4,16,72]{2,1,0:T(8,128)(2,1)S(1)}, bf16[4,16,72]{2,1,0:T(8,128)(2,1)S(1)}, u32[]{:S(2)}, u32[]{:S(2)}) %collective-permute-start.1) | collective-permute-done | bytes 9248 | tf_op jit(solution)/shard_map/ppermute | solution.py:535
  76.9 0.0 copy-start.9
  76.9 0.7 tile.4
  77.6 13.7 %all-to-all-start.2 = ((bf16[32,16,72]{2,1,0:T(8,128)(2,1)}), bf16[32,16,72]{2,1,0:T(8,128)(2,1)S(1)}, u32[]{:S(2)}, u32[]{:S(2)}) async-start(bf16[32,16,72]{2,1,0:T(8,128)(2,1)} %bitcast.18), calls=%async_computation.2 | async-start | bytes 262144 | tf_op jit(solution)/shard_map/all_to_all | solution.py:538
  91.3 3.2 %all-gather.2.cloned.1.call-done.w_ref = bf16[1152,2560]{1,0:T(8,128)(2,1)} async-done(((bf16[72,2560]{1,0:T(8,128)(2,1)}), bf16[1152,2560]{1,0:T(8,128)(2,1)}) %all-gather.2.cloned.1.call-update) | async-done | bytes 5898256 | tf_op jit(solution)/shard_map/all_gather | solution.py:460
  94.5 14.0 %shard_map.154 = (bf16[32,1920]{1,0:T(8,128)(2,1)}, f32[8,1920]{1,0:T(8,128)}, bf16[288,640]{1,0:T(8,128)(2,1)}, bf16[2304,1280]{1,0:T(8,128)(2,1)}) custom-call(s32[1]{0:T(128)} %bitcast.17.group_ref, bf16[48,1152]{1,0:T(8,128)(2,1)} %concatenate.28.few_ref, f32[6,1152]{1,0:T(8,128)} %get-tuple-element.33.mod_ref, f32[32,1152]{1,0:T(8,128)} %get-tuple-element.45.ua_ref, ...), custom_call_target="tpu_custom_call" | custom-call | flops 8000000000 | bytes 6994948 | tf_op jit(solution)/shard_map/pallas_call | solution.py:44
  108.6 0.6 copy-done.8
  109.2 12.9 %shard_map.155 = bf16[4,72,640]{2,1,0:T(8,128)(2,1)} custom-call(s32[1]{0:T(128)} %bitcast.17.group_ref, bf16[32,16,72]{2,1,0:T(8,128)(2,1)} %copy-done.8, bf16[16,32]{1,0:T(8,128)(2,1)} %pad_maximum_fusion.4.gram_ref, f32[32,24,72]{2,1,0:T(8,128)} %shard_map.150.sums_ref, bf16[32,1920]{1,0:T(8,128)(2,1)} %get-tuple-element.35.mix_ref, ...), custom_call_target="tpu_custom_call" | custom-call | flops 20000000000 | bytes 6747140 | tf_op jit(solution)/shard_map/pallas_call | solution.py:44
  122.2 3.5 %all-to-all-start.3 = ((bf16[4,72,640]{2,1,0:T(8,128)(2,1)}), bf16[4,72,640]{2,1,0:T(8,128)(2,1)S(1)}, u32[]{:S(2)}, u32[]{:S(2)}) async-start(bf16[4,72,640]{2,1,0:T(8,128)(2,1)} %shard_map.155), calls=%async_computation.3 | async-start | bytes 737280 | tf_op jit(solution)/shard_map/all_to_all | solution.py:581
  125.7 4.1 %shard_map.156.w_ref = bf16[640,1152]{1,0:T(8,128)(2,1)} custom-call(bf16[160,256]{1,0:T(8,128)(2,1)} %constant.92.clone.rows_ref, bf16[1152,2560]{1,0:T(8,128)(2,1)} %all-gather.2.cloned.1.call-done.w_ref), custom_call_target="tpu_custom_call" | custom-call | flops 20000000000 | bytes 5980160 | tf_op jit(solution)/shard_map/pallas_call | solution.py:44
  129.8 3.0 %all-to-all-done.3.att_ref = bf16[4,72,640]{2,1,0:T(8,128)(2,1)S(1)} async-done(((bf16[4,72,640]{2,1,0:T(8,128)(2,1)}), bf16[4,72,640]{2,1,0:T(8,128)(2,1)S(1)}, u32[]{:S(2)}, u32[]{:S(2)}) %all-to-all-start.3) | async-done | bytes 368672 | tf_op jit(solution)/shard_map/all_to_all | solution.py:581
  132.8 0.7 copy-done.5
  133.5 3.7 %shard_map.157 = bf16[4,72,1152]{2,1,0:T(8,128)(2,1)} custom-call(s32[1]{0:T(128)} %bitcast.16.seq_ref, bf16[4,72,640]{2,1,0:T(8,128)(2,1)} %copy-done.5, bf16[4,16,72]{2,1,0:T(8,128)(2,1)} %copy-done.9, bf16[16,1152]{1,0:T(8,128)(2,1)} %wemb_ref.3, f32[32,1152]{1,0:T(8,128)} %get-tuple-element.45.ua_ref, f32[32,1152]{1,0:T(8,128)} %get-tuple-element.44.va_ref, ...), custom_call_target="tpu_custom_call" | custom-call | flops 1000000000 | bytes 2875396 | tf_op jit(solution)/shard_map/pallas_call | solution.py:44
  (28 shorter events, 0.1 us)
Async XLA Ops:
  7.2 87.3 %all-gather.2.cloned.1.call-start = ((), (), s32[]{:S(2)}) async-start(), calls=%async_computation.4 | async-start | bytes 6266880 | tf_op jit(solution)/shard_map/all_gather | solution.py:460
  10.2 9.3 %copy-start.12 = (s32[16]{0:T(128)S(1)}, s32[16]{0:T(128)}, u32[]{:S(2)}) copy-start(s32[16]{0:T(128)} %param.18) | copy-start | bytes 196
  10.2 13.2 %copy-start.11 = (f32[65]{0:T(128)S(1)}, f32[65]{0:T(128)}, u32[]{:S(2)}) copy-start(f32[65]{0:T(128)} %param.19) | copy-start | bytes 784
  10.2 18.5 %copy-start.6 = (bf16[16,1152]{1,0:T(8,128)(2,1)S(1)}, bf16[16,1152]{1,0:T(8,128)(2,1)}, u32[]{:S(2)}) copy-start(bf16[16,1152]{1,0:T(8,128)(2,1)} %wemb_ref.3) | copy-start | bytes 110596
  10.2 36.1 %all-to-all-start = ((bf16[16,72,720]{2,1,0:T(8,128)(2,1)}), bf16[16,72,720]{2,1,0:T(8,128)(2,1)S(1)}, u32[]{:S(2)}, u32[]{:S(2)}) async-start(bf16[16,72,720]{2,1,0:T(8,128)(2,1)} %get-tuple-element.21), calls=%async_computation | async-start | bytes 3538944 | tf_op jit(solution)/shard_map/all_to_all | solution.py:462
  33.2 12.2 %copy-start.7 = (bf16[16,1152]{1,0:T(8,128)(2,1)S(1)}, bf16[16,1152]{1,0:T(8,128)(2,1)}, u32[]{:S(2)}) copy-start(bf16[16,1152]{1,0:T(8,128)(2,1)} %wemb_ref.3) | copy-start | bytes 110596
  33.8 12.5 %copy-start.3 = (bf16[432,768]{1,0:T(8,128)(2,1)S(1)}, bf16[432,768]{1,0:T(8,128)(2,1)}, u32[]{:S(2)}) copy-start(bf16[432,768]{1,0:T(8,128)(2,1)} %constant.93.clone.pick_ref) | copy-start | bytes 1990660
  46.3 2.0 %copy-start.4 = (bf16[160,256]{1,0:T(8,128)(2,1)S(1)}, bf16[160,256]{1,0:T(8,128)(2,1)}, u32[]{:S(2)}) copy-start(bf16[160,256]{1,0:T(8,128)(2,1)} %constant.92.clone.rows_ref) | copy-start | bytes 245764
  48.4 17.9 %copy-start = (bf16[4,1,72,1152]{3,2,1,0:T(8,128)(2,1)S(1)}, bf16[4,1,72,1152]{3,2,1,0:T(8,128)(2,1)}, u32[]{:S(2)}) copy-start(bf16[4,1,72,1152]{3,2,1,0:T(8,128)(2,1)} %param.15) | copy-start | bytes 1990660
  48.4 17.9 %copy-start.1 = (bf16[1152,16]{0,1:T(8,128)(2,1)S(1)}, bf16[1152,16]{0,1:T(8,128)(2,1)}, u32[]{:S(2)}) copy-start(bf16[1152,16]{0,1:T(8,128)(2,1)} %param.22) | copy-start | bytes 110596
  48.4 17.9 %copy-start.2 = (bf16[4,1,72,16]{2,3,1,0:T(8,128)(2,1)S(1)}, bf16[4,1,72,16]{2,3,1,0:T(8,128)(2,1)}, u32[]{:S(2)}) copy-start(bf16[4,1,72,16]{2,3,1,0:T(8,128)(2,1)} %param.16) | copy-start | bytes 27652
  49.1 17.2 %collective-permute-start = (bf16[640,640]{1,0:T(8,128)(2,1)S(1)}, bf16[640,640]{1,0:T(8,128)(2,1)S(1)}, u32[]{:S(2)}, u32[]{:S(2)}) collective-permute-start(bf16[640,640]{1,0:T(8,128)(2,1)S(1)} %shard_map.152.mine_ref), channel_id=1, source_target_pairs={{0,1},{1,0},{2,3},{3,2},{4,5},{5,4},{6,7},{7,6},{8,9},{9,8},{10,11... | collective-permute-start | bytes 2457608 | tf_op jit(solution)/shard_map/ppermute | solution.py:515
  66.3 10.6 %copy-start.10 = (bf16[4,72,16]{1,2,0:T(8,128)(2,1)S(1)}, bf16[4,72,16]{1,2,0:T(8,128)(2,1)}, u32[]{:S(2)}) copy-start(bf16[4,72,16]{1,2,0:T(8,128)(2,1)} %param.17) | copy-start | bytes 27652
  68.8 8.1 %collective-permute-start.1 = (bf16[4,16,72]{2,1,0:T(8,128)(2,1)S(1)}, bf16[4,16,72]{2,1,0:T(8,128)(2,1)S(1)}, u32[]{:S(2)}, u32[]{:S(2)}) collective-permute-start(bf16[4,16,72]{2,1,0:T(8,128)(2,1)S(1)} %shard_map.153), channel_id=1, source_target_pairs={{32,0},{64,32},{96,64},{128,96},{160,128},{192,160},{224,192},{256... | collective-permute-start | bytes 27656 | tf_op jit(solution)/shard_map/ppermute | solution.py:535
  76.9 31.6 %copy-start.9 = (bf16[4,16,72]{2,1,0:T(8,128)(2,1)}, bf16[4,16,72]{2,1,0:T(8,128)(2,1)S(1)}, u32[]{:S(2)}) copy-start(bf16[4,16,72]{2,1,0:T(8,128)(2,1)S(1)} %broadcast_select_fusion.lat_ref) | copy-start | bytes 27652
  77.6 31.0 %all-to-all-start.2 = ((bf16[32,16,72]{2,1,0:T(8,128)(2,1)}), bf16[32,16,72]{2,1,0:T(8,128)(2,1)S(1)}, u32[]{:S(2)}, u32[]{:S(2)}) async-start(bf16[32,16,72]{2,1,0:T(8,128)(2,1)} %bitcast.18), calls=%async_computation.2 | async-start | bytes 262144 | tf_op jit(solution)/shard_map/all_to_all | solution.py:538
  108.6 0.6 copy-start.8
  122.2 10.6 %all-to-all-start.3 = ((bf16[4,72,640]{2,1,0:T(8,128)(2,1)}), bf16[4,72,640]{2,1,0:T(8,128)(2,1)S(1)}, u32[]{:S(2)}, u32[]{:S(2)}) async-start(bf16[4,72,640]{2,1,0:T(8,128)(2,1)} %shard_map.155), calls=%async_computation.3 | async-start | bytes 737280 | tf_op jit(solution)/shard_map/all_to_all | solution.py:581
  132.8 0.7 copy-start.5
Sparse Core Ops, SparseCore 0:
  11.1 83.4 all-gather.1

commit v6 on v5

--- a/solution.py
+++ b/solution.py
@@ -13,6 +13,7 @@
 HALF = HDIM // 2
 SLOT = 80
 PADDED = HEADS * SLOT
+DENSE = HEADS * HDIM
 SCORE_SCALE = 1.0 / math.sqrt(HDIM)
 LOG2E = math.log2(math.e)
 F32 = jnp.float32
@@ -99,16 +100,13 @@
 
     weights[1].wait()
     weights[2].wait()
-    blank = jnp.zeros((tokens, SLOT - HDIM), BF16)
-    for i, part in enumerate((1, 2, 0)):
-        pieces = []
+    pieces = []
+    for part in (1, 2, 0):
         for h in range(HEADS):
             at = HDIM * (3 * h + part)
-            pieces += [sqkv[:, at : at + HDIM], blank]
-        shard[:, PADDED * i : PADDED * (i + 1)] = jnp.concatenate(pieces, axis=-1)
+            pieces.append(sqkv[:, at : at + HDIM])
     ends = jnp.concatenate([sout[:, :half].astype(F32), sout[:, half:].astype(F32)], axis=0)
-    ends = jnp.concatenate([ends, jnp.zeros((tokens, PADDED - half), F32)], axis=-1)
-    shard[:, 3 * PADDED :] = ends.astype(BF16)
+    shard[...] = jnp.concatenate(pieces + [ends.astype(BF16)], axis=-1)
     last = pltpu.make_async_copy(shard, shard_ref, w_sem.at[3])
     last.start()
 
@@ -134,12 +132,12 @@
     return pick
 
 
-def weight_rows():
-    pick = np.zeros((2 * SLOT, 256), np.float32)
+def weight_rows(slot):
+    pick = np.zeros((2 * slot, 256), np.float32)
     for shard in range(2):
         for i in range(HALF):
             pick[HALF * shard + i, HDIM * shard + i] = 1.0
-            pick[SLOT + HALF * shard + i, HDIM * shard + HALF + i] = 1.0
+            pick[slot + HALF * shard + i, HDIM * shard + HALF + i] = 1.0
     return pick
 
 
@@ -245,7 +243,7 @@
     step = 2 * rows
     steps = made.shape[0] // step
 
-    edges = (0, 512, 2 * PADDED, 3 * PADDED)
+    edges = (0, 512, 2 * DENSE, 2 * DENSE + PADDED)
 
     def load_w(part):
         at = slice(edges[part], edges[part + 1])
@@ -271,14 +269,21 @@
             if i == 0:
                 load_w(part).wait()
             columns = slice(edges[part], edges[part + 1])
-            made[here, columns] = mm(p[here, :], w[:, columns]).astype(BF16)
+            if i + 1 < steps:
+                made[here, columns] = mm(p[here, :], w[:, columns]).astype(BF16)
+            else:
+                both = mm(jnp.concatenate([p[here, :], few_ref[...]], axis=0), w[:, columns])
+                made[here, columns] = both[:step].astype(BF16)
+                few = both[step:] if part == 0 else jnp.concatenate([few, both[step:]], axis=-1)
             if part == 0 and i + 1 < steps:
                 place(i + 1)
         store(i).start()
     load_w(2).wait()
     start = pl.multiple_of(group_ref[0] * rows, rows)
-    q_out[...] = mm(p[pl.ds(start, rows), :], w[:, 2 * PADDED :]).astype(BF16)
-    few = mm(few_ref[...], w[...])
+    own = jnp.concatenate([p[pl.ds(start, rows), :], few_ref[...]], axis=0)
+    own = mm(own, w[:, edges[2] :])
+    q_out[...] = own[:rows].astype(BF16)
+    few = jnp.concatenate([few, own[rows:]], axis=-1)
     patch = mix_out.shape[0] // 2
     mix = few[:patch] + few[patch : 2 * patch]
     high = mix.astype(BF16).astype(F32)
@@ -290,7 +295,7 @@
 
 def spatial_kernel(
     group_ref, lat_ref, gram_ref, sums_ref, mix_ref, offset_ref, pq_ref, pkv_ref,
-    o_ref, held, columns, keys, vals, sem,
+    o_ref, held, columns, kvs, sem,
 ):
     chunks, patch, tokens = lat_ref.shape
     members = o_ref.shape[0]
@@ -315,11 +320,10 @@
         rows = jnp.concatenate([twice, jnp.broadcast_to(scale, (8, tokens))], axis=0)
         columns[tokens * c : tokens * (c + 1), :] = rows.T
 
-    lane = lax.broadcasted_iota(jnp.int32, (1, PADDED), 1)
-    ones = jnp.where(lane % SLOT == HDIM, 1.0, 0.0)
-
-    kv_mix = mix_ref[:, : 2 * PADDED]
-    kv_offset = offset_ref[0:1, : 2 * PADDED] + jnp.concatenate([jnp.zeros_like(ones), ones], axis=-1)
+    lane = lax.broadcasted_iota(jnp.int32, (1, 2 * DENSE), 1)
+
+    kv_mix = mix_ref[:, : 2 * DENSE]
+    kv_offset = offset_ref[0:1, : 2 * DENSE]
 
     def one(index, carry):
         start = pl.multiple_of(index * block, block)
@@ -328,41 +332,40 @@
         mixed = mm(latent, kv_mix)
         fetch(index).wait()
         kv = (mixed + held[index].astype(F32)) * scale + kv_offset
-        keys[pl.ds(start, block), :] = kv[:, :PADDED].astype(BF16)
-        vals[pl.ds(start, block), :] = kv[:, PADDED:].astype(BF16)
+        kvs[pl.ds(start, block), :] = kv.astype(BF16)
         return carry
 
     lax.fori_loop(0, blocks, one, 0)
 
     column = columns[pl.ds(pl.multiple_of(group_ref[0] * block, block), block), :]
     latent, scale = column[:, : 2 * patch].astype(BF16), column[:, 2 * patch : 2 * patch + 1]
-    q_all = (mm(latent, mix_ref[:, 2 * PADDED :]) + pq_ref[...].astype(F32)) * scale + offset_ref[0:1, 2 * PADDED :]
+    q_all = (mm(latent, mix_ref[:, 2 * DENSE :]) + pq_ref[...].astype(F32)) * scale + offset_ref[0:1, 2 * DENSE :]
     q_all = q_all.astype(BF16).astype(F32)
     merged = [None] * (PADDED // 128)
 
-    def window(h):
-        first = SLOT * h // 128
-        last = (SLOT * h + HDIM) // 128
+    def window(at):
+        first, last = at // 128, (at + HDIM - 1) // 128
         here = slice(128 * first, 128 * (last + 1))
-        inside = (lane >= SLOT * h) & (lane < SLOT * h + HDIM)
+        inside = (lane >= at) & (lane < at + HDIM)
         return first, last, here, inside[:, here]
 
     def score(h):
-        _, _, here, inside = window(h)
-        return mm_nt(jnp.where(inside, q_all[:, here], 0.0).astype(BF16), keys[:, here])
+        _, _, here, inside = window(HDIM * h)
+        return mm_nt(jnp.where(inside, q_all[:, here], 0.0).astype(BF16), kvs[:, here])
 
     def weigh(scores):
         top = jnp.max(scores, axis=-1, keepdims=True)
-        return jnp.exp2((scores - top) * (SCORE_SCALE * LOG2E)).astype(BF16)
-
-    def blend(h, raised):
-        first, last, here, inside = window(h)
-        found = mm(raised, vals[:, here])
-        at = SLOT * h + HDIM - 128 * first
-        found = jnp.where(inside, found * (1.0 / found[:, at : at + 1]), 0.0)
+        raised = jnp.exp2((scores - top) * (SCORE_SCALE * LOG2E))
+        return raised.astype(BF16), jnp.sum(raised, axis=-1, keepdims=True)
+
+    def blend(h, weighed):
+        raised, total = weighed
+        first, last, here, inside = window(DENSE + HDIM * h)
+        found = jnp.where(inside, mm(raised, kvs[:, here]) * (1.0 / total), 0.0)
         for tile in range(first, last + 1):
             piece = found[:, 128 * (tile - first) : 128 * (tile - first + 1)]
-            merged[tile] = piece if merged[tile] is None else merged[tile] + piece
+            at = tile - DENSE // 128
+            merged[at] = piece if merged[at] is None else merged[at] + piece
 
     scores = score(0)
     raised = None
@@ -377,15 +380,16 @@
 
 
 def projection_kernel(rows_ref, w_ref, w_out, raw, sem):
-    copy = pltpu.make_async_copy(w_ref.at[:, 3 * PADDED :], raw, sem)
+    width = raw.shape[-1]
+    skip = width - w_out.shape[-1] // 2
+    copy = pltpu.make_async_copy(w_ref.at[:, w_ref.shape[-1] - width :], raw, sem)
     copy.start()
     copy.wait()
-    half = w_out.shape[-1] // 2
+    made = [jnp.zeros((skip, w_out.shape[-1]), F32)]
     for h in range(HEADS):
         both = mm(rows_ref[:, : 2 * HDIM], raw[2 * HDIM * h : 2 * HDIM * (h + 1), :])
-        w_out[SLOT * h : SLOT * (h + 1), :] = jnp.concatenate(
-            [both[:SLOT, :half], both[SLOT:, :half]], axis=-1
-        ).astype(BF16)
+        made.append(jnp.concatenate([both[:HDIM, skip:], both[HDIM:, skip:]], axis=-1))
+    w_out[...] = jnp.concatenate(made, axis=0).astype(BF16)
 
 
 def finish_kernel(
@@ -438,7 +442,7 @@
         pack_kernel,
         (
             jax.ShapeDtypeStruct((frames, tokens, sent), BF16),
-            jax.ShapeDtypeStruct((w_sqkv.shape[0], 4 * PADDED), BF16),
+            jax.ShapeDtypeStruct((w_sqkv.shape[0], 4 * DENSE), BF16),
         ),
         (core.reshape(1), t_qkv.reshape(videos, tokens, -1), w_tout, w_sqkv, w_sout),
         scratch=[
@@ -447,7 +451,7 @@
             pltpu.VMEM(w_sqkv.shape, BF16),
             pltpu.VMEM(w_sout.shape, BF16),
             pltpu.VMEM((frames, tokens, sent), BF16),
-            pltpu.VMEM((w_sqkv.shape[0], 4 * PADDED), BF16),
+            pltpu.VMEM((w_sqkv.shape[0], 4 * DENSE), BF16),
             pltpu.SemaphoreType.DMA((videos,)),
             pltpu.SemaphoreType.DMA((4,)),
             pltpu.SemaphoreType.DMA((videos,)),
@@ -460,7 +464,8 @@
     w_spatial = lax.all_gather(w_shard, "queue", axis=0, tiled=True)
 
     arrived = lax.all_to_all(packed, "queue", split_axis=0, concat_axis=0, tiled=True)
-    row_pick = jnp.asarray(weight_rows(), BF16)
+    row_pick = jnp.asarray(weight_rows(SLOT), BF16)
+    dense_pick = jnp.asarray(weight_rows(HDIM), BF16)
 
     level = lax.dynamic_index_in_dim(levels, queue_pos, 0, keepdims=False)
     following = lax.dynamic_index_in_dim(
@@ -543,16 +548,16 @@
     mix, offset, pq, pkv = call(
         prepare_kernel,
         (
-            jax.ShapeDtypeStruct((2 * w_embed.shape[0], 3 * PADDED), BF16),
-            jax.ShapeDtypeStruct((8, 3 * PADDED), F32),
+            jax.ShapeDtypeStruct((2 * w_embed.shape[0], 2 * DENSE + PADDED), BF16),
+            jax.ShapeDtypeStruct((8, 2 * DENSE + PADDED), F32),
             jax.ShapeDtypeStruct((own_rows, PADDED), BF16),
-            jax.ShapeDtypeStruct((rows, 2 * PADDED), BF16),
+            jax.ShapeDtypeStruct((rows, 2 * DENSE), BF16),
         ),
         (group, few, new_mods, ua, va, cb, sb, w_spatial),
         scratch=[
             pltpu.VMEM((rows, width), BF16),
-            pltpu.VMEM((width, 3 * PADDED), BF16),
-            pltpu.VMEM((rows, 2 * PADDED), BF16),
+            pltpu.VMEM((width, 2 * DENSE + PADDED), BF16),
+            pltpu.VMEM((rows, 2 * DENSE), BF16),
             pltpu.SemaphoreType.DMA((3,)),
             pltpu.SemaphoreType.DMA((4,)),
         ],
@@ -567,10 +572,9 @@
         jax.ShapeDtypeStruct((videos, tokens, PADDED), BF16),
         (group, everyone, gram, sums, mix, offset, pq, pkv),
         scratch=[
-            pltpu.VMEM((rows // own_rows, own_rows, 2 * PADDED), BF16),
+            pltpu.VMEM((rows // own_rows, own_rows, 2 * DENSE), BF16),
             pltpu.VMEM((rows, 2 * latents.shape[-1] + 8), F32),
-            pltpu.VMEM((rows, PADDED), BF16),
-            pltpu.VMEM((rows, PADDED), BF16),
+            pltpu.VMEM((rows, 2 * DENSE), BF16),
             pltpu.SemaphoreType.DMA((rows // own_rows,)),
         ],
         smem=(0,),
@@ -585,7 +589,7 @@
     w_s = call(
         projection_kernel,
         jax.ShapeDtypeStruct((PADDED, width), BF16),
-        (row_pick, late),
+        (dense_pick, late),
         scratch=[pltpu.VMEM((width, PADDED), BF16), pltpu.SemaphoreType.DMA],
         hbm=(1,),
         flops=20_000_000_000,
@@ -597,7 +601,6 @@
         (seq_pos.reshape(1), heads_out, queued, w_embed, ua, va, cb, sb, new_mods, w_s),
         smem=(0,),
         flops=1_000_000_000,
-        vmem=56,
     )
     return (
         queued.transpose(0, 2, 1).reshape(videos, 1, tokens, -1),

time: 146 us -> 144 us (0.986)
  Pallas kernels: 52.1 us -> 50.5 us
    all_gather x1, waiting for transfers between devices: 3.23 us -> 0.46 us  [shards(): w_spatial = lax.all_gather(w_shard, 'queue', axis=0, tiled=True)]
    all_to_all x1, waiting for transfers between devices: 0.01 us -> 2.52 us  [shards(): lax.all_to_all(jnp.tile(queued, (seqs // videos, 1, 1)), 'seq', split_axi...]
    pallas_call x9, Pallas kernels: 52.1 us -> 50.5 us  [call(): pl.pallas_call(kernel, out_shape=out_shape, in_specs=in_specs, out_specs=...]
  transfers between devices with their start and end apart: 6 -> 6, of which waited for: 3 -> 4; matrix products, arithmetic and copies ran while one was open for 8% -> 8% of each run, Pallas kernels for 23% -> 23%
where the time goes in v6:
time: 144 us; the launch traced here: 143 us
  Pallas kernels  50.5 us (35%)
  starting transfers between devices  31.5 us (22%)
  between operations  21.7 us (15%)
  blocking collectives  15.3 us (11%)
  waiting for transfers between devices  10.9 us (8%)
  local copies, waits for them, and re-layouts  8.17 us (6%)
  other arithmetic  4.64 us (3%)
    pallas_call x9, Pallas kernels, call(): pl.pallas_call(kernel, out_shape=out_shape, in_specs=in_specs, out_specs=...  50.5 us
    all_to_all x1, blocking collectives, shards(): lax.all_to_all(attended, 'queue', split_axis=0, concat_axis=0, tiled=True)  15.3 us
    all_to_all x1, starting transfers between devices, shards(): lax.all_to_all(jnp.tile(queued, (seqs // videos, 1, 1)), 'seq', split_axi...  13.7 us
    all_to_all x1, starting transfers between devices, shards(): lax.all_to_all(packed, 'queue', split_axis=0, concat_axis=0, tiled=True)  9.25 us
    ppermute x1, waiting for transfers between devices, shards(): lax.ppermute(stepped, 'queue', [(f, f - 1) for f in range(1, frames)])  4.96 us
    all_to_all x1, starting transfers between devices, shards(): lax.all_to_all(spatial, 'seq', split_axis=0, concat_axis=0, tiled=True, a...  3.47 us
    ppermute x1, starting transfers between devices, shards(): lax.ppermute(stepped, 'queue', [(f, f - 1) for f in range(1, frames)])  3.08 us
    all_to_all x1, waiting for transfers between devices, shards(): lax.all_to_all(spatial, 'seq', split_axis=0, concat_axis=0, tiled=True, a...  2.92 us
  transfers between devices with their start and end apart: 6, of which 4 were waited for; matrix products, arithmetic and copies ran while one was open for 8% of the time, Pallas kernels for 23%

profile of v6, /device:TPU:24, one launch (start us, length us, event | category | flops | bytes accessed | tf_op | source)
XLA Modules:
  0.0 142.9 jit_solution(11319875607594166519)
XLA Ops:
  7.2 0.0 all-gather.2.cloned.1.call-start
  7.2 3.0 %shard_map.158 = (bf16[16,72,720]{2,1,0:T(8,128)(2,1)}, bf16[72,2304]{1,0:T(8,128)(2,1)}) custom-call(s32[1]{0:T(128)} %bitcast.core_ref, bf16[4,72,1728]{2,1,0:T(8,128)(2,1)} %bitcast.39, bf16[36,1152]{1,0:T(8,128)(2,1)} %tout_ref.1, bf16[72,1728]{1,0:T(8,128)(2,1)} %sqkv_ref.1, bf16[36,1152]{1,0:T(8,128)(2,1)} %sout_ref.1), custom_call_target="tpu_custom_call" | custom-call | bytes 1410052 | tf_op jit(solution)/shard_map/pallas_call | solution.py:45
  10.2 0.0 all-gather.2.cloned.1.call-update
  10.2 0.0 copy-start.17
  10.2 0.0 copy-start.16
  10.2 0.0 copy-start.4
  10.3 9.3 %all-to-all-start = ((bf16[16,72,720]{2,1,0:T(8,128)(2,1)}), bf16[16,72,720]{2,1,0:T(8,128)(2,1)S(1)}, u32[]{:S(2)}, u32[]{:S(2)}) async-start(bf16[16,72,720]{2,1,0:T(8,128)(2,1)} %get-tuple-element.21), calls=%async_computation | async-start | bytes 3538944 | tf_op jit(solution)/shard_map/all_to_all | solution.py:466
  19.5 0.1 slice.13
  19.6 0.6 dynamic_slice.23
  23.4 0.6 fusion.14
  26.7 0.1 pad_add_fusion
  26.8 0.6 dynamic_slice.21
  28.7 0.1 convert_reduce_fusion
  28.9 1.0 constant_dynamic-slice_fusion
  29.9 0.6 fusion.12
  30.6 0.1 fusion.4
  30.7 2.5 %concatenate.28.few_ref = bf16[48,1152]{1,0:T(8,128)(2,1)} concatenate(bf16[16,1152]{1,0:T(8,128)(2,1)S(1)} %get-tuple-element.47, bf16[16,1152]{1,0:T(8,128)(2,1)S(1)} %get-tuple-element.46, bf16[1,1152]{1,0:T(2,128)(2,1)S(1)} %fusion.11, bf16[7,1152]{1,0:T(8,128)(2,1)S(1)} %broadcast_in_dim.2, bf16[1,1152]{1,0:T(2,128)(2,1)S(1)} %fusion.9, bf16[7,1152]{1,0:T(8,128)(2,1)S(1)} %broadcast_in_dim.2), dimensions={0} | concatenate | bytes 221184 | tf_op jit(solution)/shard_map/concatenate | solution.py:498
  33.2 0.7 fusion
  33.9 0.0 copy-start.11
  33.9 0.4 fusion.6
  34.3 0.8 pad_maximum_fusion.3
  35.1 1.1 pad_maximum_fusion
  36.2 9.1 %shard_map.159.sums_ref = f32[32,24,72]{2,1,0:T(8,128)} custom-call(bf16[16,1152]{1,0:T(8,128)(2,1)} %wemb_ref.3, f32[32,1152]{1,0:T(8,128)} %get-tuple-element.45.ua_ref, f32[32,1152]{1,0:T(8,128)} %get-tuple-element.44.va_ref, f32[72,1152]{1,0:T(8,128)} %get-tuple-element.59.cb_ref, f32[72,1152]{1,0:T(8,128)} %get-tuple-element.60.sb_ref), custom_call_target="tpu_custom_call" | custom-call | flops 100000000 | bytes 995328 | tf_op jit(solution)/shard_map/pallas_call | solution.py:45
  45.3 0.1 pad_maximum_fusion.5.coef_ref
  45.4 0.3 fusion.13
  45.7 0.7 pad_maximum_fusion.4.gram_ref
  46.4 0.0 copy-start.12
  46.4 2.0 %shard_map.160 = bf16[16,96,128]{2,1,0:T(8,128)(2,1)S(1)} custom-call(bf16[16,72,720]{2,1,0:T(8,128)(2,1)S(1)} %all-to-all-done.x_ref, bf16[432,768]{1,0:T(8,128)(2,1)S(1)} %copy-done.11), custom_call_target="tpu_custom_call" | custom-call | flops 4000000000 | bytes 2322432 | tf_op jit(solution)/shard_map/pallas_call | solution.py:45
  48.4 0.0 copy-start.8
  48.5 0.0 copy-start.9
  48.5 0.7 shard_map.161.mine_ref
  49.1 1.9 %collective-permute-start = (bf16[640,640]{1,0:T(8,128)(2,1)S(1)}, bf16[640,640]{1,0:T(8,128)(2,1)S(1)}, u32[]{:S(2)}, u32[]{:S(2)}) collective-permute-start(bf16[640,640]{1,0:T(8,128)(2,1)S(1)} %shard_map.161.mine_ref), channel_id=1, source_target_pairs={{0,1},{1,0},{2,3},{3,2},{4,5},{5,4},{6,7},{7,6},{8,9},{9,8},{10,11... | collective-permute-start | bytes 2457608 | tf_op jit(solution)/shard_map/ppermute | solution.py:520
  51.1 15.3 %all_to_all.20.att_ref = bf16[16,96,128]{2,1,0:T(8,128)(2,1)S(1)} all-to-all(bf16[16,96,128]{2,1,0:T(8,128)(2,1)S(1)} %shard_map.160), channel_id=1, replica_groups=mesh['queue'=16,'seq'=32] {'queue'}, dimensions={0} | all-to-all | bytes 786432 | tf_op jit(solution)/shard_map/all_to_all | solution.py:521
  66.4 2.6 %shard_map.162 = bf16[4,16,72]{2,1,0:T(8,128)(2,1)S(1)} custom-call(f32[4]{0:T(128)S(1)} %pad_maximum_fusion.5.coef_ref, s32[1]{0:T(128)} %bitcast.core_ref, bf16[16,96,128]{2,1,0:T(8,128)(2,1)S(1)} %all_to_all.20.att_ref, bf16[4,72,1152]{2,1,0:T(8,128)(2,1)S(1)} %bitcast.36, bf16[4,16,72]{2,1,0:T(8,128)(2,1)S(1)} %bitcast.38, ...), custom_call_target="tpu_custom_call" | custom-call | flops 1000000000 | bytes 2768916 | tf_op jit(solution)/shard_map/pallas_call | solution.py:45
  68.9 3.1 %collective-permute-start.1 = (bf16[4,16,72]{2,1,0:T(8,128)(2,1)S(1)}, bf16[4,16,72]{2,1,0:T(8,128)(2,1)S(1)}, u32[]{:S(2)}, u32[]{:S(2)}) collective-permute-start(bf16[4,16,72]{2,1,0:T(8,128)(2,1)S(1)} %shard_map.162), channel_id=1, source_target_pairs={{32,0},{64,32},{96,64},{128,96},{160,128},{192,160},{224,192},{256... | collective-permute-start | bytes 27656 | tf_op jit(solution)/shard_map/ppermute | solution.py:540
  72.0 5.0 %collective-permute-done.1 = bf16[4,16,72]{2,1,0:T(8,128)(2,1)S(1)} collective-permute-done((bf16[4,16,72]{2,1,0:T(8,128)(2,1)S(1)}, bf16[4,16,72]{2,1,0:T(8,128)(2,1)S(1)}, u32[]{:S(2)}, u32[]{:S(2)}) %collective-permute-start.1) | collective-permute-done | bytes 9248 | tf_op jit(solution)/shard_map/ppermute | solution.py:540
  77.0 0.7 tile.4
  77.7 13.7 %all-to-all-start.2 = ((bf16[32,16,72]{2,1,0:T(8,128)(2,1)}), bf16[32,16,72]{2,1,0:T(8,128)(2,1)S(1)}, u32[]{:S(2)}, u32[]{:S(2)}) async-start(bf16[32,16,72]{2,1,0:T(8,128)(2,1)} %bitcast.18), calls=%async_computation.2 | async-start | bytes 262144 | tf_op jit(solution)/shard_map/all_to_all | solution.py:543
  91.4 0.5 all-gather.2.cloned.1.call-done.w_ref
  91.9 14.0 %shard_map.163 = (bf16[32,1792]{1,0:T(8,128)(2,1)}, f32[8,1792]{1,0:T(8,128)}, bf16[288,640]{1,0:T(8,128)(2,1)}, bf16[2304,1152]{1,0:T(8,128)(2,1)}) custom-call(s32[1]{0:T(128)} %bitcast.17.group_ref, bf16[48,1152]{1,0:T(8,128)(2,1)} %concatenate.28.few_ref, f32[6,1152]{1,0:T(8,128)} %get-tuple-element.33.mod_ref, f32[32,1152]{1,0:T(8,128)} %get-tuple-element.45.ua_ref, ...), custom_call_target="tpu_custom_call" | custom-call | flops 8000000000 | bytes 6405124 | tf_op jit(solution)/shard_map/pallas_call | solution.py:45
  105.9 2.5 %all-to-all-done.2.lat_ref = bf16[32,16,72]{2,1,0:T(8,128)(2,1)S(1)} async-done(((bf16[32,16,72]{2,1,0:T(8,128)(2,1)}), bf16[32,16,72]{2,1,0:T(8,128)(2,1)S(1)}, u32[]{:S(2)}, u32[]{:S(2)}) %all-to-all-start.2) | async-done | bytes 73760 | tf_op jit(solution)/shard_map/all_to_all | solution.py:543
  108.4 0.6 copy-done.14
  109.1 13.1 %shard_map.164 = bf16[4,72,640]{2,1,0:T(8,128)(2,1)} custom-call(s32[1]{0:T(128)} %bitcast.17.group_ref, bf16[32,16,72]{2,1,0:T(8,128)(2,1)} %copy-done.14, bf16[16,32]{1,0:T(8,128)(2,1)} %pad_maximum_fusion.4.gram_ref, f32[32,24,72]{2,1,0:T(8,128)} %shard_map.159.sums_ref, bf16[32,1792]{1,0:T(8,128)(2,1)} %get-tuple-element.35.mix_ref, ...), custom_call_target="tpu_custom_call" | custom-call | flops 20000000000 | bytes 6145028 | tf_op jit(solution)/shard_map/pallas_call | solution.py:45
  122.2 3.5 %all-to-all-start.3 = ((bf16[4,72,640]{2,1,0:T(8,128)(2,1)}), bf16[4,72,640]{2,1,0:T(8,128)(2,1)S(1)}, u32[]{:S(2)}, u32[]{:S(2)}) async-start(bf16[4,72,640]{2,1,0:T(8,128)(2,1)} %shard_map.164), calls=%async_computation.3 | async-start | bytes 737280 | tf_op jit(solution)/shard_map/all_to_all | solution.py:585
  125.7 4.2 %shard_map.165.w_ref = bf16[640,1152]{1,0:T(8,128)(2,1)} custom-call(bf16[144,256]{1,0:T(8,128)(2,1)} %constant.95.clone.rows_ref, bf16[1152,2304]{1,0:T(8,128)(2,1)} %all-gather.2.cloned.1.call-done.w_ref), custom_call_target="tpu_custom_call" | custom-call | flops 20000000000 | bytes 5382144 | tf_op jit(solution)/shard_map/pallas_call | solution.py:45
  129.9 2.9 %all-to-all-done.3.att_ref = bf16[4,72,640]{2,1,0:T(8,128)(2,1)S(1)} async-done(((bf16[4,72,640]{2,1,0:T(8,128)(2,1)}), bf16[4,72,640]{2,1,0:T(8,128)(2,1)S(1)}, u32[]{:S(2)}, u32[]{:S(2)}) %all-to-all-start.3) | async-done | bytes 368672 | tf_op jit(solution)/shard_map/all_to_all | solution.py:585
  132.9 1.4 copy-done.13
  134.2 1.9 %shard_map.166 = bf16[4,72,1152]{2,1,0:T(8,128)(2,1)} custom-call(s32[1]{0:T(128)} %bitcast.16.seq_ref, bf16[4,72,640]{2,1,0:T(8,128)(2,1)S(1)} %all-to-all-done.3.att_ref, bf16[4,16,72]{2,1,0:T(8,128)(2,1)S(1)} %broadcast_select_fusion.lat_ref, bf16[16,1152]{1,0:T(8,128)(2,1)S(1)} %copy-done.5, f32[32,1152]{1,0:T(8,128)S(1)} %copy-done.3, ...), custom_call_target="tpu_custom_call" | custom-call | flops 1000000000 | bytes 2875396 | tf_op jit(solution)/shard_map/pallas_call | solution.py:45
  (38 shorter events, 0.1 us)
Async XLA Ops:
  7.2 84.7 %all-gather.2.cloned.1.call-start = ((), (), s32[]{:S(2)}) async-start(), calls=%async_computation.4 | async-start | bytes 5640192 | tf_op jit(solution)/shard_map/all_gather | solution.py:464
  10.2 9.3 %copy-start.17 = (s32[16]{0:T(128)S(1)}, s32[16]{0:T(128)}, u32[]{:S(2)}) copy-start(s32[16]{0:T(128)} %param.19) | copy-start | bytes 196
  10.2 13.2 %copy-start.16 = (f32[65]{0:T(128)S(1)}, f32[65]{0:T(128)}, u32[]{:S(2)}) copy-start(f32[65]{0:T(128)} %param.20) | copy-start | bytes 784
  10.2 18.5 %copy-start.4 = (bf16[16,1152]{1,0:T(8,128)(2,1)S(1)}, bf16[16,1152]{1,0:T(8,128)(2,1)}, u32[]{:S(2)}) copy-start(bf16[16,1152]{1,0:T(8,128)(2,1)} %wemb_ref.3) | copy-start | bytes 110596
  10.3 36.1 %all-to-all-start = ((bf16[16,72,720]{2,1,0:T(8,128)(2,1)}), bf16[16,72,720]{2,1,0:T(8,128)(2,1)S(1)}, u32[]{:S(2)}, u32[]{:S(2)}) async-start(bf16[16,72,720]{2,1,0:T(8,128)(2,1)} %get-tuple-element.21), calls=%async_computation | async-start | bytes 3538944 | tf_op jit(solution)/shard_map/all_to_all | solution.py:466
  33.2 12.2 %copy-start.5 = (bf16[16,1152]{1,0:T(8,128)(2,1)S(1)}, bf16[16,1152]{1,0:T(8,128)(2,1)}, u32[]{:S(2)}) copy-start(bf16[16,1152]{1,0:T(8,128)(2,1)} %wemb_ref.3) | copy-start | bytes 110596
  33.9 12.5 %copy-start.11 = (bf16[432,768]{1,0:T(8,128)(2,1)S(1)}, bf16[432,768]{1,0:T(8,128)(2,1)}, u32[]{:S(2)}) copy-start(bf16[432,768]{1,0:T(8,128)(2,1)} %constant.96.clone.pick_ref) | copy-start | bytes 1990660
  46.4 2.0 %copy-start.12 = (bf16[160,256]{1,0:T(8,128)(2,1)S(1)}, bf16[160,256]{1,0:T(8,128)(2,1)}, u32[]{:S(2)}) copy-start(bf16[160,256]{1,0:T(8,128)(2,1)} %constant.94.clone.rows_ref) | copy-start | bytes 245764
  48.4 17.9 %copy-start.8 = (bf16[4,1,72,1152]{3,2,1,0:T(8,128)(2,1)S(1)}, bf16[4,1,72,1152]{3,2,1,0:T(8,128)(2,1)}, u32[]{:S(2)}) copy-start(bf16[4,1,72,1152]{3,2,1,0:T(8,128)(2,1)} %param.16) | copy-start | bytes 1990660
  48.5 17.9 %copy-start.9 = (bf16[1152,16]{0,1:T(8,128)(2,1)S(1)}, bf16[1152,16]{0,1:T(8,128)(2,1)}, u32[]{:S(2)}) copy-start(bf16[1152,16]{0,1:T(8,128)(2,1)} %param.23) | copy-start | bytes 110596
  48.5 17.9 %copy-start.10 = (bf16[4,1,72,16]{2,3,1,0:T(8,128)(2,1)S(1)}, bf16[4,1,72,16]{2,3,1,0:T(8,128)(2,1)}, u32[]{:S(2)}) copy-start(bf16[4,1,72,16]{2,3,1,0:T(8,128)(2,1)} %param.17) | copy-start | bytes 27652
  49.1 17.2 %collective-permute-start = (bf16[640,640]{1,0:T(8,128)(2,1)S(1)}, bf16[640,640]{1,0:T(8,128)(2,1)S(1)}, u32[]{:S(2)}, u32[]{:S(2)}) collective-permute-start(bf16[640,640]{1,0:T(8,128)(2,1)S(1)} %shard_map.161.mine_ref), channel_id=1, source_target_pairs={{0,1},{1,0},{2,3},{3,2},{4,5},{5,4},{6,7},{7,6},{8,9},{9,8},{10,11... | collective-permute-start | bytes 2457608 | tf_op jit(solution)/shard_map/ppermute | solution.py:520
  66.4 10.6 %copy-start.15 = (bf16[4,72,16]{1,2,0:T(8,128)(2,1)S(1)}, bf16[4,72,16]{1,2,0:T(8,128)(2,1)}, u32[]{:S(2)}) copy-start(bf16[4,72,16]{1,2,0:T(8,128)(2,1)} %param.18) | copy-start | bytes 27652
  68.9 8.1 %collective-permute-start.1 = (bf16[4,16,72]{2,1,0:T(8,128)(2,1)S(1)}, bf16[4,16,72]{2,1,0:T(8,128)(2,1)S(1)}, u32[]{:S(2)}, u32[]{:S(2)}) collective-permute-start(bf16[4,16,72]{2,1,0:T(8,128)(2,1)S(1)} %shard_map.162), channel_id=1, source_target_pairs={{32,0},{64,32},{96,64},{128,96},{160,128},{192,160},{224,192},{256... | collective-permute-start | bytes 27656 | tf_op jit(solution)/shard_map/ppermute | solution.py:540
  77.0 55.8 %copy-start.6 = (bf16[4,16,72]{2,1,0:T(8,128)(2,1)}, bf16[4,16,72]{2,1,0:T(8,128)(2,1)S(1)}, u32[]{:S(2)}) copy-start(bf16[4,16,72]{2,1,0:T(8,128)(2,1)S(1)} %broadcast_select_fusion.lat_ref) | copy-start | bytes 27652
  77.7 30.7 %all-to-all-start.2 = ((bf16[32,16,72]{2,1,0:T(8,128)(2,1)}), bf16[32,16,72]{2,1,0:T(8,128)(2,1)S(1)}, u32[]{:S(2)}, u32[]{:S(2)}) async-start(bf16[32,16,72]{2,1,0:T(8,128)(2,1)} %bitcast.18), calls=%async_computation.2 | async-start | bytes 262144 | tf_op jit(solution)/shard_map/all_to_all | solution.py:543
  108.4 0.7 copy-start.14
  122.2 10.6 %all-to-all-start.3 = ((bf16[4,72,640]{2,1,0:T(8,128)(2,1)}), bf16[4,72,640]{2,1,0:T(8,128)(2,1)S(1)}, u32[]{:S(2)}, u32[]{:S(2)}) async-start(bf16[4,72,640]{2,1,0:T(8,128)(2,1)} %shard_map.164), calls=%async_computation.3 | async-start | bytes 737280 | tf_op jit(solution)/shard_map/all_to_all | solution.py:585
  125.7 7.1 %copy-start = (f32[72,1152]{1,0:T(8,128)S(1)}, f32[72,1152]{1,0:T(8,128)}, u32[]{:S(2)}) copy-start(f32[72,1152]{1,0:T(8,128)} %get-tuple-element.59.cb_ref) | copy-start | bytes 995332
  125.7 7.1 %copy-start.1 = (f32[72,1152]{1,0:T(8,128)S(1)}, f32[72,1152]{1,0:T(8,128)}, u32[]{:S(2)}) copy-start(f32[72,1152]{1,0:T(8,128)} %get-tuple-element.60.sb_ref) | copy-start | bytes 995332
  125.7 7.1 %copy-start.2 = (f32[32,1152]{1,0:T(8,128)S(1)}, f32[32,1152]{1,0:T(8,128)}, u32[]{:S(2)}) copy-start(f32[32,1152]{1,0:T(8,128)} %get-tuple-element.44.va_ref) | copy-start | bytes 442372
  125.7 7.1 %copy-start.3 = (f32[32,1152]{1,0:T(8,128)S(1)}, f32[32,1152]{1,0:T(8,128)}, u32[]{:S(2)}) copy-start(f32[32,1152]{1,0:T(8,128)} %get-tuple-element.45.ua_ref) | copy-start | bytes 442372
  125.7 7.1 %copy-start.7 = (f32[6,1152]{1,0:T(8,128)S(1)}, f32[6,1152]{1,0:T(8,128)}, u32[]{:S(2)}) copy-start(f32[6,1152]{1,0:T(8,128)} %get-tuple-element.33.mod_ref) | copy-start | bytes 82948
  132.9 1.4 copy-start.13
Sparse Core Ops, SparseCore 0:
  11.1 80.7 all-gather.1

commit v7 on v6

--- a/solution.py
+++ b/solution.py
@@ -185,7 +185,9 @@
         ).astype(BF16)
 
 
-def step_kernel(coef_ref, core_ref, att_ref, hid_ref, lat_ref, mine_ref, other_ref, wf_ref, mod_ref, o_ref):
+def step_kernel(
+    coef_ref, place_ref, att_ref, hid_ref, lat_ref, fresh_ref, mine_ref, other_ref, wf_ref, mod_ref, o_ref
+):
     videos, tokens, width = hid_ref.shape
     rows = videos * tokens
     pairs = att_ref.shape[0] // videos
@@ -199,7 +201,7 @@
         own_term, far_term = mm(part, mine_ref[at, :]), mm(part, other_ref[at, :])
         own = own_term if own is None else own + own_term
         far = far_term if far is None else far + far_term
-    low = core_ref[0] == 0
+    low = place_ref[0] == 0
     half = width // 2
     proj = jnp.concatenate([jnp.where(low, own, far)[:, :half], jnp.where(low, far, own)[:, :half]], axis=-1)
     residual = hid_ref[...].astype(F32).reshape(rows, width) + mod_ref[0:1, :] * proj
@@ -208,7 +210,18 @@
     for v in range(videos):
         pred = predicted[:, tokens * v : tokens * (v + 1)]
         clean = (lat_ref[v].astype(F32) - coef_ref[0] * pred) * coef_ref[1]
-        o_ref[v] = (coef_ref[2] * clean + coef_ref[3] * pred).astype(BF16)
+        stepped = coef_ref[2] * clean + coef_ref[3] * pred
+        o_ref[v] = jnp.where(place_ref[1] == 0, fresh_ref[v].astype(F32), stepped).astype(BF16)
+
+
+def arrange_kernel(core_ref, own_ref, cross_ref, o_ref):
+    first = core_ref[0] == 0
+    for parity in range(2):
+        own = jnp.where(first, own_ref[2 * parity].astype(F32), own_ref[2 * parity + 1].astype(F32))
+        cross = jnp.where(first, cross_ref[2 * parity].astype(F32), cross_ref[2 * parity + 1].astype(F32))
+        pair = jnp.concatenate([jnp.where(first, own, cross), jnp.where(first, cross, own)], axis=0)
+        for z in range(parity, o_ref.shape[0], 2):
+            o_ref[z] = pair.astype(BF16)
 
 
 def centered_place(c, ua_ref, va_ref, cb_ref, sb_ref):
@@ -525,10 +538,11 @@
         jax.ShapeDtypeStruct((videos, latents.shape[-1], tokens), BF16),
         (
             coef,
-            core.reshape(1),
+            jnp.stack([core, queue_pos]),
             returned,
             hidden.reshape(videos, tokens, width),
             latents_t,
+            fresh_t,
             w_mine,
             w_other,
             w_final_t,
@@ -537,12 +551,23 @@
         smem=(0, 1),
         flops=1_000_000_000,
     )
-    arriving = lax.ppermute(stepped, "queue", [(f, f - 1) for f in range(1, frames)])
-    queued = jnp.where(queue_pos == frames - 1, fresh_t, arriving)
-
+    behind = [(f - 1) % frames for f in range(frames)]
+    queued = lax.ppermute(stepped, "queue", list(enumerate(behind)))
+    cross = [(f * seqs + i, behind[f] * seqs + (i ^ 1)) for f in range(frames) for i in range(seqs)]
+    queued_cross = lax.ppermute(stepped, ("queue", "seq"), cross)
+
+    chips = seqs // 2
+    patch = latents.shape[-1]
+    sent_latents = call(
+        arrange_kernel,
+        jax.ShapeDtypeStruct((chips, 2 * patch, tokens), BF16),
+        (core.reshape(1), queued, queued_cross),
+        smem=(0,),
+    )
+    same_core = [[2 * z + i for z in range(chips)] for i in range(2)]
     everyone = lax.all_to_all(
-        jnp.tile(queued, (seqs // videos, 1, 1)), "seq", split_axis=0, concat_axis=0, tiled=True
-    )
+        sent_latents, "seq", split_axis=0, concat_axis=0, tiled=True, axis_index_groups=same_core
+    ).reshape(seqs, patch, tokens)
     groups = [[videos * g + i for i in range(videos)] for g in range(seqs // videos)]
     group = (seq_pos // videos).reshape(1)
     mix, offset, pq, pkv = call(

time: 144 us -> 146 us (1.014)
  blocking collectives: 15.3 us -> 0 us
  starting transfers between devices: 31.5 us -> 40.2 us
  waiting for transfers between devices: 10.9 us -> 16.6 us
  Pallas kernels: 50.5 us -> 52.1 us
    all_to_all x1 -> x0, blocking collectives: 15.3 us -> none  [shards(): lax.all_to_all(attended, 'queue', split_axis=0, concat_axis=0, tiled=True)]
    all_to_all x1 -> x2, starting transfers between devices: 13.7 us -> 20.5 us  [the longest x1 13.2 us: shards(): lax.all_to_all(sent_latents, 'seq', split_axis=0, concat_axis=0, tiled=Tr...]
    all_to_all x1 -> x2, waiting for transfers between devices: 2.52 us -> 8.13 us  [the longest x1 8.13 us: shards(): lax.all_to_all(attended, 'queue', split_axis=0, concat_axis=0, tiled=True)]
    ppermute x1 -> x2, starting transfers between devices: 3.08 us -> 5 us  [the longest x1 3.08 us: shards(): queued = lax.ppermute(stepped, 'queue', list(enumerate(behind)))]
    pallas_call x9 -> x10, Pallas kernels: 50.5 us -> 52.1 us  [call(): pl.pallas_call(kernel, out_shape=out_shape, in_specs=in_specs, out_specs=...]
    ppermute x1 -> x2, waiting for transfers between devices: 4.96 us -> 5.55 us  [the longest x1 3.04 us: shards(): queued = lax.ppermute(stepped, 'queue', list(enumerate(behind)))]
  transfers between devices with their start and end apart: 6 -> 8, of which waited for: 4 -> 4; matrix products, arithmetic and copies ran while one was open for 8% -> 7% of each run, Pallas kernels for 23% -> 24%
where the time goes in v7:
time: 146 us; the launch traced here: 144 us
  Pallas kernels  52.1 us (36%)
  starting transfers between devices  40.2 us (28%)
  between operations  21.7 us (15%)
  waiting for transfers between devices  16.6 us (11%)
  local copies, waits for them, and re-layouts  8.08 us (6%)
  other arithmetic  4.69 us (3%)
    pallas_call x10, Pallas kernels, call(): pl.pallas_call(kernel, out_shape=out_shape, in_specs=in_specs, out_specs=...  52.1 us
    all_to_all x1, starting transfers between devices, shards(): lax.all_to_all(sent_latents, 'seq', split_axis=0, concat_axis=0, tiled=Tr...  13.2 us
    all_to_all x1, starting transfers between devices, shards(): lax.all_to_all(packed, 'queue', split_axis=0, concat_axis=0, tiled=True)  9.25 us
    all_to_all x1, waiting for transfers between devices, shards(): lax.all_to_all(attended, 'queue', split_axis=0, concat_axis=0, tiled=True)  8.13 us
    all_to_all x1, starting transfers between devices, shards(): lax.all_to_all(attended, 'queue', split_axis=0, concat_axis=0, tiled=True)  7.3 us
    all_to_all x1, starting transfers between devices, shards(): lax.all_to_all(spatial, 'seq', split_axis=0, concat_axis=0, tiled=True, a...  3.47 us
    ppermute x1, starting transfers between devices, shards(): queued = lax.ppermute(stepped, 'queue', list(enumerate(behind)))  3.08 us
    ppermute x1, waiting for transfers between devices, shards(): queued = lax.ppermute(stepped, 'queue', list(enumerate(behind)))  3.04 us
  transfers between devices with their start and end apart: 8, of which 4 were waited for; matrix products, arithmetic and copies ran while one was open for 7% of the time, Pallas kernels for 24%

profile of v7, /device:TPU:24, one launch (start us, length us, event | category | flops | bytes accessed | tf_op | source)
XLA Modules:
  0.0 143.7 jit_solution(6278099871640727372)
XLA Ops:
  7.2 0.0 all-gather.2.cloned.1.call-start
  7.2 3.0 %shard_map.158 = (bf16[16,72,720]{2,1,0:T(8,128)(2,1)}, bf16[72,2304]{1,0:T(8,128)(2,1)}) custom-call(s32[1]{0:T(128)} %bitcast.core_ref, bf16[4,72,1728]{2,1,0:T(8,128)(2,1)} %bitcast.41, bf16[36,1152]{1,0:T(8,128)(2,1)} %tout_ref.1, bf16[72,1728]{1,0:T(8,128)(2,1)} %sqkv_ref.1, bf16[36,1152]{1,0:T(8,128)(2,1)} %sout_ref.1), custom_call_target="tpu_custom_call" | custom-call | bytes 1410052 | tf_op jit(solution)/shard_map/pallas_call | solution.py:45
  10.3 0.0 all-gather.2.cloned.1.call-update
  10.3 0.0 copy-start.16
  10.3 9.3 %all-to-all-start = ((bf16[16,72,720]{2,1,0:T(8,128)(2,1)}), bf16[16,72,720]{2,1,0:T(8,128)(2,1)S(1)}, u32[]{:S(2)}, u32[]{:S(2)}) async-start(bf16[16,72,720]{2,1,0:T(8,128)(2,1)} %get-tuple-element.21), calls=%async_computation | async-start | bytes 3538944 | tf_op jit(solution)/shard_map/all_to_all | solution.py:479
  19.6 0.1 slice.13
  19.7 0.6 dynamic_slice.23
  23.5 0.6 fusion.14
  26.8 0.1 pad_add_fusion
  26.8 0.6 dynamic_slice.21
  28.8 0.1 convert_reduce_fusion
  28.9 1.0 constant_dynamic-slice_fusion
  30.0 0.6 fusion.12
  30.7 0.1 fusion.4
  30.8 2.5 %concatenate.28.few_ref = bf16[48,1152]{1,0:T(8,128)(2,1)} concatenate(bf16[16,1152]{1,0:T(8,128)(2,1)S(1)} %get-tuple-element.47, bf16[16,1152]{1,0:T(8,128)(2,1)S(1)} %get-tuple-element.46, bf16[1,1152]{1,0:T(2,128)(2,1)S(1)} %fusion.11, bf16[7,1152]{1,0:T(8,128)(2,1)S(1)} %broadcast_in_dim.2, bf16[1,1152]{1,0:T(2,128)(2,1)S(1)} %fusion.9, bf16[7,1152]{1,0:T(8,128)(2,1)S(1)} %broadcast_in_dim.2), dimensions={0} | concatenate | bytes 221184 | tf_op jit(solution)/shard_map/concatenate | solution.py:511
  33.3 0.7 fusion
  34.0 0.0 copy-start.11
  34.0 0.4 fusion.6
  34.3 0.8 pad_maximum_fusion.3
  35.2 1.0 pad_maximum_fusion
  36.2 9.1 %shard_map.159.sums_ref = f32[32,24,72]{2,1,0:T(8,128)} custom-call(bf16[16,1152]{1,0:T(8,128)(2,1)} %wemb_ref.3, f32[32,1152]{1,0:T(8,128)} %get-tuple-element.45.ua_ref, f32[32,1152]{1,0:T(8,128)} %get-tuple-element.44.va_ref, f32[72,1152]{1,0:T(8,128)} %get-tuple-element.59.cb_ref, f32[72,1152]{1,0:T(8,128)} %get-tuple-element.60.sb_ref), custom_call_target="tpu_custom_call" | custom-call | flops 100000000 | bytes 995328 | tf_op jit(solution)/shard_map/pallas_call | solution.py:45
  45.4 0.1 pad_maximum_fusion.5.coef_ref
  45.4 0.3 fusion.13
  45.7 0.7 pad_maximum_fusion.4.gram_ref
  46.4 0.0 copy-start.12
  46.4 2.8 %shard_map.160 = bf16[16,96,128]{2,1,0:T(8,128)(2,1)} custom-call(bf16[16,72,720]{2,1,0:T(8,128)(2,1)S(1)} %all-to-all-done.x_ref, bf16[432,768]{1,0:T(8,128)(2,1)S(1)} %copy-done.11), custom_call_target="tpu_custom_call" | custom-call | flops 4000000000 | bytes 2322432 | tf_op jit(solution)/shard_map/pallas_call | solution.py:45
  49.2 0.7 shard_map.161.mine_ref
  49.9 1.9 %collective-permute-start = (bf16[640,640]{1,0:T(8,128)(2,1)S(1)}, bf16[640,640]{1,0:T(8,128)(2,1)S(1)}, u32[]{:S(2)}, u32[]{:S(2)}) collective-permute-start(bf16[640,640]{1,0:T(8,128)(2,1)S(1)} %shard_map.161.mine_ref), channel_id=1, source_target_pairs={{0,1},{1,0},{2,3},{3,2},{4,5},{5,4},{6,7},{7,6},{8,9},{9,8},{10,11... | collective-permute-start | bytes 2457608 | tf_op jit(solution)/shard_map/ppermute | solution.py:533
  51.8 7.3 %all-to-all-start.1 = ((bf16[16,96,128]{2,1,0:T(8,128)(2,1)}), bf16[16,96,128]{2,1,0:T(8,128)(2,1)S(1)}, u32[]{:S(2)}, u32[]{:S(2)}) async-start(bf16[16,96,128]{2,1,0:T(8,128)(2,1)} %shard_map.160), calls=%async_computation.1 | async-start | bytes 786432 | tf_op jit(solution)/shard_map/all_to_all | solution.py:534
  59.1 0.1 pad_add_fusion.1.place_ref
  59.2 8.1 %all-to-all-done.1.att_ref = bf16[16,96,128]{2,1,0:T(8,128)(2,1)S(1)} async-done(((bf16[16,96,128]{2,1,0:T(8,128)(2,1)}), bf16[16,96,128]{2,1,0:T(8,128)(2,1)S(1)}, u32[]{:S(2)}, u32[]{:S(2)}) %all-to-all-start.1) | async-done | bytes 393248 | tf_op jit(solution)/shard_map/all_to_all | solution.py:534
  67.4 2.6 %shard_map.162 = bf16[4,16,72]{2,1,0:T(8,128)(2,1)S(1)} custom-call(f32[4]{0:T(128)S(1)} %pad_maximum_fusion.5.coef_ref, s32[2]{0:T(128)S(1)} %pad_add_fusion.1.place_ref, bf16[16,96,128]{2,1,0:T(8,128)(2,1)S(1)} %all-to-all-done.1.att_ref, bf16[4,72,1152]{2,1,0:T(8,128)(2,1)S(1)} %bitcast.37, bf16[4,16,72]{2,1,0:T(8,128)(2,1)S(1)} %bitcast.39, ...), custom_call_target="tpu_custom_call" | custom-call | flops 1000000000 | bytes 2778136 | tf_op jit(solution)/shard_map/pallas_call | solution.py:45
  70.0 3.1 %collective-permute-start.1 = (bf16[4,16,72]{2,1,0:T(8,128)(2,1)S(1)}, bf16[4,16,72]{2,1,0:T(8,128)(2,1)S(1)}, u32[]{:S(2)}, u32[]{:S(2)}) collective-permute-start(bf16[4,16,72]{2,1,0:T(8,128)(2,1)S(1)} %shard_map.162), channel_id=1, source_target_pairs={{0,480},{32,0},{64,32},{96,64},{128,96},{160,128},{192,160},{224,1... | collective-permute-start | bytes 27656 | tf_op jit(solution)/shard_map/ppermute | solution.py:555
  73.1 1.9 %collective-permute-start.2 = (bf16[4,16,72]{2,1,0:T(8,128)(2,1)S(1)}, bf16[4,16,72]{2,1,0:T(8,128)(2,1)S(1)}, u32[]{:S(2)}, u32[]{:S(2)}) collective-permute-start(bf16[4,16,72]{2,1,0:T(8,128)(2,1)S(1)} %shard_map.162), channel_id=1, source_target_pairs={{0,481},{1,480},{2,483},{3,482},{4,485},{5,484},{6,487},{7,486},{8... | collective-permute-start | bytes 27656 | tf_op jit(solution)/shard_map/ppermute | solution.py:557
  75.0 3.0 %collective-permute-done.1.own_ref.lat_ref = bf16[4,16,72]{2,1,0:T(8,128)(2,1)S(1)} collective-permute-done((bf16[4,16,72]{2,1,0:T(8,128)(2,1)S(1)}, bf16[4,16,72]{2,1,0:T(8,128)(2,1)S(1)}, u32[]{:S(2)}, u32[]{:S(2)}) %collective-permute-start.1) | collective-permute-done | bytes 9248 | tf_op jit(solution)/shard_map/ppermute | solution.py:555
  78.0 2.5 %collective-permute-done.2.cross_ref = bf16[4,16,72]{2,1,0:T(8,128)(2,1)S(1)} collective-permute-done((bf16[4,16,72]{2,1,0:T(8,128)(2,1)S(1)}, bf16[4,16,72]{2,1,0:T(8,128)(2,1)S(1)}, u32[]{:S(2)}, u32[]{:S(2)}) %collective-permute-start.2) | collective-permute-done | bytes 9248 | tf_op jit(solution)/shard_map/ppermute | solution.py:557
  80.6 0.7 shard_map.163
  81.2 13.2 %all-to-all-start.2 = ((bf16[16,32,72]{2,1,0:T(8,128)(2,1)}), bf16[16,32,72]{2,1,0:T(8,128)(2,1)S(1)}, u32[]{:S(2)}, u32[]{:S(2)}) async-start(bf16[16,32,72]{2,1,0:T(8,128)(2,1)} %shard_map.163), calls=%async_computation.2 | async-start | bytes 262144 | tf_op jit(solution)/shard_map/all_to_all | solution.py:568
  94.5 0.0 all-gather.2.cloned.1.call-done.w_ref
  94.5 14.0 %shard_map.164 = (bf16[32,1792]{1,0:T(8,128)(2,1)}, f32[8,1792]{1,0:T(8,128)}, bf16[288,640]{1,0:T(8,128)(2,1)}, bf16[2304,1152]{1,0:T(8,128)(2,1)}) custom-call(s32[1]{0:T(128)} %bitcast.18.group_ref, bf16[48,1152]{1,0:T(8,128)(2,1)} %concatenate.28.few_ref, f32[6,1152]{1,0:T(8,128)} %get-tuple-element.33.mod_ref, f32[32,1152]{1,0:T(8,128)} %get-tuple-element.45.ua_ref, ...), custom_call_target="tpu_custom_call" | custom-call | flops 8000000000 | bytes 6405124 | tf_op jit(solution)/shard_map/pallas_call | solution.py:45
  108.6 0.6 copy-done.14
  109.2 13.1 %shard_map.165 = bf16[4,72,640]{2,1,0:T(8,128)(2,1)} custom-call(s32[1]{0:T(128)} %bitcast.18.group_ref, bf16[32,16,72]{2,1,0:T(8,128)(2,1)} %bitcast.42, bf16[16,32]{1,0:T(8,128)(2,1)} %pad_maximum_fusion.4.gram_ref, f32[32,24,72]{2,1,0:T(8,128)} %shard_map.159.sums_ref, bf16[32,1792]{1,0:T(8,128)(2,1)} %get-tuple-element.35.mix_ref, ...), custom_call_target="tpu_custom_call" | custom-call | flops 20000000000 | bytes 6145028 | tf_op jit(solution)/shard_map/pallas_call | solution.py:45
  122.3 3.5 %all-to-all-start.3 = ((bf16[4,72,640]{2,1,0:T(8,128)(2,1)}), bf16[4,72,640]{2,1,0:T(8,128)(2,1)S(1)}, u32[]{:S(2)}, u32[]{:S(2)}) async-start(bf16[4,72,640]{2,1,0:T(8,128)(2,1)} %shard_map.165), calls=%async_computation.3 | async-start | bytes 737280 | tf_op jit(solution)/shard_map/all_to_all | solution.py:610
  125.8 4.2 %shard_map.166.w_ref = bf16[640,1152]{1,0:T(8,128)(2,1)} custom-call(bf16[144,256]{1,0:T(8,128)(2,1)} %constant.93.clone.rows_ref, bf16[1152,2304]{1,0:T(8,128)(2,1)} %all-gather.2.cloned.1.call-done.w_ref), custom_call_target="tpu_custom_call" | custom-call | flops 20000000000 | bytes 5382144 | tf_op jit(solution)/shard_map/pallas_call | solution.py:45
  130.0 2.9 %all-to-all-done.3.att_ref = bf16[4,72,640]{2,1,0:T(8,128)(2,1)S(1)} async-done(((bf16[4,72,640]{2,1,0:T(8,128)(2,1)}), bf16[4,72,640]{2,1,0:T(8,128)(2,1)S(1)}, u32[]{:S(2)}, u32[]{:S(2)}) %all-to-all-start.3) | async-done | bytes 368672 | tf_op jit(solution)/shard_map/all_to_all | solution.py:610
  133.0 1.4 copy-done.13
  134.3 1.9 %shard_map.167 = bf16[4,72,1152]{2,1,0:T(8,128)(2,1)} custom-call(s32[1]{0:T(128)} %bitcast.17.seq_ref, bf16[4,72,640]{2,1,0:T(8,128)(2,1)S(1)} %all-to-all-done.3.att_ref, bf16[4,16,72]{2,1,0:T(8,128)(2,1)S(1)} %collective-permute-done.1.own_ref.lat_ref, bf16[16,1152]{1,0:T(8,128)(2,1)S(1)} %copy-done.5, f32[32,1152]{1,0:T(8,128)S(1)} %copy-done.3, ...), custom_call_target="tpu_custom_call" | custom-call | flops 1000000000 | bytes 2875396 | tf_op jit(solution)/shard_map/pallas_call | solution.py:45
  136.2 0.6 copy.30
  (40 shorter events, 0.1 us)
Async XLA Ops:
  7.2 87.3 %all-gather.2.cloned.1.call-start = ((), (), s32[]{:S(2)}) async-start(), calls=%async_computation.4 | async-start | bytes 5640192 | tf_op jit(solution)/shard_map/all_gather | solution.py:477
  10.3 9.3 %copy-start.16 = (s32[16]{0:T(128)S(1)}, s32[16]{0:T(128)}, u32[]{:S(2)}) copy-start(s32[16]{0:T(128)} %param.19) | copy-start | bytes 196
  10.3 13.2 %copy-start.15 = (f32[65]{0:T(128)S(1)}, f32[65]{0:T(128)}, u32[]{:S(2)}) copy-start(f32[65]{0:T(128)} %param.20) | copy-start | bytes 784
  10.3 18.5 %copy-start.4 = (bf16[16,1152]{1,0:T(8,128)(2,1)S(1)}, bf16[16,1152]{1,0:T(8,128)(2,1)}, u32[]{:S(2)}) copy-start(bf16[16,1152]{1,0:T(8,128)(2,1)} %wemb_ref.3) | copy-start | bytes 110596
  10.3 36.1 %all-to-all-start = ((bf16[16,72,720]{2,1,0:T(8,128)(2,1)}), bf16[16,72,720]{2,1,0:T(8,128)(2,1)S(1)}, u32[]{:S(2)}, u32[]{:S(2)}) async-start(bf16[16,72,720]{2,1,0:T(8,128)(2,1)} %get-tuple-element.21), calls=%async_computation | async-start | bytes 3538944 | tf_op jit(solution)/shard_map/all_to_all | solution.py:479
  33.3 12.2 %copy-start.5 = (bf16[16,1152]{1,0:T(8,128)(2,1)S(1)}, bf16[16,1152]{1,0:T(8,128)(2,1)}, u32[]{:S(2)}) copy-start(bf16[16,1152]{1,0:T(8,128)(2,1)} %wemb_ref.3) | copy-start | bytes 110596
  34.0 12.5 %copy-start.11 = (bf16[432,768]{1,0:T(8,128)(2,1)S(1)}, bf16[432,768]{1,0:T(8,128)(2,1)}, u32[]{:S(2)}) copy-start(bf16[432,768]{1,0:T(8,128)(2,1)} %constant.94.clone.pick_ref) | copy-start | bytes 1990660
  46.4 2.8 %copy-start.12 = (bf16[160,256]{1,0:T(8,128)(2,1)S(1)}, bf16[160,256]{1,0:T(8,128)(2,1)}, u32[]{:S(2)}) copy-start(bf16[160,256]{1,0:T(8,128)(2,1)} %constant.92.clone.rows_ref) | copy-start | bytes 245764
  49.2 18.1 %copy-start.7 = (bf16[4,1,72,1152]{3,2,1,0:T(8,128)(2,1)S(1)}, bf16[4,1,72,1152]{3,2,1,0:T(8,128)(2,1)}, u32[]{:S(2)}) copy-start(bf16[4,1,72,1152]{3,2,1,0:T(8,128)(2,1)} %param.16) | copy-start | bytes 1990660
  49.2 18.1 %copy-start.8 = (bf16[1152,16]{0,1:T(8,128)(2,1)S(1)}, bf16[1152,16]{0,1:T(8,128)(2,1)}, u32[]{:S(2)}) copy-start(bf16[1152,16]{0,1:T(8,128)(2,1)} %param.23) | copy-start | bytes 110596
  49.2 18.1 %copy-start.9 = (bf16[4,1,72,16]{2,3,1,0:T(8,128)(2,1)S(1)}, bf16[4,1,72,16]{2,3,1,0:T(8,128)(2,1)}, u32[]{:S(2)}) copy-start(bf16[4,1,72,16]{2,3,1,0:T(8,128)(2,1)} %param.17) | copy-start | bytes 27652
  49.2 18.1 %copy-start.10 = (bf16[4,72,16]{1,2,0:T(8,128)(2,1)S(1)}, bf16[4,72,16]{1,2,0:T(8,128)(2,1)}, u32[]{:S(2)}) copy-start(bf16[4,72,16]{1,2,0:T(8,128)(2,1)} %param.18) | copy-start | bytes 27652
  49.9 17.4 %collective-permute-start = (bf16[640,640]{1,0:T(8,128)(2,1)S(1)}, bf16[640,640]{1,0:T(8,128)(2,1)S(1)}, u32[]{:S(2)}, u32[]{:S(2)}) collective-permute-start(bf16[640,640]{1,0:T(8,128)(2,1)S(1)} %shard_map.161.mine_ref), channel_id=1, source_target_pairs={{0,1},{1,0},{2,3},{3,2},{4,5},{5,4},{6,7},{7,6},{8,9},{9,8},{10,11... | collective-permute-start | bytes 2457608 | tf_op jit(solution)/shard_map/ppermute | solution.py:533
  51.8 15.5 %all-to-all-start.1 = ((bf16[16,96,128]{2,1,0:T(8,128)(2,1)}), bf16[16,96,128]{2,1,0:T(8,128)(2,1)S(1)}, u32[]{:S(2)}, u32[]{:S(2)}) async-start(bf16[16,96,128]{2,1,0:T(8,128)(2,1)} %shard_map.160), calls=%async_computation.1 | async-start | bytes 786432 | tf_op jit(solution)/shard_map/all_to_all | solution.py:534
  70.0 8.1 %collective-permute-start.1 = (bf16[4,16,72]{2,1,0:T(8,128)(2,1)S(1)}, bf16[4,16,72]{2,1,0:T(8,128)(2,1)S(1)}, u32[]{:S(2)}, u32[]{:S(2)}) collective-permute-start(bf16[4,16,72]{2,1,0:T(8,128)(2,1)S(1)} %shard_map.162), channel_id=1, source_target_pairs={{0,480},{32,0},{64,32},{96,64},{128,96},{160,128},{192,160},{224,1... | collective-permute-start | bytes 27656 | tf_op jit(solution)/shard_map/ppermute | solution.py:555
  73.1 7.5 %collective-permute-start.2 = (bf16[4,16,72]{2,1,0:T(8,128)(2,1)S(1)}, bf16[4,16,72]{2,1,0:T(8,128)(2,1)S(1)}, u32[]{:S(2)}, u32[]{:S(2)}) collective-permute-start(bf16[4,16,72]{2,1,0:T(8,128)(2,1)S(1)} %shard_map.162), channel_id=1, source_target_pairs={{0,481},{1,480},{2,483},{3,482},{4,485},{5,484},{6,487},{7,486},{8... | collective-permute-start | bytes 27656 | tf_op jit(solution)/shard_map/ppermute | solution.py:557
  81.2 27.3 %all-to-all-start.2 = ((bf16[16,32,72]{2,1,0:T(8,128)(2,1)}), bf16[16,32,72]{2,1,0:T(8,128)(2,1)S(1)}, u32[]{:S(2)}, u32[]{:S(2)}) async-start(bf16[16,32,72]{2,1,0:T(8,128)(2,1)} %shard_map.163), calls=%async_computation.2 | async-start | bytes 262144 | tf_op jit(solution)/shard_map/all_to_all | solution.py:568
  108.5 0.7 copy-start.14
  122.3 10.6 %all-to-all-start.3 = ((bf16[4,72,640]{2,1,0:T(8,128)(2,1)}), bf16[4,72,640]{2,1,0:T(8,128)(2,1)S(1)}, u32[]{:S(2)}, u32[]{:S(2)}) async-start(bf16[4,72,640]{2,1,0:T(8,128)(2,1)} %shard_map.165), calls=%async_computation.3 | async-start | bytes 737280 | tf_op jit(solution)/shard_map/all_to_all | solution.py:610
  125.8 7.1 %copy-start = (f32[72,1152]{1,0:T(8,128)S(1)}, f32[72,1152]{1,0:T(8,128)}, u32[]{:S(2)}) copy-start(f32[72,1152]{1,0:T(8,128)} %get-tuple-element.59.cb_ref) | copy-start | bytes 995332
  125.8 7.1 %copy-start.1 = (f32[72,1152]{1,0:T(8,128)S(1)}, f32[72,1152]{1,0:T(8,128)}, u32[]{:S(2)}) copy-start(f32[72,1152]{1,0:T(8,128)} %get-tuple-element.60.sb_ref) | copy-start | bytes 995332
  125.8 7.1 %copy-start.2 = (f32[32,1152]{1,0:T(8,128)S(1)}, f32[32,1152]{1,0:T(8,128)}, u32[]{:S(2)}) copy-start(f32[32,1152]{1,0:T(8,128)} %get-tuple-element.44.va_ref) | copy-start | bytes 442372
  125.8 7.1 %copy-start.3 = (f32[32,1152]{1,0:T(8,128)S(1)}, f32[32,1152]{1,0:T(8,128)}, u32[]{:S(2)}) copy-start(f32[32,1152]{1,0:T(8,128)} %get-tuple-element.45.ua_ref) | copy-start | bytes 442372
  125.8 7.1 %copy-start.6 = (f32[6,1152]{1,0:T(8,128)S(1)}, f32[6,1152]{1,0:T(8,128)}, u32[]{:S(2)}) copy-start(f32[6,1152]{1,0:T(8,128)} %get-tuple-element.33.mod_ref) | copy-start | bytes 82948
  133.0 1.4 copy-start.13
Sparse Core Ops, SparseCore 0:
  11.1 80.9 all-gather.1

commit v8 on v6

--- a/solution.py
+++ b/solution.py
@@ -221,8 +221,8 @@
     blank = jnp.zeros((tokens, 7), F32)
 
     def one(few, carry):
-        for i in range(4):
-            c = 4 * few + i
+        for i in range(8):
+            c = 8 * few + i
             center = centered_place(c, ua_ref, va_ref, cb_ref, sb_ref)
             high = center.astype(BF16)
             low = (center - high.astype(F32)).astype(BF16)
@@ -231,7 +231,7 @@
             sums_ref[c] = jnp.concatenate([cross, square, blank], axis=-1).T
         return carry
 
-    lax.fori_loop(0, sums_ref.shape[0] // 4, one, 0)
+    lax.fori_loop(0, sums_ref.shape[0] // 8, one, 0)
 
 
 def prepare_kernel(

time: 144 us -> 144 us (level)
  no operation moved by 1% of the time
where the time goes in v8:
time: 144 us; the launch traced here: 143 us
  Pallas kernels  50.1 us (35%)
  starting transfers between devices  31.4 us (22%)
  between operations  21.7 us (15%)
  blocking collectives  15.3 us (11%)
  waiting for transfers between devices  10.9 us (8%)
  local copies, waits for them, and re-layouts  8.15 us (6%)
  other arithmetic  4.64 us (3%)
    pallas_call x9, Pallas kernels, call(): pl.pallas_call(kernel, out_shape=out_shape, in_specs=in_specs, out_specs=...  50.1 us
    all_to_all x1, blocking collectives, shards(): lax.all_to_all(attended, 'queue', split_axis=0, concat_axis=0, tiled=True)  15.3 us
    all_to_all x1, starting transfers between devices, shards(): lax.all_to_all(jnp.tile(queued, (seqs // videos, 1, 1)), 'seq', split_axi...  13.7 us
    all_to_all x1, starting transfers between devices, shards(): lax.all_to_all(packed, 'queue', split_axis=0, concat_axis=0, tiled=True)  9.25 us
    ppermute x1, waiting for transfers between devices, shards(): lax.ppermute(stepped, 'queue', [(f, f - 1) for f in range(1, frames)])  4.96 us
    all_to_all x1, starting transfers between devices, shards(): lax.all_to_all(spatial, 'seq', split_axis=0, concat_axis=0, tiled=True, a...  3.47 us
    ppermute x1, starting transfers between devices, shards(): lax.ppermute(stepped, 'queue', [(f, f - 1) for f in range(1, frames)])  3.08 us
    all_to_all x1, waiting for transfers between devices, shards(): lax.all_to_all(spatial, 'seq', split_axis=0, concat_axis=0, tiled=True, a...  2.92 us
  transfers between devices with their start and end apart: 6, of which 4 were waited for; matrix products, arithmetic and copies ran while one was open for 8% of the time, Pallas kernels for 23%

profile of v8, /device:TPU:24, one launch (start us, length us, event | category | flops | bytes accessed | tf_op | source)
XLA Modules:
  0.0 142.5 jit_solution(5082870420816719475)
XLA Ops:
  7.2 0.0 all-gather.2.cloned.1.call-start
  7.2 3.0 %shard_map.158 = (bf16[16,72,720]{2,1,0:T(8,128)(2,1)}, bf16[72,2304]{1,0:T(8,128)(2,1)}) custom-call(s32[1]{0:T(128)} %bitcast.core_ref, bf16[4,72,1728]{2,1,0:T(8,128)(2,1)} %bitcast.39, bf16[36,1152]{1,0:T(8,128)(2,1)} %tout_ref.1, bf16[72,1728]{1,0:T(8,128)(2,1)} %sqkv_ref.1, bf16[36,1152]{1,0:T(8,128)(2,1)} %sout_ref.1), custom_call_target="tpu_custom_call" | custom-call | bytes 1410052 | tf_op jit(solution)/shard_map/pallas_call | solution.py:45
  10.2 0.0 all-gather.2.cloned.1.call-update
  10.2 0.0 copy-start.16
  10.2 0.0 copy-start.4
  10.3 9.3 %all-to-all-start = ((bf16[16,72,720]{2,1,0:T(8,128)(2,1)}), bf16[16,72,720]{2,1,0:T(8,128)(2,1)S(1)}, u32[]{:S(2)}, u32[]{:S(2)}) async-start(bf16[16,72,720]{2,1,0:T(8,128)(2,1)} %get-tuple-element.21), calls=%async_computation | async-start | bytes 3538944 | tf_op jit(solution)/shard_map/all_to_all | solution.py:466
  19.5 0.1 slice.13
  19.6 0.6 dynamic_slice.23
  23.4 0.6 fusion.14
  26.7 0.1 pad_add_fusion
  26.8 0.6 dynamic_slice.21
  28.7 0.1 convert_reduce_fusion
  28.9 1.0 constant_dynamic-slice_fusion
  29.9 0.6 fusion.12
  30.6 0.1 fusion.4
  30.7 2.5 %concatenate.28.few_ref = bf16[48,1152]{1,0:T(8,128)(2,1)} concatenate(bf16[16,1152]{1,0:T(8,128)(2,1)S(1)} %get-tuple-element.47, bf16[16,1152]{1,0:T(8,128)(2,1)S(1)} %get-tuple-element.46, bf16[1,1152]{1,0:T(2,128)(2,1)S(1)} %fusion.11, bf16[7,1152]{1,0:T(8,128)(2,1)S(1)} %broadcast_in_dim.2, bf16[1,1152]{1,0:T(2,128)(2,1)S(1)} %fusion.9, bf16[7,1152]{1,0:T(8,128)(2,1)S(1)} %broadcast_in_dim.2), dimensions={0} | concatenate | bytes 221184 | tf_op jit(solution)/shard_map/concatenate | solution.py:498
  33.2 0.7 fusion
  33.9 0.0 copy-start.11
  33.9 0.4 fusion.6
  34.3 0.8 pad_maximum_fusion.3
  35.1 1.1 pad_maximum_fusion
  36.2 8.8 %shard_map.159.sums_ref = f32[32,24,72]{2,1,0:T(8,128)} custom-call(bf16[16,1152]{1,0:T(8,128)(2,1)} %wemb_ref.3, f32[32,1152]{1,0:T(8,128)} %get-tuple-element.45.ua_ref, f32[32,1152]{1,0:T(8,128)} %get-tuple-element.44.va_ref, f32[72,1152]{1,0:T(8,128)} %get-tuple-element.59.cb_ref, f32[72,1152]{1,0:T(8,128)} %get-tuple-element.60.sb_ref), custom_call_target="tpu_custom_call" | custom-call | flops 100000000 | bytes 995328 | tf_op jit(solution)/shard_map/pallas_call | solution.py:45
  44.9 0.1 pad_maximum_fusion.5.coef_ref
  45.0 0.3 fusion.13
  45.3 0.7 pad_maximum_fusion.4.gram_ref
  46.0 0.0 copy-start.12
  46.0 2.0 %shard_map.160 = bf16[16,96,128]{2,1,0:T(8,128)(2,1)S(1)} custom-call(bf16[16,72,720]{2,1,0:T(8,128)(2,1)S(1)} %all-to-all-done.x_ref, bf16[432,768]{1,0:T(8,128)(2,1)S(1)} %copy-done.11), custom_call_target="tpu_custom_call" | custom-call | flops 4000000000 | bytes 2322432 | tf_op jit(solution)/shard_map/pallas_call | solution.py:45
  48.0 0.0 copy-start.8
  48.0 0.0 copy-start.9
  48.1 0.7 shard_map.161.mine_ref
  48.7 1.9 %collective-permute-start = (bf16[640,640]{1,0:T(8,128)(2,1)S(1)}, bf16[640,640]{1,0:T(8,128)(2,1)S(1)}, u32[]{:S(2)}, u32[]{:S(2)}) collective-permute-start(bf16[640,640]{1,0:T(8,128)(2,1)S(1)} %shard_map.161.mine_ref), channel_id=1, source_target_pairs={{0,1},{1,0},{2,3},{3,2},{4,5},{5,4},{6,7},{7,6},{8,9},{9,8},{10,11... | collective-permute-start | bytes 2457608 | tf_op jit(solution)/shard_map/ppermute | solution.py:520
  50.7 15.3 %all_to_all.20.att_ref = bf16[16,96,128]{2,1,0:T(8,128)(2,1)S(1)} all-to-all(bf16[16,96,128]{2,1,0:T(8,128)(2,1)S(1)} %shard_map.160), channel_id=1, replica_groups=mesh['queue'=16,'seq'=32] {'queue'}, dimensions={0} | all-to-all | bytes 786432 | tf_op jit(solution)/shard_map/all_to_all | solution.py:521
  66.0 2.6 %shard_map.162 = bf16[4,16,72]{2,1,0:T(8,128)(2,1)S(1)} custom-call(f32[4]{0:T(128)S(1)} %pad_maximum_fusion.5.coef_ref, s32[1]{0:T(128)} %bitcast.core_ref, bf16[16,96,128]{2,1,0:T(8,128)(2,1)S(1)} %all_to_all.20.att_ref, bf16[4,72,1152]{2,1,0:T(8,128)(2,1)S(1)} %bitcast.36, bf16[4,16,72]{2,1,0:T(8,128)(2,1)S(1)} %bitcast.38, ...), custom_call_target="tpu_custom_call" | custom-call | flops 1000000000 | bytes 2768916 | tf_op jit(solution)/shard_map/pallas_call | solution.py:45
  68.5 3.1 %collective-permute-start.1 = (bf16[4,16,72]{2,1,0:T(8,128)(2,1)S(1)}, bf16[4,16,72]{2,1,0:T(8,128)(2,1)S(1)}, u32[]{:S(2)}, u32[]{:S(2)}) collective-permute-start(bf16[4,16,72]{2,1,0:T(8,128)(2,1)S(1)} %shard_map.162), channel_id=1, source_target_pairs={{32,0},{64,32},{96,64},{128,96},{160,128},{192,160},{224,192},{256... | collective-permute-start | bytes 27656 | tf_op jit(solution)/shard_map/ppermute | solution.py:540
  71.6 5.0 %collective-permute-done.1 = bf16[4,16,72]{2,1,0:T(8,128)(2,1)S(1)} collective-permute-done((bf16[4,16,72]{2,1,0:T(8,128)(2,1)S(1)}, bf16[4,16,72]{2,1,0:T(8,128)(2,1)S(1)}, u32[]{:S(2)}, u32[]{:S(2)}) %collective-permute-start.1) | collective-permute-done | bytes 9248 | tf_op jit(solution)/shard_map/ppermute | solution.py:540
  76.6 0.0 copy-start.6
  76.6 0.7 tile.4
  77.3 13.7 %all-to-all-start.2 = ((bf16[32,16,72]{2,1,0:T(8,128)(2,1)}), bf16[32,16,72]{2,1,0:T(8,128)(2,1)S(1)}, u32[]{:S(2)}, u32[]{:S(2)}) async-start(bf16[32,16,72]{2,1,0:T(8,128)(2,1)} %bitcast.18), calls=%async_computation.2 | async-start | bytes 262144 | tf_op jit(solution)/shard_map/all_to_all | solution.py:543
  91.0 0.9 all-gather.2.cloned.1.call-done.w_ref
  91.9 14.0 %shard_map.163 = (bf16[32,1792]{1,0:T(8,128)(2,1)}, f32[8,1792]{1,0:T(8,128)}, bf16[288,640]{1,0:T(8,128)(2,1)}, bf16[2304,1152]{1,0:T(8,128)(2,1)}) custom-call(s32[1]{0:T(128)} %bitcast.17.group_ref, bf16[48,1152]{1,0:T(8,128)(2,1)} %concatenate.28.few_ref, f32[6,1152]{1,0:T(8,128)} %get-tuple-element.33.mod_ref, f32[32,1152]{1,0:T(8,128)} %get-tuple-element.45.ua_ref, ...), custom_call_target="tpu_custom_call" | custom-call | flops 8000000000 | bytes 6405124 | tf_op jit(solution)/shard_map/pallas_call | solution.py:45
  105.9 2.1 %all-to-all-done.2.lat_ref = bf16[32,16,72]{2,1,0:T(8,128)(2,1)S(1)} async-done(((bf16[32,16,72]{2,1,0:T(8,128)(2,1)}), bf16[32,16,72]{2,1,0:T(8,128)(2,1)S(1)}, u32[]{:S(2)}, u32[]{:S(2)}) %all-to-all-start.2) | async-done | bytes 73760 | tf_op jit(solution)/shard_map/all_to_all | solution.py:543
  108.0 0.6 copy-done.14
  108.7 13.1 %shard_map.164 = bf16[4,72,640]{2,1,0:T(8,128)(2,1)} custom-call(s32[1]{0:T(128)} %bitcast.17.group_ref, bf16[32,16,72]{2,1,0:T(8,128)(2,1)} %copy-done.14, bf16[16,32]{1,0:T(8,128)(2,1)} %pad_maximum_fusion.4.gram_ref, f32[32,24,72]{2,1,0:T(8,128)} %shard_map.159.sums_ref, bf16[32,1792]{1,0:T(8,128)(2,1)} %get-tuple-element.35.mix_ref, ...), custom_call_target="tpu_custom_call" | custom-call | flops 20000000000 | bytes 6145028 | tf_op jit(solution)/shard_map/pallas_call | solution.py:45
  121.8 3.5 %all-to-all-start.3 = ((bf16[4,72,640]{2,1,0:T(8,128)(2,1)}), bf16[4,72,640]{2,1,0:T(8,128)(2,1)S(1)}, u32[]{:S(2)}, u32[]{:S(2)}) async-start(bf16[4,72,640]{2,1,0:T(8,128)(2,1)} %shard_map.164), calls=%async_computation.3 | async-start | bytes 737280 | tf_op jit(solution)/shard_map/all_to_all | solution.py:585
  125.3 4.2 %shard_map.165.w_ref = bf16[640,1152]{1,0:T(8,128)(2,1)} custom-call(bf16[144,256]{1,0:T(8,128)(2,1)} %constant.95.clone.rows_ref, bf16[1152,2304]{1,0:T(8,128)(2,1)} %all-gather.2.cloned.1.call-done.w_ref), custom_call_target="tpu_custom_call" | custom-call | flops 20000000000 | bytes 5382144 | tf_op jit(solution)/shard_map/pallas_call | solution.py:45
  129.5 2.9 %all-to-all-done.3.att_ref = bf16[4,72,640]{2,1,0:T(8,128)(2,1)S(1)} async-done(((bf16[4,72,640]{2,1,0:T(8,128)(2,1)}), bf16[4,72,640]{2,1,0:T(8,128)(2,1)S(1)}, u32[]{:S(2)}, u32[]{:S(2)}) %all-to-all-start.3) | async-done | bytes 368672 | tf_op jit(solution)/shard_map/all_to_all | solution.py:585
  132.5 1.4 copy-done.13
  133.8 1.9 %shard_map.166 = bf16[4,72,1152]{2,1,0:T(8,128)(2,1)} custom-call(s32[1]{0:T(128)} %bitcast.16.seq_ref, bf16[4,72,640]{2,1,0:T(8,128)(2,1)S(1)} %all-to-all-done.3.att_ref, bf16[4,16,72]{2,1,0:T(8,128)(2,1)S(1)} %broadcast_select_fusion.lat_ref, bf16[16,1152]{1,0:T(8,128)(2,1)S(1)} %copy-done.5, f32[32,1152]{1,0:T(8,128)S(1)} %copy-done.3, ...), custom_call_target="tpu_custom_call" | custom-call | flops 1000000000 | bytes 2875396 | tf_op jit(solution)/shard_map/pallas_call | solution.py:45
  (38 shorter events, 0.1 us)
Async XLA Ops:
  7.2 84.7 %all-gather.2.cloned.1.call-start = ((), (), s32[]{:S(2)}) async-start(), calls=%async_computation.4 | async-start | bytes 5640192 | tf_op jit(solution)/shard_map/all_gather | solution.py:464
  10.2 9.3 %copy-start.17 = (s32[16]{0:T(128)S(1)}, s32[16]{0:T(128)}, u32[]{:S(2)}) copy-start(s32[16]{0:T(128)} %param.19) | copy-start | bytes 196
  10.2 13.2 %copy-start.16 = (f32[65]{0:T(128)S(1)}, f32[65]{0:T(128)}, u32[]{:S(2)}) copy-start(f32[65]{0:T(128)} %param.20) | copy-start | bytes 784
  10.2 18.5 %copy-start.4 = (bf16[16,1152]{1,0:T(8,128)(2,1)S(1)}, bf16[16,1152]{1,0:T(8,128)(2,1)}, u32[]{:S(2)}) copy-start(bf16[16,1152]{1,0:T(8,128)(2,1)} %wemb_ref.3) | copy-start | bytes 110596
  10.3 35.7 %all-to-all-start = ((bf16[16,72,720]{2,1,0:T(8,128)(2,1)}), bf16[16,72,720]{2,1,0:T(8,128)(2,1)S(1)}, u32[]{:S(2)}, u32[]{:S(2)}) async-start(bf16[16,72,720]{2,1,0:T(8,128)(2,1)} %get-tuple-element.21), calls=%async_computation | async-start | bytes 3538944 | tf_op jit(solution)/shard_map/all_to_all | solution.py:466
  33.2 11.8 %copy-start.5 = (bf16[16,1152]{1,0:T(8,128)(2,1)S(1)}, bf16[16,1152]{1,0:T(8,128)(2,1)}, u32[]{:S(2)}) copy-start(bf16[16,1152]{1,0:T(8,128)(2,1)} %wemb_ref.3) | copy-start | bytes 110596
  33.9 12.1 %copy-start.11 = (bf16[432,768]{1,0:T(8,128)(2,1)S(1)}, bf16[432,768]{1,0:T(8,128)(2,1)}, u32[]{:S(2)}) copy-start(bf16[432,768]{1,0:T(8,128)(2,1)} %constant.96.clone.pick_ref) | copy-start | bytes 1990660
  46.0 2.0 %copy-start.12 = (bf16[160,256]{1,0:T(8,128)(2,1)S(1)}, bf16[160,256]{1,0:T(8,128)(2,1)}, u32[]{:S(2)}) copy-start(bf16[160,256]{1,0:T(8,128)(2,1)} %constant.94.clone.rows_ref) | copy-start | bytes 245764
  48.0 17.9 %copy-start.8 = (bf16[4,1,72,1152]{3,2,1,0:T(8,128)(2,1)S(1)}, bf16[4,1,72,1152]{3,2,1,0:T(8,128)(2,1)}, u32[]{:S(2)}) copy-start(bf16[4,1,72,1152]{3,2,1,0:T(8,128)(2,1)} %param.16) | copy-start | bytes 1990660
  48.0 17.9 %copy-start.9 = (bf16[1152,16]{0,1:T(8,128)(2,1)S(1)}, bf16[1152,16]{0,1:T(8,128)(2,1)}, u32[]{:S(2)}) copy-start(bf16[1152,16]{0,1:T(8,128)(2,1)} %param.23) | copy-start | bytes 110596
  48.1 17.9 %copy-start.10 = (bf16[4,1,72,16]{2,3,1,0:T(8,128)(2,1)S(1)}, bf16[4,1,72,16]{2,3,1,0:T(8,128)(2,1)}, u32[]{:S(2)}) copy-start(bf16[4,1,72,16]{2,3,1,0:T(8,128)(2,1)} %param.17) | copy-start | bytes 27652
  48.7 17.2 %collective-permute-start = (bf16[640,640]{1,0:T(8,128)(2,1)S(1)}, bf16[640,640]{1,0:T(8,128)(2,1)S(1)}, u32[]{:S(2)}, u32[]{:S(2)}) collective-permute-start(bf16[640,640]{1,0:T(8,128)(2,1)S(1)} %shard_map.161.mine_ref), channel_id=1, source_target_pairs={{0,1},{1,0},{2,3},{3,2},{4,5},{5,4},{6,7},{7,6},{8,9},{9,8},{10,11... | collective-permute-start | bytes 2457608 | tf_op jit(solution)/shard_map/ppermute | solution.py:520
  66.0 10.6 %copy-start.15 = (bf16[4,72,16]{1,2,0:T(8,128)(2,1)S(1)}, bf16[4,72,16]{1,2,0:T(8,128)(2,1)}, u32[]{:S(2)}) copy-start(bf16[4,72,16]{1,2,0:T(8,128)(2,1)} %param.18) | copy-start | bytes 27652
  68.5 8.1 %collective-permute-start.1 = (bf16[4,16,72]{2,1,0:T(8,128)(2,1)S(1)}, bf16[4,16,72]{2,1,0:T(8,128)(2,1)S(1)}, u32[]{:S(2)}, u32[]{:S(2)}) collective-permute-start(bf16[4,16,72]{2,1,0:T(8,128)(2,1)S(1)} %shard_map.162), channel_id=1, source_target_pairs={{32,0},{64,32},{96,64},{128,96},{160,128},{192,160},{224,192},{256... | collective-permute-start | bytes 27656 | tf_op jit(solution)/shard_map/ppermute | solution.py:540
  76.6 55.8 %copy-start.6 = (bf16[4,16,72]{2,1,0:T(8,128)(2,1)}, bf16[4,16,72]{2,1,0:T(8,128)(2,1)S(1)}, u32[]{:S(2)}) copy-start(bf16[4,16,72]{2,1,0:T(8,128)(2,1)S(1)} %broadcast_select_fusion.lat_ref) | copy-start | bytes 27652
  77.3 30.7 %all-to-all-start.2 = ((bf16[32,16,72]{2,1,0:T(8,128)(2,1)}), bf16[32,16,72]{2,1,0:T(8,128)(2,1)S(1)}, u32[]{:S(2)}, u32[]{:S(2)}) async-start(bf16[32,16,72]{2,1,0:T(8,128)(2,1)} %bitcast.18), calls=%async_computation.2 | async-start | bytes 262144 | tf_op jit(solution)/shard_map/all_to_all | solution.py:543
  108.0 0.7 copy-start.14
  121.8 10.6 %all-to-all-start.3 = ((bf16[4,72,640]{2,1,0:T(8,128)(2,1)}), bf16[4,72,640]{2,1,0:T(8,128)(2,1)S(1)}, u32[]{:S(2)}, u32[]{:S(2)}) async-start(bf16[4,72,640]{2,1,0:T(8,128)(2,1)} %shard_map.164), calls=%async_computation.3 | async-start | bytes 737280 | tf_op jit(solution)/shard_map/all_to_all | solution.py:585
  125.3 7.1 %copy-start = (f32[72,1152]{1,0:T(8,128)S(1)}, f32[72,1152]{1,0:T(8,128)}, u32[]{:S(2)}) copy-start(f32[72,1152]{1,0:T(8,128)} %get-tuple-element.59.cb_ref) | copy-start | bytes 995332
  125.3 7.1 %copy-start.1 = (f32[72,1152]{1,0:T(8,128)S(1)}, f32[72,1152]{1,0:T(8,128)}, u32[]{:S(2)}) copy-start(f32[72,1152]{1,0:T(8,128)} %get-tuple-element.60.sb_ref) | copy-start | bytes 995332
  125.3 7.1 %copy-start.2 = (f32[32,1152]{1,0:T(8,128)S(1)}, f32[32,1152]{1,0:T(8,128)}, u32[]{:S(2)}) copy-start(f32[32,1152]{1,0:T(8,128)} %get-tuple-element.44.va_ref) | copy-start | bytes 442372
  125.3 7.1 %copy-start.3 = (f32[32,1152]{1,0:T(8,128)S(1)}, f32[32,1152]{1,0:T(8,128)}, u32[]{:S(2)}) copy-start(f32[32,1152]{1,0:T(8,128)} %get-tuple-element.45.ua_ref) | copy-start | bytes 442372
  125.3 7.1 %copy-start.7 = (f32[6,1152]{1,0:T(8,128)S(1)}, f32[6,1152]{1,0:T(8,128)}, u32[]{:S(2)}) copy-start(f32[6,1152]{1,0:T(8,128)} %get-tuple-element.33.mod_ref) | copy-start | bytes 82948
  132.4 1.4 copy-start.13
Sparse Core Ops, SparseCore 0:
  11.1 80.7 all-gather.1
